TPU v7x, 512 devices: a whole 4x8x8 slice. The times are simulated.
512 devices in a mesh: group: 16 (over y, core), node: 32 (over x, z).
Axes of the slice: x: 4, y: 8, z: 8, core: 2. Of those that a mesh axis runs over, the one named last changes fastest.
Arguments:
- desc: bfloat16 [524288, 512], P(('group', 'node')), may hold values from -8 to 8
- scales: float32 [4, 524288], P(None, ('group', 'node')), may hold values from 0.5 to 2
- labels: int32 [524288], P(('group', 'node')), may hold values from -1000 to 999
- prior: bfloat16 [524288, 1000], P(('group', 'node')), may hold values from -6 to 6
- block_cols: int32 [4096, 2], P(('group', 'node')), may hold values from 0 to 255, as said below
- cross_group: int32 [65536, 1], P(('group', 'node')), may hold values from 0 to 15; in each aligned block of 128 rows (0 to 127, 128 to 255, ...) at most 12 rows name the same one
- cross_row: int32 [65536], P(('group', 'node')), may hold values from 0 to 1023
Outputs:
- scores: bfloat16 [524288, 1000], P(('group', 'node'))
Inputs may be any that keep to these rules, and one draw needn't show every extreme that they name: `block_cols`: block row r of the device at node position p names tiles p * 8 to p * 8 + 8 of its group, the last being the next device's first tile, which the device at the last position never names. A device's first block row names its own first tile first; its last block row names the next device's first tile second, or at the last position its own last tile. `cross_group`: among the 128 cross entries of one device, at most 12 name any one group.
All inputs are finite; a program needn't handle non-finite values.
Results may differ from a plain program's by a relative error of at most 0.0039.
Values may be sent and summed in bfloat16 or wider, within the bound.
No kernel may reach another device: no remote copies, remote signals or barrier semaphores. Data moves between devices by JAX's collectives and lax.ppermute only.
A program may use at most 64 MiB of HBM per device.

v0:
```python
import jax
import jax.numpy as jnp
from jax import lax
from jax.sharding import PartitionSpec as P

D = 512
C = 1000
SCALE_BLK = 128
BLK = 128


alpha_mix = 0.8
eps_norm = 1e-06


def passed_along(block, axis, distance):
    devices = range(lax.axis_size(axis))
    route = [(i - distance, i) for i in devices if i - distance in devices]
    return lax.ppermute(block, axis, route)


def unit_rows(desc, scales):
    count = desc.shape[0]
    widened = desc.astype(jnp.float32).reshape(count, D // SCALE_BLK, SCALE_BLK)
    widened = widened * jnp.transpose(scales)[:, :, None]
    widened = widened.reshape(count, D)
    norm_inv = lax.rsqrt(jnp.sum(widened * widened, axis=1, keepdims=True) + eps_norm)
    return (widened * norm_inv).astype(jnp.bfloat16)


def cube_pos(values):
    positive = jnp.maximum(values, 0.0)
    return positive * positive * positive


def choose_tiles(tiles, following, select_own, is_next):
    picked = jnp.einsum("rkt,tjw->rkjw", select_own, tiles, preferred_element_type=jnp.bfloat16)
    return jnp.where(is_next[:, :, None, None], following[None, None, :, :], picked)


def affinities(own, picked, cross):
    self_w = cube_pos(jnp.einsum("rid,rjd->rij", own, own, preferred_element_type=jnp.float32))
    near = cube_pos(jnp.einsum("rid,rkjd->rikj", own, picked, preferred_element_type=jnp.float32))
    far = cube_pos(jnp.einsum("rid,jd->rij", own, cross, preferred_element_type=jnp.float32))
    degree = jnp.sum(self_w, axis=2) + jnp.sum(near, axis=(2, 3)) + jnp.sum(far, axis=2)
    return (
        self_w.astype(jnp.bfloat16),
        near.astype(jnp.bfloat16),
        far.astype(jnp.bfloat16),
        lax.rsqrt(degree),
    )


def spread(self_w, near_w, far_w, own, picked, cross):
    total = jnp.einsum("rij,rjc->ric", self_w, own, preferred_element_type=jnp.float32)
    total = total + jnp.einsum("rikj,rkjc->ric", near_w, picked, preferred_element_type=jnp.float32)
    return total + jnp.einsum("rij,jc->ric", far_w, cross, preferred_element_type=jnp.float32)


def local(desc, scales, labels, prior, block_cols, cross_group, cross_row):
    groups = lax.axis_size("group")
    spots = 3 * BLK // (2 * groups)
    place = lax.axis_index("node")
    rows_here = desc.shape[0]
    blocks = rows_here // BLK
    units = unit_rows(desc, scales)
    classes = jnp.arange(C, dtype=jnp.int32)
    seeds = jnp.where(
        labels[:, None] >= 0, (labels[:, None] == classes[None, :]).astype(jnp.bfloat16), prior
    )
    named = block_cols - place * blocks
    tile_ids = jnp.arange(blocks, dtype=jnp.int32)
    select_own = (named[:, :, None] == tile_ids[None, None, :]).astype(jnp.bfloat16)
    is_next = named == blocks
    target = cross_group[:, 0]
    member = (target[:, None] == jnp.arange(groups, dtype=jnp.int32)[None, :]).astype(jnp.int32)
    earlier = jnp.cumsum(member, axis=0) - member
    slot = jnp.sum(earlier * member, axis=1)
    flat_pos = target * spots + slot
    hits = flat_pos[None, :] == jnp.arange(groups * spots, dtype=jnp.int32)[:, None]
    wanted = jnp.sum(jnp.where(hits, cross_row[None, :], 0), axis=1).reshape(groups, spots)
    asked = lax.all_to_all(wanted, "group", split_axis=0, concat_axis=0, tiled=True)
    placer = jnp.transpose(hits)

    def collect(reply, width):
        flat = reply.reshape(groups * spots, width)
        return jnp.dot(
            placer.astype(flat.dtype),
            flat,
            preferred_element_type=flat.dtype,
            precision=lax.Precision.HIGHEST,
        )

    own_units = units.reshape(blocks, BLK, D)
    next_units = passed_along(units[:BLK], "node", -1)
    far_units = collect(
        lax.all_to_all(
            jnp.take(units, asked, axis=0), "group", split_axis=0, concat_axis=0, tiled=True
        ),
        D,
    )
    picked_units = choose_tiles(own_units, next_units, select_own, is_next)
    self_w, near_w, far_w, rinv = affinities(own_units, picked_units, far_units)
    rinv_flat = rinv.reshape(rows_here)
    first = (rinv_flat[:, None] * seeds.astype(jnp.float32)).astype(jnp.bfloat16)
    next_first = passed_along(first[:BLK], "node", -1)
    far_first = collect(
        lax.all_to_all(
            jnp.take(first, asked, axis=0), "group", split_axis=0, concat_axis=0, tiled=True
        ),
        C,
    )
    weight = rinv[:, :, None]
    seed_rows = seeds.reshape(blocks, BLK, C).astype(jnp.float32)
    own_first = first.reshape(blocks, BLK, C)
    total = spread(
        self_w,
        near_w,
        far_w,
        own_first,
        choose_tiles(own_first, next_first, select_own, is_next),
        far_first,
    )
    mixed = alpha_mix * weight * total + (1.0 - alpha_mix) * seed_rows
    second = (weight * mixed).astype(jnp.bfloat16).reshape(rows_here, C)
    next_second = passed_along(second[:BLK], "node", -1)
    far_second = collect(
        lax.all_to_all(
            jnp.take(second, asked, axis=0), "group", split_axis=0, concat_axis=0, tiled=True
        ),
        C,
    )
    own_second = second.reshape(blocks, BLK, C)
    total = spread(
        self_w,
        near_w,
        far_w,
        own_second,
        choose_tiles(own_second, next_second, select_own, is_next),
        far_second,
    )
    mixed = alpha_mix * weight * total + (1.0 - alpha_mix) * seed_rows
    return mixed.astype(jnp.bfloat16).reshape(rows_here, C)


def solution(mesh):
    in_specs = (
        P(("group", "node"), None),
        P(None, ("group", "node")),
        P(("group", "node")),
        P(("group", "node"), None),
        P(("group", "node"), None),
        P(("group", "node"), None),
        P(("group", "node")),
    )
    out_specs = P(("group", "node"), None)
    return jax.shard_map(local, mesh=mesh, in_specs=in_specs, out_specs=out_specs, check_vma=False)
```

profile of v0, /device:TPU:7, one launch (start us, length us, event | category | flops | bytes accessed | tf_op | source)
XLA Modules:
  0.0 139.7 jit_solution(7046694037958139346)
XLA Ops:
  4.0 7.8 %all-to-all-start = ((s32[16,1,12]{2,1,0:T(1,128)}), s32[16,1,12]{2,1,0:T(1,128)S(1)}, u32[]{:S(2)}, u32[]{:S(2)}) async-start(s32[16,1,12]{2,1,0:T(1,128)} %bitcast.8), calls=%async_computation | async-start | bytes 16384 | tf_op jit(solution)/shard_map/all_to_all | solution.py:82
  14.6 11.0 %collective-permute-start = (bf16[128,512]{1,0:T(8,128)(2,1)S(1)}, bf16[128,512]{1,0:T(8,128)(2,1)S(1)}, u32[]{:S(2)}, u32[]{:S(2)}) collective-permute-start(bf16[128,512]{1,0:T(8,128)(2,1)S(1)} %slice.22), channel_id=1, source_target_pairs={{1,0},{2,1},{3,2},{4,3},{5,4},{6,5},{7,6},{8,7},{9,8},{10,9},{11,1... | collective-permute-start | bytes 393224 | tf_op jit(solution)/shard_map/ppermute | solution.py:19
  26.8 3.9 %copy.65 = bf16[1024,1000]{1,0:T(8,128)(2,1)} copy(bf16[1024,1000]{0,1:T(8,128)(2,1)} %param.12) | data formatting | bytes 4096000 | tf_op args[3]
  32.8 7.5 %all-to-all-start.1 = ((bf16[16,12,512]{2,1,0:T(8,128)(2,1)}), bf16[16,12,512]{2,1,0:T(8,128)(2,1)S(1)}, u32[]{:S(2)}, u32[]{:S(2)}) async-start(bf16[16,12,512]{2,1,0:T(8,128)(2,1)} %broadcast_select_fusion.5), calls=%async_computation.1 | async-start | bytes 524288 | tf_op jit(solution)/shard_map/all_to_all | solution.py:97
  42.1 9.9 %all-to-all-done.1 = bf16[16,12,512]{2,1,0:T(8,128)(2,1)S(1)} async-done(((bf16[16,12,512]{2,1,0:T(8,128)(2,1)}), bf16[16,12,512]{2,1,0:T(8,128)(2,1)S(1)}, u32[]{:S(2)}, u32[]{:S(2)}) %all-to-all-start.1) | async-done | bytes 196640 | tf_op jit(solution)/shard_map/all_to_all | solution.py:97
  53.5 3.9 %fusion = (bf16[1024,1000]{1,0:T(8,128)(2,1)S(1)}, f32[1024,1000]{1,0:T(8,128)}) fusion(f32[1024]{0:T(1024)S(1)} %bitcast.114, bf16[1024,1000]{1,0:T(8,128)(2,1)} %copy.65, s32[1024]{0:T(1024)S(1)} %copy-done.6, pred[1024]{0:T(1024)(128)(4,1)S(1)} %broadcast_compare_fusion), kind=kLoop, calls=%fused_computation.5 | loop fusion | flops 7168000 | bytes 8201216 | tf_op jit(solution)/shard_map/convert_element_type | solution.py:105
  57.4 5.3 %copy.73 = f32[8,128,1000]{1,2,0:T(8,128)} copy(f32[8,128,1000]{2,1,0:T(8,128)} %bitcast.108) | data formatting | bytes 8192000 | tf_op jit(solution)/shard_map/mul | solution.py:124
  63.4 2.2 %collective-permute-start.1 = (bf16[128,1000]{1,0:T(8,128)(2,1)}, bf16[128,1000]{1,0:T(8,128)(2,1)}, u32[]{:S(2)}, u32[]{:S(2)}) collective-permute-start(bf16[128,1000]{1,0:T(8,128)(2,1)} %slice.23), channel_id=1, source_target_pairs={{1,0},{2,1},{3,2},{4,3},{5,4},{6,5},{7,6},{8,7},{9,8},{10,9},{11,1... | collective-permute-start | bytes 768008 | tf_op jit(solution)/shard_map/ppermute | solution.py:19
  67.7 3.6 %all-to-all-start.2 = ((bf16[16,12,1000]{2,1,0:T(8,128)(2,1)}), bf16[16,12,1000]{2,1,0:T(8,128)(2,1)S(1)}, u32[]{:S(2)}, u32[]{:S(2)}) async-start(bf16[16,12,1000]{2,1,0:T(8,128)(2,1)} %broadcast_select_fusion.4), calls=%async_computation.2 | async-start | bytes 1048576 | tf_op jit(solution)/shard_map/all_to_all | solution.py:108
  71.4 2.9 %copy.69 = bf16[8,128,1000]{1,0,2:T(8,128)(2,1)} copy(bf16[8,128,1000]{2,1,0:T(8,128)(2,1)S(1)} %bitcast.103) | data formatting | bytes 4096000 | tf_op jit(solution)/shard_map/reshape | solution.py:115
  74.3 3.3 %fusion.43 = f32[8,128,1000]{1,2,0:T(8,128)} fusion(bf16[8,128,1000]{2,1,0:T(8,128)(2,1)S(1)} %bitcast.104, bf16[8,128,128]{1,2,0:T(8,128)(2,1)S(1)} %copy-done.3), kind=kOutput, calls=%fused_computation.61 | convolution fusion | flops 262144000 | bytes 6406144 | tf_op jit(solution)/shard_map/rij,rjc->ric/dot_general | solution.py:55
  78.7 4.9 %broadcast_select_fusion.1 = bf16[8,2,128,1000]{2,0,3,1:T(8,128)(2,1)} fusion(pred[8,2]{0,1:T(4,128)(4,1)S(1)} %copy-done.12, bf16[128,1000]{0,1:T(8,128)(2,1)S(1)} %copy.68, bf16[8,128,1000]{1,0,2:T(8,128)(2,1)} %copy.69, s32[8,2]{0,1:T(2,128)S(1)} %copy-done.10), kind=kOutput, calls=%fused_computation.24 | convolution fusion | flops 34816128 | bytes 6400080 | tf_op jit(solution)/shard_map/rkt,tjw->rkjw/dot_general | solution.py:37
  83.6 4.4 %all-to-all-done.2 = bf16[16,12,1000]{2,1,0:T(8,128)(2,1)S(1)} async-done(((bf16[16,12,1000]{2,1,0:T(8,128)(2,1)}), bf16[16,12,1000]{2,1,0:T(8,128)(2,1)S(1)}, u32[]{:S(2)}, u32[]{:S(2)}) %all-to-all-start.2) | async-done | bytes 384032 | tf_op jit(solution)/shard_map/all_to_all | solution.py:108
  90.4 4.7 %fusion.10 = bf16[8,128,1000]{1,2,0:T(8,128)(2,1)S(1)} fusion(f32[8,128,1000]{1,2,0:T(8,128)S(1)} %copy-done, f32[8,128,1000]{1,2,0:T(8,128)S(1)} %fusion.39, f32[8,128,1000]{1,2,0:T(8,128)} %fusion.43, f32[8,128]{1,0:T(8,128)S(1)} %get-tuple-element.7, f32[8,128]{1,0:T(8,128)S(1)} %get-tuple-element.6, ...), kind=kOutput, calls=%fused_computation.18 | convolution fusion | flops 530432000 | bytes 18964480 | tf_op jit(solution)/shard_map/rikj,rkjc->ric/dot_general | solution.py:56
  95.8 3.1 %copy.78 = bf16[8,128,1000]{2,1,0:T(8,128)(2,1)} copy(bf16[8,128,1000]{1,2,0:T(8,128)(2,1)S(1)} %fusion.10) | data formatting | bytes 4096000 | tf_op jit(solution)/shard_map/convert_element_type | solution.py:125
  99.0 2.2 %collective-permute-start.2 = (bf16[128,1000]{0,1:T(8,128)(2,1)}, bf16[128,1000]{0,1:T(8,128)(2,1)}, u32[]{:S(2)}, u32[]{:S(2)}) collective-permute-start(bf16[128,1000]{0,1:T(8,128)(2,1)} %slice_bitcast_fusion), channel_id=1, source_target_pairs={{1,0},{2,1},{3,2},{4,3},{5,4},{6,5},{7,6},{8,7},{9,8},{10,9},{11,1... | collective-permute-start | bytes 768008 | tf_op jit(solution)/shard_map/ppermute | solution.py:19
  101.2 3.2 %gather_fusion.2 = bf16[192,1000]{1,0:T(8,128)(2,1)S(1)} fusion(bf16[1024,1000]{1,0:T(8,128)(2,1)} %bitcast.105, s32[1024]{0:T(1024)S(1)} %pad_clamp_fusion), kind=kCustom, calls=%fused_computation.1.clone | custom fusion | bytes 768768 | tf_op jit(solution)/shard_map/jit(_take)/gather | solution.py:129
  105.4 3.7 %all-to-all-start.3 = ((bf16[16,12,1000]{2,1,0:T(8,128)(2,1)}), bf16[16,12,1000]{2,1,0:T(8,128)(2,1)S(1)}, u32[]{:S(2)}, u32[]{:S(2)}) async-start(bf16[16,12,1000]{2,1,0:T(8,128)(2,1)} %broadcast_select_fusion.3), calls=%async_computation.3 | async-start | bytes 1048576 | tf_op jit(solution)/shard_map/all_to_all | solution.py:128
  109.1 4.1 %fusion.41 = f32[8,128,1000]{1,2,0:T(8,128)} fusion(bf16[8,128,1000]{1,2,0:T(8,128)(2,1)S(1)} %fusion.10, bf16[8,128,128]{1,2,0:T(8,128)(2,1)} %get-tuple-element.15), kind=kOutput, calls=%fused_computation.59 | convolution fusion | flops 262144000 | bytes 6406144 | tf_op jit(solution)/shard_map/rij,rjc->ric/dot_general | solution.py:55
  113.2 4.3 %broadcast_select_fusion = bf16[8,2,128,1000]{2,0,3,1:T(8,128)(2,1)} fusion(pred[8,2]{0,1:T(4,128)(4,1)S(1)} %copy-done.12, bf16[128,1000]{0,1:T(8,128)(2,1)} %collective-permute-done.2, bf16[8,128,1000]{1,2,0:T(8,128)(2,1)S(1)} %fusion.10, s32[8,2]{0,1:T(2,128)S(1)} %copy-done.10), kind=kOutput, calls=%fused_computation.23 | convolution fusion | flops 34816128 | bytes 6400080 | tf_op jit(solution)/shard_map/rkt,tjw->rkjw/dot_general | solution.py:37
  117.5 8.6 %all-to-all-done.3 = bf16[16,12,1000]{2,1,0:T(8,128)(2,1)S(1)} async-done(((bf16[16,12,1000]{2,1,0:T(8,128)(2,1)}), bf16[16,12,1000]{2,1,0:T(8,128)(2,1)S(1)}, u32[]{:S(2)}, u32[]{:S(2)}) %all-to-all-start.3) | async-done | bytes 384032 | tf_op jit(solution)/shard_map/all_to_all | solution.py:128
  128.4 6.0 %fusion.5 = bf16[8,128,1000]{1,2,0:T(8,128)(2,1)} fusion(f32[8,128,1000]{1,2,0:T(8,128)S(1)} %copy-done.1, f32[8,128,1000]{1,2,0:T(8,128)S(1)} %fusion.37, f32[8,128,1000]{1,2,0:T(8,128)} %fusion.41, f32[8,128]{1,0:T(8,128)S(1)} %get-tuple-element.6, bf16[8,2,128,1000]{2,0,3,1:T(8,128)(2,1)} %broadcast_select_fusion, ...), kind=kOutput, calls=%fused_computation.12 | convolution fusion | flops 529408000 | bytes 18960384 | tf_op jit(solution)/shard_map/rikj,rkjc->ric/dot_general | solution.py:56
  134.4 2.8 %copy.81 = bf16[8,128,1000]{2,1,0:T(8,128)(2,1)S(1)} copy(bf16[8,128,1000]{1,2,0:T(8,128)(2,1)} %fusion.5) | data formatting | bytes 4096000 | tf_op jit(solution)/shard_map/convert_element_type | solution.py:143
  137.3 2.4 %copy.82 = bf16[1024,1000]{0,1:T(8,128)(2,1)} copy(bf16[1024,1000]{1,0:T(8,128)(2,1)S(1)} %bitcast.113) | data formatting | bytes 4096000 | tf_op jit(solution)/shard_map/reshape | solution.py:143
  (77 shorter events, 23.6 us)
Async XLA Ops:
  0.0 14.0 %copy-start.2 = (bf16[1024,512]{1,0:T(8,128)(2,1)S(1)}, bf16[1024,512]{1,0:T(8,128)(2,1)}, u32[]{:S(2)}) copy-start(bf16[1024,512]{1,0:T(8,128)(2,1)} %param.9) | copy-start | bytes 3145732
  2.5 49.6 %copy-start.7 = (s32[128]{0:T(128)}, s32[128]{0:T(128)S(1)}, u32[]{:S(2)}) copy-start(s32[128]{0:T(128)S(1)} %multiply_add_fusion) | copy-start | bytes 1540
  4.0 26.8 %all-to-all-start = ((s32[16,1,12]{2,1,0:T(1,128)}), s32[16,1,12]{2,1,0:T(1,128)S(1)}, u32[]{:S(2)}, u32[]{:S(2)}) async-start(s32[16,1,12]{2,1,0:T(1,128)} %bitcast.8), calls=%async_computation | async-start | bytes 16384 | tf_op jit(solution)/shard_map/all_to_all | solution.py:82
  13.9 11.7 %copy-start.6 = (s32[1024]{0:T(1024)S(1)}, s32[1024]{0:T(1024)}, u32[]{:S(2)}) copy-start(s32[1024]{0:T(1024)} %param.11) | copy-start | bytes 12292
  14.3 12.5 %copy-start.13 = (s32[8,2]{0,1:T(2,128)S(1)}, s32[8,2]{0,1:T(2,128)}, u32[]{:S(2)}) copy-start(s32[8,2]{0,1:T(2,128)} %param.13) | copy-start | bytes 196
  14.6 25.7 %collective-permute-start = (bf16[128,512]{1,0:T(8,128)(2,1)S(1)}, bf16[128,512]{1,0:T(8,128)(2,1)S(1)}, u32[]{:S(2)}, u32[]{:S(2)}) collective-permute-start(bf16[128,512]{1,0:T(8,128)(2,1)S(1)} %slice.22), channel_id=1, source_target_pairs={{1,0},{2,1},{3,2},{4,3},{5,4},{6,5},{7,6},{8,7},{9,8},{10,9},{11,1... | collective-permute-start | bytes 393224 | tf_op jit(solution)/shard_map/ppermute | solution.py:19
  26.8 14.4 %copy-start.9 = (s32[8,2]{0,1:T(2,128)}, s32[8,2]{0,1:T(2,128)S(1)}, u32[]{:S(2)}) copy-start(s32[8,2]{0,1:T(2,128)S(1)} %get-tuple-element.9) | copy-start | bytes 196
  26.8 14.5 %copy-start.11 = (pred[8,2]{0,1:T(4,128)(4,1)}, pred[8,2]{0,1:T(4,128)(4,1)S(1)}, u32[]{:S(2)}) copy-start(pred[8,2]{0,1:T(4,128)(4,1)S(1)} %get-tuple-element.8) | copy-start | bytes 52
  32.8 19.2 %all-to-all-start.1 = ((bf16[16,12,512]{2,1,0:T(8,128)(2,1)}), bf16[16,12,512]{2,1,0:T(8,128)(2,1)S(1)}, u32[]{:S(2)}, u32[]{:S(2)}) async-start(bf16[16,12,512]{2,1,0:T(8,128)(2,1)} %broadcast_select_fusion.5), calls=%async_computation.1 | async-start | bytes 524288 | tf_op jit(solution)/shard_map/all_to_all | solution.py:97
  63.4 14.1 %collective-permute-start.1 = (bf16[128,1000]{1,0:T(8,128)(2,1)}, bf16[128,1000]{1,0:T(8,128)(2,1)}, u32[]{:S(2)}, u32[]{:S(2)}) collective-permute-start(bf16[128,1000]{1,0:T(8,128)(2,1)} %slice.23), channel_id=1, source_target_pairs={{1,0},{2,1},{3,2},{4,3},{5,4},{6,5},{7,6},{8,7},{9,8},{10,9},{11,1... | collective-permute-start | bytes 768008 | tf_op jit(solution)/shard_map/ppermute | solution.py:19
  66.8 7.5 %copy-start.3 = (bf16[8,128,128]{1,2,0:T(8,128)(2,1)S(1)}, bf16[8,128,128]{1,2,0:T(8,128)(2,1)}, u32[]{:S(2)}) copy-start(bf16[8,128,128]{1,2,0:T(8,128)(2,1)} %get-tuple-element.15) | copy-start | bytes 786436
  67.7 20.3 %all-to-all-start.2 = ((bf16[16,12,1000]{2,1,0:T(8,128)(2,1)}), bf16[16,12,1000]{2,1,0:T(8,128)(2,1)S(1)}, u32[]{:S(2)}, u32[]{:S(2)}) async-start(bf16[16,12,1000]{2,1,0:T(8,128)(2,1)} %broadcast_select_fusion.4), calls=%async_computation.2 | async-start | bytes 1048576 | tf_op jit(solution)/shard_map/all_to_all | solution.py:108
  74.3 4.4 %copy-start.10 = (s32[8,2]{0,1:T(2,128)S(1)}, s32[8,2]{0,1:T(2,128)}, u32[]{:S(2)}) copy-start(s32[8,2]{0,1:T(2,128)} %copy-done.9) | copy-start | bytes 196
  74.3 4.4 %copy-start.12 = (pred[8,2]{0,1:T(4,128)(4,1)S(1)}, pred[8,2]{0,1:T(4,128)(4,1)}, u32[]{:S(2)}) copy-start(pred[8,2]{0,1:T(4,128)(4,1)} %copy-done.11) | copy-start | bytes 52
  77.5 10.6 %copy-start.8 = (s32[128]{0:T(128)S(1)}, s32[128]{0:T(128)}, u32[]{:S(2)}) copy-start(s32[128]{0:T(128)} %copy-done.7) | copy-start | bytes 1540
  78.7 9.9 %copy-start.4 = (bf16[8,128,128]{1,2,0:T(8,128)(2,1)S(1)}, bf16[8,128,128]{1,2,0:T(8,128)(2,1)}, u32[]{:S(2)}) copy-start(bf16[8,128,128]{1,2,0:T(8,128)(2,1)} %get-tuple-element.13) | copy-start | bytes 786436
  88.2 2.2 %copy-start = (f32[8,128,1000]{1,2,0:T(8,128)S(1)}, f32[8,128,1000]{1,2,0:T(8,128)}, u32[]{:S(2)}) copy-start(f32[8,128,1000]{1,2,0:T(8,128)} %copy.73) | copy-start | bytes 12288004
  99.0 14.2 %collective-permute-start.2 = (bf16[128,1000]{0,1:T(8,128)(2,1)}, bf16[128,1000]{0,1:T(8,128)(2,1)}, u32[]{:S(2)}, u32[]{:S(2)}) collective-permute-start(bf16[128,1000]{0,1:T(8,128)(2,1)} %slice_bitcast_fusion), channel_id=1, source_target_pairs={{1,0},{2,1},{3,2},{4,3},{5,4},{6,5},{7,6},{8,7},{9,8},{10,9},{11,1... | collective-permute-start | bytes 768008 | tf_op jit(solution)/shard_map/ppermute | solution.py:19
  105.4 20.7 %all-to-all-start.3 = ((bf16[16,12,1000]{2,1,0:T(8,128)(2,1)}), bf16[16,12,1000]{2,1,0:T(8,128)(2,1)S(1)}, u32[]{:S(2)}, u32[]{:S(2)}) async-start(bf16[16,12,1000]{2,1,0:T(8,128)(2,1)} %broadcast_select_fusion.3), calls=%async_computation.3 | async-start | bytes 1048576 | tf_op jit(solution)/shard_map/all_to_all | solution.py:128
  113.2 13.4 %copy-start.5 = (bf16[8,128,128]{1,2,0:T(8,128)(2,1)S(1)}, bf16[8,128,128]{1,2,0:T(8,128)(2,1)}, u32[]{:S(2)}) copy-start(bf16[8,128,128]{1,2,0:T(8,128)(2,1)} %get-tuple-element.13) | copy-start | bytes 786436
  126.2 2.2 %copy-start.1 = (f32[8,128,1000]{1,2,0:T(8,128)S(1)}, f32[8,128,1000]{1,2,0:T(8,128)}, u32[]{:S(2)}) copy-start(f32[8,128,1000]{1,2,0:T(8,128)} %copy.73) | copy-start | bytes 12288004
where the time goes:
time: 141 us; the launch traced here: 140 us
  starting transfers between devices  37.9 us (27%)
  local copies, waits for them, and re-layouts  34.2 us (24%)
  matrix products  33.8 us (24%)
  waiting for transfers between devices  22.9 us (16%)
  other arithmetic  10.5 us (7%)
    ppermute x3, starting transfers between devices, passed_along(): return lax.ppermute(block, axis, route)  15.3 us
    dot_general x2, matrix products, spread(): jnp.einsum('rikj,rkjc->ric', near_w, picked, preferred_element_type=jnp.f...  10.8 us
    dot_general x3, matrix products, choose_tiles(): jnp.einsum('rkt,tjw->rkjw', select_own, tiles, preferred_element_type=jnp...  10.1 us
    all_to_all x1, waiting for transfers between devices, local(): lax.all_to_all(jnp.take(units, asked, axis=0), 'group', split_axis=0, con...  9.93 us
    all_to_all x1, waiting for transfers between devices, local(): lax.all_to_all(jnp.take(second, asked, axis=0), 'group', split_axis=0, co...  8.56 us
    all_to_all x1, starting transfers between devices, local(): lax.all_to_all(wanted, 'group', split_axis=0, concat_axis=0, tiled=True)  7.79 us
    all_to_all x1, starting transfers between devices, local(): lax.all_to_all(jnp.take(units, asked, axis=0), 'group', split_axis=0, con...  7.5 us
    dot_general x2, matrix products, spread(): jnp.einsum('rij,rjc->ric', self_w, own, preferred_element_type=jnp.float32)  7.42 us
  transfers between devices with their start and end apart: 7, of which 3 were waited for; matrix products, arithmetic and copies ran while one was open for 28% of the time, Pallas kernels for 0%

commit v1 on v0

v1 whole, which is shorter than its diff:
```python
import jax
import jax.numpy as jnp
from jax import lax
from jax.experimental import pallas as pl
from jax.experimental.pallas import tpu as pltpu
from jax.sharding import PartitionSpec as P

D = 512
C = 1000
CP = 1024
BLK = 128
ROWS = 1024
TILES = ROWS // BLK
GROUPS = 16
EXT = ROWS + BLK

alpha_mix = 0.8
eps_norm = 1e-06

F32 = jnp.float32
BF16 = jnp.bfloat16
VM = pl.BlockSpec(memory_space=pltpu.VMEM)
SM = pl.BlockSpec(memory_space=pltpu.SMEM)
NN = (((1,), (0,)), ((), ()))
NT = (((1,), (1,)), ((), ()))
TN = (((0,), (0,)), ((), ()))


def dot(a, b, dims=NN):
    return lax.dot_general(a, b, dims, preferred_element_type=F32)


def iota(shape, dim):
    return lax.broadcasted_iota(jnp.int32, shape, dim)


def call(body, name, outs, ins, scratch=(), flops=10**9, nbytes=10**6):
    specs = [SM if s else VM for s in ins]
    return pl.pallas_call(
        body,
        name=name,
        out_shape=[jax.ShapeDtypeStruct(s, t) for s, t in outs],
        in_specs=specs,
        out_specs=[VM] * len(outs),
        scratch_shapes=list(scratch),
        cost_estimate=pl.CostEstimate(flops=flops, bytes_accessed=nbytes, transcendentals=0),
        compiler_params=pltpu.CompilerParams(vmem_limit_bytes=32 * 2**20),
    )


def index_body(group_ref, row_ref, wanted_ref, place_ref):
    target = group_ref[...]
    rows = row_ref[...]
    member = (iota((GROUPS, BLK), 0) == target).astype(F32)
    before = (iota((BLK, BLK), 0) < iota((BLK, BLK), 1)).astype(BF16)
    earlier = dot(member.astype(BF16), before)
    slot = jnp.sum(earlier * member, axis=0, keepdims=True).astype(jnp.int32)
    in_slot = (iota((BLK, BLK), 0) == slot).astype(BF16)
    high = (rows >> 5).astype(F32)
    low = (rows & 31).astype(F32)
    wanted = 32.0 * dot((member * high).astype(BF16), in_slot, NT)
    wanted = wanted + dot((member * low).astype(BF16), in_slot, NT)
    wanted_ref[:, 0, :] = wanted.astype(jnp.int32)
    place_ref[0:1, :] = target
    place_ref[1:2, :] = slot


def unit_body(desc_ref, scales_ref, unit_ref, head_ref):
    columns = jnp.transpose(jnp.concatenate([scales_ref[...], scales_ref[...]], axis=0))
    parts = []
    total = None
    for k in range(D // BLK):
        x = desc_ref[:, k * BLK : (k + 1) * BLK].astype(F32) * columns[:, k : k + 1]
        parts.append(x)
        square = x * x
        total = square if total is None else total + square
    inv = lax.rsqrt(jnp.sum(total, axis=1, keepdims=True) + eps_norm)
    for k in range(D // BLK):
        out = (parts[k] * inv).astype(BF16)
        unit_ref[:, k * BLK : (k + 1) * BLK] = out
        head_ref[:, k * BLK : (k + 1) * BLK] = out[:BLK]


def request_rows(asked_ref):
    asked = jnp.broadcast_to(asked_ref[...].astype(F32), (GROUPS, 8, BLK))
    lane, row = iota((GROUPS, 8, BLK), 2), iota((GROUPS, 8, BLK), 1)
    node = iota((GROUPS, 8, ROWS), 2).astype(F32)
    made = []
    for slot in (row, 8 + row % 4):
        column = jnp.sum(jnp.where(lane == slot, asked, 0.0), axis=2, keepdims=True)
        made.append(jnp.where(node == column, 1.0, 0.0).astype(BF16).reshape(BLK, ROWS))
    return jnp.concatenate(made, axis=0)


def pack_rows(res, chunks, send_ref):
    first = iota((BLK, BLK), 0) % 8 < 4

    def part(start, k):
        return res[start : start + BLK, k * BLK : (k + 1) * BLK]

    def put(at, upper, lower):
        both = jnp.concatenate(
            [upper.reshape(GROUPS, 8, BLK), lower.reshape(GROUPS, 8, BLK)], axis=1
        )
        send_ref[:, at : at + 16, :] = both.astype(BF16)

    for k in range(chunks // 2):
        put(16 * k, part(0, 2 * k), part(0, 2 * k + 1))
    for m in range(chunks // 4):
        upper = jnp.where(first, part(BLK, 4 * m), part(BLK, 4 * m + 1))
        lower = jnp.where(first, part(BLK, 4 * m + 2), part(BLK, 4 * m + 3))
        put(8 * chunks + 16 * m, upper, lower)


def placers(place_ref):
    target, slot = place_ref[0:1, :], place_ref[1:2, :]
    row = iota((2 * BLK, BLK), 0)
    low, high = [], []
    for h in range(2):
        at = jnp.where(slot < 8, target * 16 + slot + 8 * h, -1)
        low.append((row == at).astype(F32).astype(BF16))
    for q in range(4):
        at = jnp.where(slot >= 8, target * 16 + slot - 8 + 4 * q, -1)
        high.append((row == at).astype(F32).astype(BF16))
    return jnp.concatenate(low, axis=1), jnp.concatenate(high, axis=1)


def received(recv_ref, at):
    return recv_ref[:, at : at + 16, :].reshape(2 * BLK, BLK)


def gather_units_body(asked_ref, unit_ref, send_ref):
    res = dot(request_rows(asked_ref), unit_ref[...])
    pack_rows(res, D // BLK, send_ref)


def cube_pos(values):
    positive = jnp.maximum(values, 0.0)
    return positive * positive * positive


def near_body(named_ref, unit_ref, next_ref, w_ref, degree_ref, ext_ref):
    ext_ref[:ROWS, :] = unit_ref[...]
    ext_ref[ROWS:, :] = next_ref[...]
    for r in range(TILES):
        own = ext_ref[r * BLK : (r + 1) * BLK, :]
        sources = [own]
        for k in range(2):
            start = pl.multiple_of(named_ref[r, k] * BLK, BLK)
            sources.append(ext_ref[pl.ds(start, BLK), :])
        degree = None
        for k, source in enumerate(sources):
            w = cube_pos(dot(source, own, NT))
            part = jnp.sum(w, axis=0, keepdims=True)
            degree = part if degree is None else degree + part
            w_ref[r, k * BLK : (k + 1) * BLK, :] = w.astype(BF16)
        degree_ref[r : r + 1, :] = degree


def seed_body(labels_ref, prior_ref, seed_ref):
    labels = labels_ref[...]
    for k in range(CP // BLK):
        size = min(BLK, C - k * BLK)
        prior = prior_ref[k * BLK : k * BLK + size, :].astype(F32)
        classes = iota((size, ROWS), 0) + k * BLK
        hot = jnp.where(classes == labels, 1.0, 0.0)
        seed = jnp.where(labels >= 0, hot, prior)
        if size < BLK:
            seed = jnp.concatenate([seed, jnp.zeros((BLK - size, ROWS), F32)], axis=0)
        seed_ref[k * BLK : (k + 1) * BLK, :] = seed.astype(BF16)


def degree_body(
    recv_ref, place_ref, asked_ref, unit_ref, near_ref, seed_ref,
    w_ref, rinv_ref, first_ref, head_ref, send_ref, far_ref,
):
    low, high = placers(place_ref)
    for m in range(D // (4 * BLK)):
        deep = dot(high, received(recv_ref, 4 * D // BLK * 2 + 16 * m), TN)
        for j in range(2):
            flat = dot(low, received(recv_ref, 16 * (2 * m + j)), TN)
            for h in range(2):
                k = 4 * m + 2 * j + h
                part = flat[h * BLK : (h + 1) * BLK] + deep[(2 * j + h) * BLK :][:BLK]
                far_ref[:, k * BLK : (k + 1) * BLK] = part.astype(BF16)
    far = far_ref[...]
    for r in range(TILES):
        cols = slice(r * BLK, (r + 1) * BLK)
        w = cube_pos(dot(far, unit_ref[cols, :], NT))
        w_ref[:, cols] = w.astype(BF16)
        degree = near_ref[r : r + 1, :] + jnp.sum(w, axis=0, keepdims=True)
        rinv = lax.rsqrt(degree)
        rinv_ref[0:1, cols] = rinv
        first_ref[:, cols] = (rinv * seed_ref[:, cols].astype(F32)).astype(BF16)
    head_ref[...] = first_ref[:, :BLK]
    pack_rows(dot(request_rows(asked_ref), first_ref[...], NT), CP // BLK, send_ref)


def spread_near_body(named_ref, own_ref, next_ref, w_ref, out_ref, ext_ref):
    ext_ref[:, :ROWS] = own_ref[...]
    ext_ref[:, ROWS:] = next_ref[...]
    for r in range(TILES):
        sources = [ext_ref[:, r * BLK : (r + 1) * BLK]]
        for k in range(2):
            start = pl.multiple_of(named_ref[r, k] * BLK, BLK)
            sources.append(ext_ref[:, pl.ds(start, BLK)])
        out_ref[:, r * BLK : (r + 1) * BLK] = dot(jnp.concatenate(sources, axis=1), w_ref[r])


def far_scores(recv_ref, place_ref, far_ref):
    low, high = placers(place_ref)
    for m in range(CP // (4 * BLK)):
        deep = dot(received(recv_ref, 8 * CP // BLK + 16 * m), high, TN)
        for j in range(2):
            flat = dot(received(recv_ref, 16 * (2 * m + j)), low, TN)
            for h in range(2):
                k = 4 * m + 2 * j + h
                part = flat[:, h * BLK : (h + 1) * BLK]
                part = part + deep[:, (2 * j + h) * BLK : (2 * j + h + 1) * BLK]
                far_ref[k * BLK : (k + 1) * BLK, :] = part.astype(BF16)


def second_body(
    recv_ref, place_ref, asked_ref, w_ref, near_ref, rinv_ref, seed_ref,
    second_ref, head_ref, send_ref, far_ref,
):
    far_scores(recv_ref, place_ref, far_ref)
    for r in range(TILES // 2):
        cols = slice(2 * r * BLK, 2 * (r + 1) * BLK)
        total = dot(far_ref[...], w_ref[:, cols]) + near_ref[:, cols]
        weight = rinv_ref[0:1, cols]
        mixed = (alpha_mix * weight) * total + (1.0 - alpha_mix) * seed_ref[:, cols].astype(F32)
        second_ref[:, cols] = (weight * mixed).astype(BF16)
    head_ref[...] = second_ref[:, :BLK]
    pack_rows(dot(request_rows(asked_ref), second_ref[...], NT), CP // BLK, send_ref)


def last_body(recv_ref, place_ref, w_ref, near_ref, rinv_ref, seed_ref, out_ref, far_ref):
    far_scores(recv_ref, place_ref, far_ref)
    for r in range(TILES // 2):
        cols = slice(2 * r * BLK, 2 * (r + 1) * BLK)
        total = dot(far_ref[:C, :], w_ref[:, cols]) + near_ref[:C, cols]
        weight = rinv_ref[0:1, cols]
        mixed = (alpha_mix * weight) * total + (1.0 - alpha_mix) * seed_ref[:C, cols].astype(F32)
        out_ref[:, cols] = mixed.astype(BF16)


def passed_back(block):
    size = lax.axis_size("node")
    return lax.ppermute(block, "node", [(i, i - 1) for i in range(1, size)])


def exchanged(block):
    return lax.all_to_all(block, "group", split_axis=0, concat_axis=0, tiled=True)


def local(desc, scales, labels, prior, block_cols, cross_group, cross_row):
    named = block_cols - lax.axis_index("node") * TILES
    wanted, place = call(
        index_body,
        "index",
        [((GROUPS, 1, BLK), jnp.int32), ((8, BLK), jnp.int32)],
        [0, 0],
    )(cross_group.reshape(1, BLK), cross_row.reshape(1, BLK))
    asked = exchanged(wanted)
    units, head = call(
        unit_body, "units", [((ROWS, D), BF16), ((BLK, D), BF16)], [0, 0], nbytes=4 * 10**6
    )(desc, scales)
    next_units = passed_back(head)
    (send,) = call(
        gather_units_body, "gather_units", [((GROUPS, 48, BLK), BF16)], [0, 0]
    )(asked, units)
    far_units = exchanged(send)
    near_w, near_degree = call(
        near_body,
        "near",
        [((TILES, 3 * BLK, BLK), BF16), ((TILES, BLK), F32)],
        [1, 0, 0],
        [pltpu.VMEM((EXT, D), BF16)],
    )(named, units, next_units)
    (seeds,) = call(seed_body, "seeds", [((CP, ROWS), BF16)], [0, 0], nbytes=4 * 10**6)(
        labels.reshape(1, ROWS), jnp.transpose(prior)
    )
    class_rows = ((CP, ROWS), BF16)
    stepped = [class_rows, ((CP, BLK), BF16), ((GROUPS, 96, BLK), BF16)]
    far_w, rinv, first, head, send = call(
        degree_body,
        "degree",
        [((BLK, ROWS), BF16), ((1, ROWS), F32)] + stepped,
        [0] * 6,
        [pltpu.VMEM((BLK, D), BF16)],
    )(far_units, place, asked, units, near_degree, seeds)

    def near_part(scores, head, name):
        return call(
            spread_near_body,
            name,
            [((CP, ROWS), F32)],
            [1, 0, 0, 0],
            [pltpu.VMEM((CP, EXT), BF16)],
            flops=2 * 10**9,
        )(named, scores, passed_back(head), near_w)[0]

    far_scratch = [pltpu.VMEM((CP, BLK), BF16)]
    recv = exchanged(send)
    near = near_part(first, head, "near_first")
    second, head, send = call(second_body, "second", stepped, [0] * 7, far_scratch)(
        recv, place, asked, far_w, near, rinv, seeds
    )
    recv = exchanged(send)
    near = near_part(second, head, "near_second")
    (out,) = call(last_body, "last", [((C, ROWS), BF16)], [0] * 6, far_scratch)(
        recv, place, far_w, near, rinv, seeds
    )
    return jnp.transpose(out)


def solution(mesh):
    both = ("group", "node")
    in_specs = (P(both, None), P(None, both), P(both), P(both, None), P(both, None), P(both, None), P(both))
    return jax.shard_map(
        local, mesh=mesh, in_specs=in_specs, out_specs=P(both, None), check_vma=False
    )
```

time: 141 us -> 104 us (0.74)
  matrix products: 33.8 us -> 0 us
  Pallas kernels: 0 us -> 18.2 us
  local copies, waits for them, and re-layouts: 34.2 us -> 22.2 us
  other arithmetic: 10.5 us -> 0.01 us
  starting transfers between devices: 37.9 us -> 43.8 us
  waiting for transfers between devices: 22.9 us -> 18.2 us
    dot_general x15 -> x0, matrix products: 33.8 us -> none  [the longest x2 10.8 us: spread(): jnp.einsum('rikj,rkjc->ric', near_w, picked, preferred_element_type=jnp.f...]
    pallas_call x0 -> x10, Pallas kernels: none -> 18.2 us  [the longest x2 5.15 us: near_part(): call(spread_near_body, name, [((CP, ROWS), F32)], [1, 0, 0, 0], [pltpu.VM...]
    all_to_all x4, waiting for transfers between devices: 22.9 us -> 4.97 us  [exchanged(): lax.all_to_all(block, 'group', split_axis=0, concat_axis=0, tiled=True)]
    unnamed x29 -> x43, local copies, waits for them, and re-layouts: 6.19 us -> 22.2 us
    ppermute x3, waiting for transfers between devices: 0.01 us -> 13.2 us  [passed_back(): return lax.ppermute(block, 'node', [(i, i - 1) for i in range(1, size)])]
    mul x2 -> x0, local copies, waits for them, and re-layouts: 6.54 us -> none  [the longest x1 5.3 us: local(): mixed = alpha_mix * weight * total + (1.0 - alpha_mix) * seed_rows]
    convert_element_type x2 -> x0, local copies, waits for them, and re-layouts: 5.99 us -> none  [the longest x1 3.14 us: local(): second = (weight * mixed).astype(jnp.bfloat16).reshape(rows_here, C)]
    reshape x5 -> x0, local copies, waits for them, and re-layouts: 5.67 us -> none  [the longest x1 2.87 us: local(): own_first = first.reshape(blocks, BLK, C)]
  transfers between devices with their start and end apart: 7 -> 7, of which waited for: 3 -> 3; matrix products, arithmetic and copies ran while one was open for 28% -> 0% of each run, Pallas kernels for 0% -> 9%
where the time goes in v1:
time: 104 us; the launch traced here: 103 us
  starting transfers between devices  43.8 us (42%)
  local copies, waits for them, and re-layouts  22.2 us (21%)
  Pallas kernels  18.2 us (18%)
  waiting for transfers between devices  18.2 us (18%)
    all_to_all x4, starting transfers between devices, exchanged(): lax.all_to_all(block, 'group', split_axis=0, concat_axis=0, tiled=True)  26.1 us
    unnamed x43, local copies, waits for them, and re-layouts  22.2 us
    ppermute x3, starting transfers between devices, passed_back(): return lax.ppermute(block, 'node', [(i, i - 1) for i in range(1, size)])  17.7 us
    ppermute x3, waiting for transfers between devices, passed_back(): return lax.ppermute(block, 'node', [(i, i - 1) for i in range(1, size)])  13.2 us
    pallas_call x2, Pallas kernels, near_part(): call(spread_near_body, name, [((CP, ROWS), F32)], [1, 0, 0, 0], [pltpu.VM...  5.15 us
    all_to_all x4, waiting for transfers between devices, exchanged(): lax.all_to_all(block, 'group', split_axis=0, concat_axis=0, tiled=True)  4.97 us
    pallas_call x1, Pallas kernels, local(): call(second_body, 'second', stepped, [0] * 7, far_scratch)  2.78 us
    pallas_call x1, Pallas kernels, local(): call(last_body, 'last', [((C, ROWS), BF16)], [0] * 6, far_scratch)  2.51 us
  transfers between devices with their start and end apart: 7, of which 3 were waited for; matrix products, arithmetic and copies ran while one was open for 0% of the time, Pallas kernels for 9%

profile of v1, /device:TPU:7, one launch (start us, length us, event | category | flops | bytes accessed | tf_op | source)
XLA Modules:
  0.0 102.5 jit_solution(12484890527669161925)
XLA Ops:
  2.3 7.9 %all-to-all-start = ((s32[16,1,128]{2,1,0:T(1,128)}), s32[16,1,128]{2,1,0:T(1,128)S(1)}, u32[]{:S(2)}, u32[]{:S(2)}) async-start(s32[16,1,128]{2,1,0:T(1,128)} %get-tuple-element.19), calls=%async_computation | async-start | bytes 16384 | tf_op jit(solution)/shard_map/all_to_all | solution.py:254
  11.4 11.1 %collective-permute-start = (bf16[128,512]{1,0:T(8,128)(2,1)S(1)}, bf16[128,512]{1,0:T(8,128)(2,1)S(1)}, u32[]{:S(2)}, u32[]{:S(2)}) collective-permute-start(bf16[128,512]{1,0:T(8,128)(2,1)S(1)} %get-tuple-element.22), channel_id=1, source_target_pairs={{1,0},{2,1},{3,2},{4,3},{5,4},{6,5},{7,6},{8,7},{9,8},{10,9},{11,1... | collective-permute-start | bytes 393224 | tf_op jit(solution)/shard_map/ppermute | solution.py:250
  23.8 7.5 %all-to-all-start.1 = ((bf16[16,48,128]{2,1,0:T(8,128)(2,1)}), bf16[16,48,128]{2,1,0:T(8,128)(2,1)S(1)}, u32[]{:S(2)}, u32[]{:S(2)}) async-start(bf16[16,48,128]{2,1,0:T(8,128)(2,1)} %gather_units.1), calls=%async_computation.1 | async-start | bytes 393216 | tf_op jit(solution)/shard_map/all_to_all | solution.py:254
  31.3 1.6 %copy-done.4 = bf16[1024,1000]{0,1:T(8,128)(2,1)S(1)} copy-done((bf16[1024,1000]{0,1:T(8,128)(2,1)S(1)}, bf16[1024,1000]{0,1:T(8,128)(2,1)}, u32[]{:S(2)}) %copy-start.4) | copy-done | bytes 2048024
  34.1 1.6 %near.1 = (bf16[8,384,128]{2,1,0:T(8,128)(2,1)S(1)}, f32[8,128]{1,0:T(8,128)S(1)}) custom-call(s32[8,2]{1,0:T(8,128)S(1)} %broadcast_subtract_fusion.named_ref, bf16[1024,512]{1,0:T(8,128)(2,1)S(1)} %copy-done.18, bf16[128,512]{1,0:T(8,128)(2,1)S(1)} %collective-permute-done.next_ref), custom_call_target="tpu_custom_call" | custom-call | flops 1000000000 | bytes 1000000 | tf_op jit(solution)/shard_map/near/pallas_call | solution.py:274
  36.6 5.0 %all-to-all-done.1.recv_ref = bf16[16,48,128]{2,1,0:T(8,128)(2,1)S(1)} async-done(((bf16[16,48,128]{2,1,0:T(8,128)(2,1)}), bf16[16,48,128]{2,1,0:T(8,128)(2,1)S(1)}, u32[]{:S(2)}, u32[]{:S(2)}) %all-to-all-start.1) | async-done | bytes 196640 | tf_op jit(solution)/shard_map/all_to_all | solution.py:254
  42.8 2.3 %degree.1 = (bf16[128,1024]{1,0:T(8,128)(2,1)S(1)}, f32[1,1024]{1,0:T(1,128)S(1)}, bf16[1024,1024]{1,0:T(8,128)(2,1)S(1)}, bf16[1024,128]{1,0:T(8,128)(2,1)S(1)}, bf16[16,96,128]{2,1,0:T(8,128)(2,1)}) custom-call(bf16[16,48,128]{2,1,0:T(8,128)(2,1)S(1)} %all-to-all-done.1.recv_ref, s32[8,128]{1,0:T(8,128)S(1)} %get-tuple-element.21.place_ref, ...), custom_call_target="tpu_custom_call" | custom-call | flops 1000000000 | bytes 1000000 | tf_op jit(solution)/shard_map/degree/pallas_call | solution.py:286
  45.1 1.3 %copy-done.12 = bf16[1024,1024]{1,0:T(8,128)(2,1)} copy-done((bf16[1024,1024]{1,0:T(8,128)(2,1)}, bf16[1024,1024]{1,0:T(8,128)(2,1)S(1)}, u32[]{:S(2)}) %copy-start.12) | copy-done | bytes 2097176
  46.4 3.5 %all-to-all-start.2 = ((bf16[16,96,128]{2,1,0:T(8,128)(2,1)}), bf16[16,96,128]{2,1,0:T(8,128)(2,1)S(1)}, u32[]{:S(2)}, u32[]{:S(2)}) async-start(bf16[16,96,128]{2,1,0:T(8,128)(2,1)} %get-tuple-element.24), calls=%async_computation.2 | async-start | bytes 786432 | tf_op jit(solution)/shard_map/all_to_all | solution.py:254
  49.9 2.2 %collective-permute-start.1 = (bf16[1024,128]{1,0:T(8,128)(2,1)S(1)}, bf16[1024,128]{1,0:T(8,128)(2,1)S(1)}, u32[]{:S(2)}, u32[]{:S(2)}) collective-permute-start(bf16[1024,128]{1,0:T(8,128)(2,1)S(1)} %get-tuple-element.27), channel_id=1, source_target_pairs={{1,0},{2,1},{3,2},{4,3},{5,4},{6,5},{7,6},{8,7},{9,8},{10,9},{11,1... | collective-permute-start | bytes 786440 | tf_op jit(solution)/shard_map/ppermute | solution.py:250
  52.1 7.7 %collective-permute-done.1.next_ref = bf16[1024,128]{1,0:T(8,128)(2,1)S(1)} collective-permute-done((bf16[1024,128]{1,0:T(8,128)(2,1)S(1)}, bf16[1024,128]{1,0:T(8,128)(2,1)S(1)}, u32[]{:S(2)}, u32[]{:S(2)}) %collective-permute-start.1) | collective-permute-done | bytes 262176 | tf_op jit(solution)/shard_map/ppermute | solution.py:250
  59.8 1.6 %copy-done.13 = bf16[1024,1024]{1,0:T(8,128)(2,1)S(1)} copy-done((bf16[1024,1024]{1,0:T(8,128)(2,1)S(1)}, bf16[1024,1024]{1,0:T(8,128)(2,1)}, u32[]{:S(2)}) %copy-start.13) | copy-done | bytes 2097176
  62.5 2.6 %near_first.1.near_ref = f32[1024,1024]{1,0:T(8,128)S(1)} custom-call(s32[8,2]{1,0:T(8,128)S(1)} %broadcast_subtract_fusion.named_ref, bf16[1024,1024]{1,0:T(8,128)(2,1)S(1)} %copy-done.13, bf16[1024,128]{1,0:T(8,128)(2,1)S(1)} %collective-permute-done.1.next_ref, bf16[8,384,128]{2,1,0:T(8,128)(2,1)S(1)} %copy-done.15), custom_call_target="tpu_custom_call" | custom-call | flops 2000000000 | bytes 1000000 | tf_op jit(solution)/shard_map/near_first/pallas_call | solution.py:295
  65.1 2.0 %copy-done.2 = f32[1024,1024]{1,0:T(8,128)} copy-done((f32[1024,1024]{1,0:T(8,128)}, f32[1024,1024]{1,0:T(8,128)S(1)}, u32[]{:S(2)}) %copy-start.2) | copy-done | bytes 4194328
  67.1 2.2 %copy-done.3 = f32[1024,1024]{1,0:T(8,128)S(1)} copy-done((f32[1024,1024]{1,0:T(8,128)S(1)}, f32[1024,1024]{1,0:T(8,128)}, u32[]{:S(2)}) %copy-start.3) | copy-done | bytes 4194328
  69.3 2.8 %second.1 = (bf16[1024,1024]{1,0:T(8,128)(2,1)S(1)}, bf16[1024,128]{1,0:T(8,128)(2,1)S(1)}, bf16[16,96,128]{2,1,0:T(8,128)(2,1)}) custom-call(bf16[16,96,128]{2,1,0:T(8,128)(2,1)S(1)} %all-to-all-done.2.recv_ref, s32[8,128]{1,0:T(8,128)S(1)} %get-tuple-element.21.place_ref, s32[16,1,128]{2,1,0:T(1,128)S(1)} %all-to-all-done.asked_ref, ...), custom_call_target="tpu_custom_call" | custom-call | flops 1000000000 | bytes 1000000 | tf_op jit(solution)/shard_map/second/pallas_call | solution.py:307
  73.4 7.2 %all-to-all-start.3 = ((bf16[16,96,128]{2,1,0:T(8,128)(2,1)}), bf16[16,96,128]{2,1,0:T(8,128)(2,1)S(1)}, u32[]{:S(2)}, u32[]{:S(2)}) async-start(bf16[16,96,128]{2,1,0:T(8,128)(2,1)} %get-tuple-element.30), calls=%async_computation.3 | async-start | bytes 786432 | tf_op jit(solution)/shard_map/all_to_all | solution.py:254
  80.6 4.5 %collective-permute-start.2 = (bf16[1024,128]{1,0:T(8,128)(2,1)S(1)}, bf16[1024,128]{1,0:T(8,128)(2,1)S(1)}, u32[]{:S(2)}, u32[]{:S(2)}) collective-permute-start(bf16[1024,128]{1,0:T(8,128)(2,1)S(1)} %get-tuple-element.32), channel_id=1, source_target_pairs={{1,0},{2,1},{3,2},{4,3},{5,4},{6,5},{7,6},{8,7},{9,8},{10,9},{11,1... | collective-permute-start | bytes 786440 | tf_op jit(solution)/shard_map/ppermute | solution.py:250
  85.1 5.4 %collective-permute-done.2.next_ref = bf16[1024,128]{1,0:T(8,128)(2,1)S(1)} collective-permute-done((bf16[1024,128]{1,0:T(8,128)(2,1)S(1)}, bf16[1024,128]{1,0:T(8,128)(2,1)S(1)}, u32[]{:S(2)}, u32[]{:S(2)}) %collective-permute-start.2) | collective-permute-done | bytes 262176 | tf_op jit(solution)/shard_map/ppermute | solution.py:250
  90.5 1.6 %copy-done.7 = bf16[1024,1024]{1,0:T(8,128)(2,1)S(1)} copy-done((bf16[1024,1024]{1,0:T(8,128)(2,1)S(1)}, bf16[1024,1024]{1,0:T(8,128)(2,1)}, u32[]{:S(2)}) %copy-start.7) | copy-done | bytes 2097176
  93.3 2.6 %near_second.1.near_ref = f32[1024,1024]{1,0:T(8,128)S(1)} custom-call(s32[8,2]{1,0:T(8,128)S(1)} %broadcast_subtract_fusion.named_ref, bf16[1024,1024]{1,0:T(8,128)(2,1)S(1)} %copy-done.7, bf16[1024,128]{1,0:T(8,128)(2,1)S(1)} %collective-permute-done.2.next_ref, bf16[8,384,128]{2,1,0:T(8,128)(2,1)S(1)} %copy-done.16), custom_call_target="tpu_custom_call" | custom-call | flops 2000000000 | bytes 1000000 | tf_op jit(solution)/shard_map/near_second/pallas_call | solution.py:295
  95.8 2.0 %copy-done = f32[1024,1024]{1,0:T(8,128)} copy-done((f32[1024,1024]{1,0:T(8,128)}, f32[1024,1024]{1,0:T(8,128)S(1)}, u32[]{:S(2)}) %copy-start) | copy-done | bytes 4194328
  97.8 2.2 %copy-done.1 = f32[1024,1024]{1,0:T(8,128)S(1)} copy-done((f32[1024,1024]{1,0:T(8,128)S(1)}, f32[1024,1024]{1,0:T(8,128)}, u32[]{:S(2)}) %copy-start.1) | copy-done | bytes 4194328
  100.0 2.5 %last.1 = bf16[1000,1024]{1,0:T(8,128)(2,1)} custom-call(bf16[16,96,128]{2,1,0:T(8,128)(2,1)S(1)} %all-to-all-done.3.recv_ref, s32[8,128]{1,0:T(8,128)S(1)} %get-tuple-element.21.place_ref, bf16[128,1024]{1,0:T(8,128)(2,1)S(1)} %get-tuple-element.25.w_ref, f32[1024,1024]{1,0:T(8,128)S(1)} %copy-done.1, f32[1,1024]{1,0:T(1,128)S(1)} %get-tuple-element.29.rinv_ref, ...), custom_call_target="tpu_custom_call" | custom-call | flops 1000000000 | bytes 1000000 | tf_op jit(solution)/shard_map/last/pallas_call | solution.py:312
  (44 shorter events, 11.6 us)
Async XLA Ops:
  0.0 10.2 %copy-start.9 = (f32[4,1024]{1,0:T(4,128)S(1)}, f32[4,1024]{1,0:T(4,128)}, u32[]{:S(2)}) copy-start(f32[4,1024]{1,0:T(4,128)} %scales_ref.1) | copy-start | bytes 49156
  0.0 10.2 %copy-start.8 = (bf16[1024,512]{1,0:T(8,128)(2,1)S(1)}, bf16[1024,512]{1,0:T(8,128)(2,1)}, u32[]{:S(2)}) copy-start(bf16[1024,512]{1,0:T(8,128)(2,1)} %desc_ref.1) | copy-start | bytes 3145732
  2.3 20.2 %copy-start.20 = (s32[8,2]{0,1:T(2,128)S(1)}, s32[8,2]{0,1:T(2,128)}, u32[]{:S(2)}) copy-start(s32[8,2]{0,1:T(2,128)} %param.11) | copy-start | bytes 196
  2.3 20.3 %all-to-all-start = ((s32[16,1,128]{2,1,0:T(1,128)}), s32[16,1,128]{2,1,0:T(1,128)S(1)}, u32[]{:S(2)}, u32[]{:S(2)}) async-start(s32[16,1,128]{2,1,0:T(1,128)} %get-tuple-element.19), calls=%async_computation | async-start | bytes 16384 | tf_op jit(solution)/shard_map/all_to_all | solution.py:254
  11.4 19.9 %copy-start.17 = (bf16[1024,512]{1,0:T(8,128)(2,1)}, bf16[1024,512]{1,0:T(8,128)(2,1)S(1)}, u32[]{:S(2)}) copy-start(bf16[1024,512]{1,0:T(8,128)(2,1)S(1)} %get-tuple-element.20.unit_ref) | copy-start | bytes 3145732
  11.4 19.9 %copy-start.5 = (s32[1024]{0:T(1024)S(1)}, s32[1024]{0:T(1024)}, u32[]{:S(2)}) copy-start(s32[1024]{0:T(1024)} %param.9) | copy-start | bytes 12292
  11.4 22.1 %collective-permute-start = (bf16[128,512]{1,0:T(8,128)(2,1)S(1)}, bf16[128,512]{1,0:T(8,128)(2,1)S(1)}, u32[]{:S(2)}, u32[]{:S(2)}) collective-permute-start(bf16[128,512]{1,0:T(8,128)(2,1)S(1)} %get-tuple-element.22), channel_id=1, source_target_pairs={{1,0},{2,1},{3,2},{4,3},{5,4},{6,5},{7,6},{8,7},{9,8},{10,9},{11,1... | collective-permute-start | bytes 393224 | tf_op jit(solution)/shard_map/ppermute | solution.py:250
  23.8 17.8 %all-to-all-start.1 = ((bf16[16,48,128]{2,1,0:T(8,128)(2,1)}), bf16[16,48,128]{2,1,0:T(8,128)(2,1)S(1)}, u32[]{:S(2)}, u32[]{:S(2)}) async-start(bf16[16,48,128]{2,1,0:T(8,128)(2,1)} %gather_units.1), calls=%async_computation.1 | async-start | bytes 393216 | tf_op jit(solution)/shard_map/all_to_all | solution.py:254
  31.3 1.6 %copy-start.4 = (bf16[1024,1000]{0,1:T(8,128)(2,1)S(1)}, bf16[1024,1000]{0,1:T(8,128)(2,1)}, u32[]{:S(2)}) copy-start(bf16[1024,1000]{0,1:T(8,128)(2,1)} %param.10) | copy-start | bytes 6144004
  32.8 1.2 %copy-start.18 = (bf16[1024,512]{1,0:T(8,128)(2,1)S(1)}, bf16[1024,512]{1,0:T(8,128)(2,1)}, u32[]{:S(2)}) copy-start(bf16[1024,512]{1,0:T(8,128)(2,1)} %copy-done.17) | copy-start | bytes 3145732
  41.6 1.2 %copy-start.19 = (bf16[1024,512]{1,0:T(8,128)(2,1)S(1)}, bf16[1024,512]{1,0:T(8,128)(2,1)}, u32[]{:S(2)}) copy-start(bf16[1024,512]{1,0:T(8,128)(2,1)} %copy-done.17) | copy-start | bytes 3145732
  45.1 1.3 %copy-start.12 = (bf16[1024,1024]{1,0:T(8,128)(2,1)}, bf16[1024,1024]{1,0:T(8,128)(2,1)S(1)}, u32[]{:S(2)}) copy-start(bf16[1024,1024]{1,0:T(8,128)(2,1)S(1)} %get-tuple-element.26.own_ref) | copy-start | bytes 6291460
  46.4 20.7 %all-to-all-start.2 = ((bf16[16,96,128]{2,1,0:T(8,128)(2,1)}), bf16[16,96,128]{2,1,0:T(8,128)(2,1)S(1)}, u32[]{:S(2)}, u32[]{:S(2)}) async-start(bf16[16,96,128]{2,1,0:T(8,128)(2,1)} %get-tuple-element.24), calls=%async_computation.2 | async-start | bytes 786432 | tf_op jit(solution)/shard_map/all_to_all | solution.py:254
  49.9 9.9 %collective-permute-start.1 = (bf16[1024,128]{1,0:T(8,128)(2,1)S(1)}, bf16[1024,128]{1,0:T(8,128)(2,1)S(1)}, u32[]{:S(2)}, u32[]{:S(2)}) collective-permute-start(bf16[1024,128]{1,0:T(8,128)(2,1)S(1)} %get-tuple-element.27), channel_id=1, source_target_pairs={{1,0},{2,1},{3,2},{4,3},{5,4},{6,5},{7,6},{8,7},{9,8},{10,9},{11,1... | collective-permute-start | bytes 786440 | tf_op jit(solution)/shard_map/ppermute | solution.py:250
  59.8 1.6 %copy-start.13 = (bf16[1024,1024]{1,0:T(8,128)(2,1)S(1)}, bf16[1024,1024]{1,0:T(8,128)(2,1)}, u32[]{:S(2)}) copy-start(bf16[1024,1024]{1,0:T(8,128)(2,1)} %copy-done.12) | copy-start | bytes 6291460
  61.4 1.1 %copy-start.15 = (bf16[8,384,128]{2,1,0:T(8,128)(2,1)S(1)}, bf16[8,384,128]{2,1,0:T(8,128)(2,1)}, u32[]{:S(2)}) copy-start(bf16[8,384,128]{2,1,0:T(8,128)(2,1)} %copy-done.14) | copy-start | bytes 2359300
  65.1 2.0 %copy-start.2 = (f32[1024,1024]{1,0:T(8,128)}, f32[1024,1024]{1,0:T(8,128)S(1)}, u32[]{:S(2)}) copy-start(f32[1024,1024]{1,0:T(8,128)S(1)} %near_first.1.near_ref) | copy-start | bytes 12582916
  67.1 2.2 %copy-start.3 = (f32[1024,1024]{1,0:T(8,128)S(1)}, f32[1024,1024]{1,0:T(8,128)}, u32[]{:S(2)}) copy-start(f32[1024,1024]{1,0:T(8,128)} %copy-done.2) | copy-start | bytes 12582916
  72.1 1.3 %copy-start.6 = (bf16[1024,1024]{1,0:T(8,128)(2,1)}, bf16[1024,1024]{1,0:T(8,128)(2,1)S(1)}, u32[]{:S(2)}) copy-start(bf16[1024,1024]{1,0:T(8,128)(2,1)S(1)} %get-tuple-element.31.own_ref) | copy-start | bytes 6291460
  73.4 24.4 %all-to-all-start.3 = ((bf16[16,96,128]{2,1,0:T(8,128)(2,1)}), bf16[16,96,128]{2,1,0:T(8,128)(2,1)S(1)}, u32[]{:S(2)}, u32[]{:S(2)}) async-start(bf16[16,96,128]{2,1,0:T(8,128)(2,1)} %get-tuple-element.30), calls=%async_computation.3 | async-start | bytes 786432 | tf_op jit(solution)/shard_map/all_to_all | solution.py:254
  80.6 9.9 %collective-permute-start.2 = (bf16[1024,128]{1,0:T(8,128)(2,1)S(1)}, bf16[1024,128]{1,0:T(8,128)(2,1)S(1)}, u32[]{:S(2)}, u32[]{:S(2)}) collective-permute-start(bf16[1024,128]{1,0:T(8,128)(2,1)S(1)} %get-tuple-element.32), channel_id=1, source_target_pairs={{1,0},{2,1},{3,2},{4,3},{5,4},{6,5},{7,6},{8,7},{9,8},{10,9},{11,1... | collective-permute-start | bytes 786440 | tf_op jit(solution)/shard_map/ppermute | solution.py:250
  90.5 1.6 %copy-start.7 = (bf16[1024,1024]{1,0:T(8,128)(2,1)S(1)}, bf16[1024,1024]{1,0:T(8,128)(2,1)}, u32[]{:S(2)}) copy-start(bf16[1024,1024]{1,0:T(8,128)(2,1)} %copy-done.6) | copy-start | bytes 6291460
  95.8 2.0 %copy-start = (f32[1024,1024]{1,0:T(8,128)}, f32[1024,1024]{1,0:T(8,128)S(1)}, u32[]{:S(2)}) copy-start(f32[1024,1024]{1,0:T(8,128)S(1)} %near_second.1.near_ref) | copy-start | bytes 12582916
  97.8 2.2 %copy-start.1 = (f32[1024,1024]{1,0:T(8,128)S(1)}, f32[1024,1024]{1,0:T(8,128)}, u32[]{:S(2)}) copy-start(f32[1024,1024]{1,0:T(8,128)} %copy-done) | copy-start | bytes 12582916
  (4 other events, 3.4 us)

commit v2 on v1

v2 whole, which is shorter than its diff:
```python
import jax
import jax.numpy as jnp
from jax import lax
from jax.experimental import pallas as pl
from jax.experimental.pallas import tpu as pltpu
from jax.sharding import PartitionSpec as P

D = 512
C = 1000
CP = 1024
BLK = 128
ROWS = 1024
TILES = ROWS // BLK
GROUPS = 16
EXT = ROWS + BLK
PAIR = 2 * BLK
PAIRS = ROWS // PAIR
UNIT_WIDE = 12 * D
SCORE_WIDE = 6 * ROWS
WEIGHT_DEEP = 16 * TILES

alpha_mix = 0.8
eps_norm = 1e-06

F32 = jnp.float32
BF16 = jnp.bfloat16
VM = pl.BlockSpec(memory_space=pltpu.VMEM)
SM = pl.BlockSpec(memory_space=pltpu.SMEM)
HB = pl.BlockSpec(memory_space=pltpu.HBM)
SPECS = {"v": VM, "s": SM, "h": HB}
NN = (((1,), (0,)), ((), ()))
NT = (((1,), (1,)), ((), ()))
TN = (((0,), (0,)), ((), ()))


def dot(a, b, dims=NN):
    return lax.dot_general(a, b, dims, preferred_element_type=F32)


def iota(shape, dim):
    return lax.broadcasted_iota(jnp.int32, shape, dim)


def call(body, name, outs, ins, out_kinds=None, scratch=(), flops=10**9, nbytes=10**6, limit=44):
    out_kinds = out_kinds or "v" * len(outs)
    return pl.pallas_call(
        body,
        name=name,
        out_shape=[jax.ShapeDtypeStruct(s, t) for s, t in outs],
        in_specs=[SPECS[k] for k in ins],
        out_specs=[SPECS[k] for k in out_kinds],
        scratch_shapes=list(scratch),
        cost_estimate=pl.CostEstimate(flops=flops, bytes_accessed=nbytes, transcendentals=0),
        compiler_params=pltpu.CompilerParams(vmem_limit_bytes=limit * 2**20),
    )


def started(copies):
    for copy in copies:
        copy.start()
    return copies


def fetched(source_ref, to_ref, sems):
    made = []
    for r in range(PAIRS):
        cols = pl.ds(r * PAIR, PAIR)
        made.append(pltpu.make_async_copy(source_ref.at[:, cols], to_ref.at[:, cols], sems.at[r]))
    return started(made)


def index_body(group_any, row_any, wanted_ref, place_ref, group_ref, row_ref, sems):
    copies = started(
        [
            pltpu.make_async_copy(group_any, group_ref, sems.at[0]),
            pltpu.make_async_copy(row_any, row_ref, sems.at[1]),
        ]
    )
    for copy in copies:
        copy.wait()
    target = group_ref[...]
    rows = row_ref[...]
    member = (iota((GROUPS, BLK), 0) == target).astype(F32)
    before = (iota((BLK, BLK), 0) < iota((BLK, BLK), 1)).astype(BF16)
    earlier = dot(member.astype(BF16), before)
    slot = jnp.sum(earlier * member, axis=0, keepdims=True).astype(jnp.int32)
    in_slot = (iota((BLK, BLK), 0) == slot).astype(BF16)
    high = (rows >> 5).astype(F32)
    low = (rows & 31).astype(F32)
    wanted = 32.0 * dot((member * high).astype(BF16), in_slot, NT)
    wanted = wanted + dot((member * low).astype(BF16), in_slot, NT)
    wanted_ref[:, 0, :] = wanted.astype(jnp.int32)
    place_ref[0:1, :] = target
    place_ref[1:2, :] = slot


def unit_body(desc_ref, scales_ref, unit_ref, head_ref):
    columns = jnp.transpose(jnp.concatenate([scales_ref[...], scales_ref[...]], axis=0))
    parts = []
    total = None
    for k in range(D // BLK):
        x = desc_ref[:, k * BLK : (k + 1) * BLK].astype(F32) * columns[:, k : k + 1]
        parts.append(x)
        square = x * x
        total = square if total is None else total + square
    inv = lax.rsqrt(jnp.sum(total, axis=1, keepdims=True) + eps_norm)
    for k in range(D // BLK):
        out = (parts[k] * inv).astype(BF16)
        unit_ref[:, k * BLK : (k + 1) * BLK] = out
        head_ref[:, k * BLK : (k + 1) * BLK] = out[:BLK]


def request_rows(asked_ref):
    asked = jnp.broadcast_to(asked_ref[...].astype(F32), (GROUPS, 8, BLK))
    lane, row = iota((GROUPS, 8, BLK), 2), iota((GROUPS, 8, BLK), 1)
    node = iota((GROUPS, 8, ROWS), 2).astype(F32)
    made = []
    for slot in (row, 8 + row % 4):
        column = jnp.sum(jnp.where(lane == slot, asked, 0.0), axis=2, keepdims=True)
        made.append(jnp.where(node == column, 1.0, 0.0).astype(BF16).reshape(BLK, ROWS))
    return jnp.concatenate(made, axis=0)


def pack_rows(res, chunks, send_ref):
    first = iota((BLK, BLK), 0) % 8 < 4

    def part(start, k):
        return res[start : start + BLK, k * BLK : (k + 1) * BLK]

    def put(at, upper, lower):
        both = jnp.concatenate(
            [upper.reshape(GROUPS, 8, BLK), lower.reshape(GROUPS, 8, BLK)], axis=1
        )
        send_ref[:, at : at + 16, :] = both.astype(BF16)

    for k in range(chunks // 2):
        put(16 * k, part(0, 2 * k), part(0, 2 * k + 1))
    for m in range(chunks // 4):
        upper = jnp.where(first, part(BLK, 4 * m), part(BLK, 4 * m + 1))
        lower = jnp.where(first, part(BLK, 4 * m + 2), part(BLK, 4 * m + 3))
        put(8 * chunks + 16 * m, upper, lower)


def placers(place_ref):
    target, slot = place_ref[0:1, :], place_ref[1:2, :]
    row = iota((2 * BLK, BLK), 0)
    low, high = [], []
    for h in range(2):
        at = jnp.where(slot < 8, target * 16 + slot + 8 * h, -1)
        low.append((row == at).astype(F32).astype(BF16))
    for q in range(4):
        at = jnp.where(slot >= 8, target * 16 + slot - 8 + 4 * q, -1)
        high.append((row == at).astype(F32).astype(BF16))
    return jnp.concatenate(low, axis=1), jnp.concatenate(high, axis=1)


def received(recv_ref, at):
    return recv_ref[:, at : at + 16, :].reshape(2 * BLK, BLK)


def gather_units_body(asked_ref, unit_ref, send_ref):
    pack_rows(dot(request_rows(asked_ref), unit_ref[...]), D // BLK, send_ref)


def cube_pos(values):
    positive = jnp.maximum(values, 0.0)
    return positive * positive * positive


def near_body(
    named_ref, unit_ref, next_ref, w_any, after_ref, degree_ref, unit_any, ext_ref, w_ref, sem, w_sem
):
    ext_ref[:ROWS, :] = unit_ref[...]
    ext_ref[ROWS:, :] = next_ref[...]
    kept = pltpu.make_async_copy(
        ext_ref.at[pl.ds(0, ROWS), :], unit_any.at[:, pl.ds(0, D)], sem
    )
    kept.start()
    for r in range(TILES):
        own = ext_ref[r * BLK : (r + 1) * BLK, :]
        w = cube_pos(dot(own, own, NT))
        degree = jnp.sum(w, axis=0, keepdims=True)
        w_ref[r, :BLK, :] = w.astype(BF16)
        after = jnp.zeros((BLK, BLK), F32)
        for k in range(2):
            tile = named_ref[r, k]
            start = pl.multiple_of(tile * BLK, BLK)
            w = cube_pos(dot(ext_ref[pl.ds(start, BLK), :], own, NT))
            degree = degree + jnp.sum(w, axis=0, keepdims=True)
            w = w.astype(BF16).astype(F32)
            inside = (tile < TILES).astype(F32)
            after = after + w * (1.0 - inside)
            w_ref[r, (k + 1) * BLK : (k + 2) * BLK, :] = (w * inside).astype(BF16)
        after_ref[:, r * BLK : (r + 1) * BLK] = after.astype(BF16)
        degree_ref[r : r + 1, :] = degree
    w_copy = pltpu.make_async_copy(w_ref, w_any.at[pl.ds(0, TILES)], w_sem)
    w_copy.start()
    kept.wait()
    w_copy.wait()


def seed_body(labels_ref, prior_ref, seed_any, seed_ref, sem):
    labels = labels_ref[...]
    for k in range(CP // BLK):
        size = min(BLK, C - k * BLK)
        prior = prior_ref[k * BLK : k * BLK + size, :].astype(F32)
        classes = iota((size, ROWS), 0) + k * BLK
        hot = jnp.where(classes == labels, 1.0, 0.0)
        seed = jnp.where(labels >= 0, hot, prior)
        if size < BLK:
            seed = jnp.concatenate([seed, jnp.zeros((BLK - size, ROWS), F32)], axis=0)
        seed_ref[k * BLK : (k + 1) * BLK, :] = seed.astype(BF16)
    copy = pltpu.make_async_copy(seed_ref, seed_any.at[:, pl.ds(0, ROWS)], sem)
    copy.start()
    copy.wait()


def degree_body(
    recv_ref, place_ref, asked_ref, unit_any, near_ref, after_ref, seed_any,
    w_ref, rinv_ref, head_ref, send_ref, far_ref, unit_ref, seed_ref, first_ref, sem, sems,
):
    copy = pltpu.make_async_copy(unit_any.at[:, pl.ds(0, D)], unit_ref, sem)
    copy.start()
    arriving = fetched(seed_any, seed_ref, sems)
    low, high = placers(place_ref)
    for m in range(D // (4 * BLK)):
        deep = dot(high, received(recv_ref, 8 * D // BLK + 16 * m), TN)
        for j in range(2):
            flat = dot(low, received(recv_ref, 16 * (2 * m + j)), TN)
            for h in range(2):
                k = 4 * m + 2 * j + h
                part = flat[h * BLK : (h + 1) * BLK] + deep[(2 * j + h) * BLK :][:BLK]
                far_ref[:, k * BLK : (k + 1) * BLK] = part.astype(BF16)
    far = far_ref[...]
    copy.wait()
    for r in range(TILES):
        cols = slice(r * BLK, (r + 1) * BLK)
        w = cube_pos(dot(far, unit_ref[cols, :], NT))
        w_ref[:BLK, cols] = w.astype(BF16)
        degree = near_ref[r : r + 1, :] + jnp.sum(w, axis=0, keepdims=True)
        rinv = lax.rsqrt(degree)
        rinv_ref[0:1, cols] = rinv
        if r % 2 == 0:
            arriving[r // 2].wait()
        first_ref[:, cols] = (rinv * seed_ref[:, cols].astype(F32)).astype(BF16)
    w_ref[BLK:, :] = after_ref[...]
    head_ref[...] = first_ref[:, :BLK]
    pack_rows(dot(request_rows(asked_ref), first_ref[...], NT), CP // BLK, send_ref)


def spread_near(named_ref, source_ref, w_ref, r):
    sources = [source_ref[:, r * BLK : (r + 1) * BLK]]
    for k in range(2):
        start = pl.multiple_of(lax.rem(named_ref[r, k], TILES) * BLK, BLK)
        sources.append(source_ref[:, pl.ds(start, BLK)])
    return dot(jnp.concatenate(sources, axis=1), w_ref[r])


def mixed_near(total, weight, seed):
    return (alpha_mix * weight) * total + (1.0 - alpha_mix) * seed.astype(F32)


def near_first_body(
    named_ref, seed_any, rinv_ref, w_any, out_ref, seed_ref, first_ref, w_ref, sems, w_sem
):
    w_copy = pltpu.make_async_copy(w_any.at[pl.ds(0, TILES)], w_ref, w_sem)
    w_copy.start()
    arriving = fetched(seed_any, seed_ref, sems)
    for r in range(PAIRS):
        arriving[r].wait()
        cols = slice(r * PAIR, (r + 1) * PAIR)
        first_ref[:, cols] = (rinv_ref[0:1, cols] * seed_ref[:, cols].astype(F32)).astype(BF16)
    w_copy.wait()
    for r in range(TILES):
        cols = slice(r * BLK, (r + 1) * BLK)
        weight = rinv_ref[0:1, cols]
        total = spread_near(named_ref, first_ref, w_ref, r)
        out_ref[:, cols] = (weight * mixed_near(total, weight, seed_ref[:, cols])).astype(BF16)


def near_second_body(
    named_ref, second_any, seed_any, rinv_ref, w_any, out_ref,
    seed_ref, second_ref, w_ref, sems, seed_sems, w_sem,
):
    arriving = started([pltpu.make_async_copy(w_any.at[pl.ds(0, TILES)], w_ref, w_sem)])
    arriving += fetched(second_any, second_ref, sems) + fetched(seed_any, seed_ref, seed_sems)
    for copy in arriving:
        copy.wait()
    for r in range(TILES):
        cols = slice(r * BLK, (r + 1) * BLK)
        total = spread_near(named_ref, second_ref, w_ref, r)
        out_ref[:, cols] = mixed_near(total, rinv_ref[0:1, cols], seed_ref[:, cols]).astype(BF16)


def far_scores(recv_ref, place_ref, next_ref, far_ref):
    low, high = placers(place_ref)
    for m in range(CP // (4 * BLK)):
        deep = dot(received(recv_ref, 8 * CP // BLK + 16 * m), high, TN)
        for j in range(2):
            flat = dot(received(recv_ref, 16 * (2 * m + j)), low, TN)
            for h in range(2):
                k = 4 * m + 2 * j + h
                part = flat[:, h * BLK : (h + 1) * BLK]
                part = part + deep[:, (2 * j + h) * BLK : (2 * j + h + 1) * BLK]
                far_ref[k * BLK : (k + 1) * BLK, :BLK] = part.astype(BF16)
    far_ref[:, BLK:] = next_ref[...]


def second_body(
    recv_ref, place_ref, asked_ref, next_ref, w_ref, near_ref, rinv_ref,
    second_any, head_ref, send_ref, far_ref, second_ref, sems,
):
    far_scores(recv_ref, place_ref, next_ref, far_ref)
    leaving = []
    for r in range(PAIRS):
        cols = slice(r * PAIR, (r + 1) * PAIR)
        total = dot(far_ref[...], w_ref[:, cols])
        weight = rinv_ref[0:1, cols]
        total = near_ref[:, cols].astype(F32) + (alpha_mix * weight * weight) * total
        second_ref[:, cols] = total.astype(BF16)
        at = pl.ds(r * PAIR, PAIR)
        leaving += started(
            [pltpu.make_async_copy(second_ref.at[:, at], second_any.at[:, at], sems.at[r])]
        )
    head_ref[...] = second_ref[:, :BLK]
    pack_rows(dot(request_rows(asked_ref), second_ref[...], NT), CP // BLK, send_ref)
    for copy in leaving:
        copy.wait()


def last_body(
    recv_ref, place_ref, next_ref, w_ref, near_ref, rinv_ref, out_any, far_ref, out_ref, sems
):
    far_scores(recv_ref, place_ref, next_ref, far_ref)
    leaving = []
    for r in range(PAIRS):
        cols = slice(r * PAIR, (r + 1) * PAIR)
        total = dot(far_ref[:C, :], w_ref[:, cols])
        total = near_ref[:C, cols].astype(F32) + (alpha_mix * rinv_ref[0:1, cols]) * total
        out_ref[:, cols] = total.astype(BF16)
        at = pl.ds(r * PAIR, PAIR)
        leaving += started(
            [pltpu.make_async_copy(out_ref.at[:, at], out_any.at[:, at], sems.at[r])]
        )
    for copy in leaving:
        copy.wait()


def passed_back(block):
    size = lax.axis_size("node")
    return lax.ppermute(block, "node", [(i, i - 1) for i in range(1, size)])


def exchanged(block):
    return lax.all_to_all(block, "group", split_axis=0, concat_axis=0, tiled=True)


def local(desc, scales, labels, prior, block_cols, cross_group, cross_row):
    named = block_cols - lax.axis_index("node") * TILES
    sem = pltpu.SemaphoreType.DMA
    sems = pltpu.SemaphoreType.DMA((PAIRS,))
    row_vector = pltpu.VMEM((1, BLK), jnp.int32)
    plane = pltpu.VMEM((CP, ROWS), BF16)
    far_scratch = pltpu.VMEM((CP, 2 * BLK), BF16)
    near_w_scratch = pltpu.VMEM((TILES, 3 * BLK, BLK), BF16)
    wanted, place = call(
        index_body,
        "index",
        [((GROUPS, 1, BLK), jnp.int32), ((8, BLK), jnp.int32)],
        "hh",
        scratch=[row_vector, row_vector, pltpu.SemaphoreType.DMA((2,))],
        limit=60,
    )(cross_group.reshape(1, BLK), cross_row.reshape(1, BLK))
    asked = exchanged(wanted)
    units, head = call(
        unit_body,
        "units",
        [((ROWS, D), BF16), ((BLK, D), BF16)],
        "vv",
        nbytes=4 * 10**6,
        limit=60,
    )(desc, scales)
    next_units = passed_back(head)
    (send,) = call(gather_units_body, "gather_units", [((GROUPS, 48, BLK), BF16)], "vv")(asked, units)
    far_units = exchanged(send)
    near_w, after_w, near_degree, unit_wide = call(
        near_body,
        "near",
        [
            ((WEIGHT_DEEP, 3 * BLK, BLK), BF16),
            ((BLK, ROWS), BF16),
            ((TILES, BLK), F32),
            ((ROWS, UNIT_WIDE), BF16),
        ],
        "svv",
        "hvvh",
        scratch=[pltpu.VMEM((EXT, D), BF16), near_w_scratch, sem, sem],
    )(named, units, next_units)
    scores_shape = ((CP, ROWS), BF16)
    wide_shape = ((CP, SCORE_WIDE), BF16)
    (seeds,) = call(
        seed_body, "seeds", [wide_shape], "vv", "h", scratch=[plane, sem], nbytes=4 * 10**6
    )(labels.reshape(1, ROWS), jnp.transpose(prior))
    head_send = [((CP, BLK), BF16), ((GROUPS, 96, BLK), BF16)]
    w, rinv, head, send = call(
        degree_body,
        "degree",
        [((2 * BLK, ROWS), BF16), ((1, ROWS), F32)] + head_send,
        "vvvhvvh",
        scratch=[
            pltpu.VMEM((BLK, D), BF16), pltpu.VMEM((ROWS, D), BF16), plane, plane, sem, sems
        ],
        limit=50,
    )(far_units, place, asked, unit_wide, near_degree, after_w, seeds)
    recv = exchanged(send)
    next_head = passed_back(head)
    (near,) = call(
        near_first_body,
        "near_first",
        [scores_shape],
        "shvh",
        scratch=[plane, plane, near_w_scratch, sems, sem],
        flops=2 * 10**9,
    )(named, seeds, rinv, near_w)
    second, head, send = call(
        second_body,
        "second",
        [wide_shape] + head_send,
        "vvvvvvv",
        "hvv",
        scratch=[far_scratch, plane, sems],
        limit=50,
    )(recv, place, asked, next_head, w, near, rinv)
    recv = exchanged(send)
    next_head = passed_back(head)
    (near,) = call(
        near_second_body,
        "near_second",
        [scores_shape],
        "shhvh",
        scratch=[plane, plane, near_w_scratch, sems, sems, sem],
        flops=2 * 10**9,
    )(named, second, seeds, rinv, near_w)
    (out,) = call(
        last_body,
        "last",
        [((C, ROWS), BF16)],
        "vvvvvv",
        "h",
        scratch=[far_scratch, pltpu.VMEM((C, ROWS), BF16), sems],
    )(recv, place, next_head, w, near, rinv)
    return jnp.transpose(out)


def solution(mesh):
    both = ("group", "node")
    in_specs = (P(both, None), P(None, both), P(both), P(both, None), P(both, None), P(both, None), P(both))
    return jax.shard_map(
        local, mesh=mesh, in_specs=in_specs, out_specs=P(both, None), check_vma=False
    )
```

time: 104 us -> 92.3 us (0.89)
  local copies, waits for them, and re-layouts: 22.2 us -> 4.33 us
  Pallas kernels: 18.2 us -> 30.1 us
  starting transfers between devices: 43.8 us -> 40 us
  waiting for transfers between devices: 18.2 us -> 17 us
    unnamed x43 -> x15, local copies, waits for them, and re-layouts: 22.2 us -> 4.33 us
    pallas_call x9, Pallas kernels: 17.3 us -> 28.4 us  [the longest x1 4.96 us: local(): call(near_second_body, 'near_second', [scores_shape], 'shhvh', scratch=[p...]
    ppermute x3, waiting for transfers between devices: 13.2 us -> 3.83 us  [passed_back(): return lax.ppermute(block, 'node', [(i, i - 1) for i in range(1, size)])]
    all_to_all x4, waiting for transfers between devices: 4.97 us -> 13.1 us  [exchanged(): lax.all_to_all(block, 'group', split_axis=0, concat_axis=0, tiled=True)]
    all_to_all x4, starting transfers between devices: 26.1 us -> 22.3 us  [exchanged(): lax.all_to_all(block, 'group', split_axis=0, concat_axis=0, tiled=True)]
  transfers between devices with their start and end apart: 7 -> 7, of which waited for: 3 -> 5; matrix products, arithmetic and copies ran while one was open for 0% -> 1% of each run, Pallas kernels for 9% -> 20%
where the time goes in v2:
time: 92.3 us; the launch traced here: 91.7 us
  starting transfers between devices  40 us (43%)
  Pallas kernels  30.1 us (33%)
  waiting for transfers between devices  17 us (18%)
  local copies, waits for them, and re-layouts  4.33 us (5%)
    all_to_all x4, starting transfers between devices, exchanged(): lax.all_to_all(block, 'group', split_axis=0, concat_axis=0, tiled=True)  22.3 us
    ppermute x3, starting transfers between devices, passed_back(): return lax.ppermute(block, 'node', [(i, i - 1) for i in range(1, size)])  17.6 us
    all_to_all x4, waiting for transfers between devices, exchanged(): lax.all_to_all(block, 'group', split_axis=0, concat_axis=0, tiled=True)  13.1 us
    pallas_call x1, Pallas kernels, local(): call(near_second_body, 'near_second', [scores_shape], 'shhvh', scratch=[p...  4.96 us
    pallas_call x1, Pallas kernels, local(): call(degree_body, 'degree', [((2 * BLK, ROWS), BF16), ((1, ROWS), F32)] +...  4.72 us
    pallas_call x1, Pallas kernels, local(): call(near_first_body, 'near_first', [scores_shape], 'shvh', scratch=[plan...  4.37 us
    unnamed x15, local copies, waits for them, and re-layouts  4.33 us
    ppermute x3, waiting for transfers between devices, passed_back(): return lax.ppermute(block, 'node', [(i, i - 1) for i in range(1, size)])  3.83 us
  transfers between devices with their start and end apart: 7, of which 5 were waited for; matrix products, arithmetic and copies ran while one was open for 1% of the time, Pallas kernels for 20%

profile of v2, /device:TPU:7, one launch (start us, length us, event | category | flops | bytes accessed | tf_op | source)
XLA Modules:
  0.0 91.7 jit_solution(697172933825881895)
XLA Ops:
  0.0 1.7 %index.1 = (s32[16,1,128]{2,1,0:T(1,128)}, s32[8,128]{1,0:T(8,128)}) custom-call(s32[1,128]{1,0:T(1,128)} %bitcast.7, s32[1,128]{1,0:T(1,128)} %bitcast.8), custom_call_target="tpu_custom_call" | custom-call | flops 1000000000 | bytes 1000000 | tf_op jit(solution)/shard_map/index/pallas_call | solution.py:366
  1.7 7.8 %all-to-all-start = ((s32[16,1,128]{2,1,0:T(1,128)}), s32[16,1,128]{2,1,0:T(1,128)S(1)}, u32[]{:S(2)}, u32[]{:S(2)}) async-start(s32[16,1,128]{2,1,0:T(1,128)} %get-tuple-element.20), calls=%async_computation | async-start | bytes 16384 | tf_op jit(solution)/shard_map/all_to_all | solution.py:355
  9.6 3.3 %units.1 = (bf16[1024,512]{1,0:T(8,128)(2,1)}, bf16[128,512]{1,0:T(8,128)(2,1)}) custom-call(bf16[1024,512]{1,0:T(8,128)(2,1)} %desc_ref.1, f32[4,1024]{1,0:T(4,128)} %scales_ref.1), custom_call_target="tpu_custom_call" | custom-call | flops 1000000000 | bytes 4000000 | tf_op jit(solution)/shard_map/units/pallas_call | solution.py:375
  12.9 10.9 %collective-permute-start = (bf16[128,512]{1,0:T(8,128)(2,1)}, bf16[128,512]{1,0:T(8,128)(2,1)S(1)}, u32[]{:S(2)}, u32[]{:S(2)}) collective-permute-start(bf16[128,512]{1,0:T(8,128)(2,1)} %get-tuple-element.23), channel_id=1, source_target_pairs={{1,0},{2,1},{3,2},{4,3},{5,4},{6,5},{7,6},{8,7},{9,8},{10,9},{11,1... | collective-permute-start | bytes 393224 | tf_op jit(solution)/shard_map/ppermute | solution.py:351
  23.8 0.8 copy.8
  24.6 1.2 %copy-done.5 = bf16[1024,512]{1,0:T(8,128)(2,1)S(1)} copy-done((bf16[1024,512]{1,0:T(8,128)(2,1)S(1)}, bf16[1024,512]{1,0:T(8,128)(2,1)}, u32[]{:S(2)}) %copy-start.5) | copy-done | bytes 1048600
  25.8 1.2 %gather_units.1 = bf16[16,48,128]{2,1,0:T(8,128)(2,1)} custom-call(s32[16,1,128]{2,1,0:T(1,128)S(1)} %all-to-all-done.asked_ref, bf16[1024,512]{1,0:T(8,128)(2,1)S(1)} %copy-done.5), custom_call_target="tpu_custom_call" | custom-call | flops 1000000000 | bytes 1000000 | tf_op jit(solution)/shard_map/gather_units/pallas_call | solution.py:384
  27.0 7.5 %all-to-all-start.1 = ((bf16[16,48,128]{2,1,0:T(8,128)(2,1)}), bf16[16,48,128]{2,1,0:T(8,128)(2,1)S(1)}, u32[]{:S(2)}, u32[]{:S(2)}) async-start(bf16[16,48,128]{2,1,0:T(8,128)(2,1)} %gather_units.1), calls=%async_computation.1 | async-start | bytes 393216 | tf_op jit(solution)/shard_map/all_to_all | solution.py:355
  35.2 2.0 %seeds.1.seed_any = bf16[1024,6144]{1,0:T(8,128)(2,1)} custom-call(s32[1,1024]{1,0:T(1,128)S(1)} %bitcast.6, bf16[1000,1024]{1,0:T(8,128)(2,1)S(1)} %bitcast.5), custom_call_target="tpu_custom_call" | custom-call | flops 1000000000 | bytes 4000000 | tf_op jit(solution)/shard_map/seeds/pallas_call | solution.py:401
  37.2 2.7 %near.1 = (bf16[128,384,128]{2,1,0:T(8,128)(2,1)}, bf16[128,1024]{1,0:T(8,128)(2,1)S(1)}, f32[8,128]{1,0:T(8,128)S(1)}, bf16[1024,6144]{1,0:T(8,128)(2,1)}) custom-call(s32[8,2]{1,0:T(8,128)S(1)} %broadcast_subtract_fusion.named_ref, bf16[1024,512]{1,0:T(8,128)(2,1)S(1)} %copy-done.6, bf16[128,512]{1,0:T(8,128)(2,1)S(1)} %collective-permute-done.next_ref), custom_call_target="tpu_custom_call" | custom-call | flops 1000000000 | bytes 1000000 | tf_op jit(solution)/shard_map/near/pallas_call | solution.py:386
  39.9 4.9 %all-to-all-done.1.recv_ref = bf16[16,48,128]{2,1,0:T(8,128)(2,1)S(1)} async-done(((bf16[16,48,128]{2,1,0:T(8,128)(2,1)}), bf16[16,48,128]{2,1,0:T(8,128)(2,1)S(1)}, u32[]{:S(2)}, u32[]{:S(2)}) %all-to-all-start.1) | async-done | bytes 196640 | tf_op jit(solution)/shard_map/all_to_all | solution.py:355
  44.8 4.7 %degree.1 = (bf16[256,1024]{1,0:T(8,128)(2,1)S(1)}, f32[1,1024]{1,0:T(1,128)S(1)}, bf16[1024,128]{1,0:T(8,128)(2,1)S(1)}, bf16[16,96,128]{2,1,0:T(8,128)(2,1)}) custom-call(bf16[16,48,128]{2,1,0:T(8,128)(2,1)S(1)} %all-to-all-done.1.recv_ref, s32[8,128]{1,0:T(8,128)S(1)} %copy-done.1, s32[16,1,128]{2,1,0:T(1,128)S(1)} %all-to-all-done.asked_ref, ...), custom_call_target="tpu_custom_call" | custom-call | flops 1000000000 | bytes 1000000 | tf_op jit(solution)/shard_map/degree/pallas_call | solution.py:405
  49.5 3.5 %all-to-all-start.2 = ((bf16[16,96,128]{2,1,0:T(8,128)(2,1)}), bf16[16,96,128]{2,1,0:T(8,128)(2,1)S(1)}, u32[]{:S(2)}, u32[]{:S(2)}) async-start(bf16[16,96,128]{2,1,0:T(8,128)(2,1)} %get-tuple-element.27), calls=%async_computation.2 | async-start | bytes 786432 | tf_op jit(solution)/shard_map/all_to_all | solution.py:355
  53.0 2.2 %collective-permute-start.1 = (bf16[1024,128]{1,0:T(8,128)(2,1)S(1)}, bf16[1024,128]{1,0:T(8,128)(2,1)S(1)}, u32[]{:S(2)}, u32[]{:S(2)}) collective-permute-start(bf16[1024,128]{1,0:T(8,128)(2,1)S(1)} %get-tuple-element.28), channel_id=1, source_target_pairs={{1,0},{2,1},{3,2},{4,3},{5,4},{6,5},{7,6},{8,7},{9,8},{10,9},{11,1... | collective-permute-start | bytes 786440 | tf_op jit(solution)/shard_map/ppermute | solution.py:351
  55.2 4.4 %near_first.1.near_ref = bf16[1024,1024]{1,0:T(8,128)(2,1)S(1)} custom-call(s32[8,2]{1,0:T(8,128)S(1)} %broadcast_subtract_fusion.named_ref, bf16[1024,6144]{1,0:T(8,128)(2,1)} %seeds.1.seed_any, f32[1,1024]{1,0:T(1,128)S(1)} %get-tuple-element.30.rinv_ref, bf16[128,384,128]{2,1,0:T(8,128)(2,1)} %get-tuple-element.31.w_any), custom_call_target="tpu_custom_call" | custom-call | flops 2000000000 | bytes 1000000 | tf_op jit(solution)/shard_map/near_first/pallas_call | solution.py:417
  59.6 3.4 %collective-permute-done.1.next_ref = bf16[1024,128]{1,0:T(8,128)(2,1)S(1)} collective-permute-done((bf16[1024,128]{1,0:T(8,128)(2,1)S(1)}, bf16[1024,128]{1,0:T(8,128)(2,1)S(1)}, u32[]{:S(2)}, u32[]{:S(2)}) %collective-permute-start.1) | collective-permute-done | bytes 262176 | tf_op jit(solution)/shard_map/ppermute | solution.py:351
  63.6 3.6 %all-to-all-done.2.recv_ref = bf16[16,96,128]{2,1,0:T(8,128)(2,1)S(1)} async-done(((bf16[16,96,128]{2,1,0:T(8,128)(2,1)}), bf16[16,96,128]{2,1,0:T(8,128)(2,1)S(1)}, u32[]{:S(2)}, u32[]{:S(2)}) %all-to-all-start.2) | async-done | bytes 393248 | tf_op jit(solution)/shard_map/all_to_all | solution.py:355
  67.2 0.9 %copy-done.4 = bf16[1024,128]{1,0:T(8,128)(2,1)S(1)} copy-done((bf16[1024,128]{1,0:T(8,128)(2,1)S(1)}, bf16[1024,128]{1,0:T(8,128)(2,1)}, u32[]{:S(2)}) %copy-start.4) | copy-done | bytes 262168
  68.2 3.1 %second.1 = (bf16[1024,6144]{1,0:T(8,128)(2,1)}, bf16[1024,128]{1,0:T(8,128)(2,1)S(1)}, bf16[16,96,128]{2,1,0:T(8,128)(2,1)}) custom-call(bf16[16,96,128]{2,1,0:T(8,128)(2,1)S(1)} %all-to-all-done.2.recv_ref, s32[8,128]{1,0:T(8,128)S(1)} %copy-done.1, s32[16,1,128]{2,1,0:T(1,128)S(1)} %all-to-all-done.asked_ref, bf16[1024,128]{1,0:T(8,128)(2,1)S(1)} %copy-done.4, ...), custom_call_target="tpu_custom_call" | custom-call | flops 1000000000 | bytes 1000000 | tf_op jit(solution)/shard_map/second/pallas_call | solution.py:425
  71.3 3.6 %all-to-all-start.3 = ((bf16[16,96,128]{2,1,0:T(8,128)(2,1)}), bf16[16,96,128]{2,1,0:T(8,128)(2,1)S(1)}, u32[]{:S(2)}, u32[]{:S(2)}) async-start(bf16[16,96,128]{2,1,0:T(8,128)(2,1)} %get-tuple-element.32), calls=%async_computation.3 | async-start | bytes 786432 | tf_op jit(solution)/shard_map/all_to_all | solution.py:355
  74.9 4.5 %collective-permute-start.2 = (bf16[1024,128]{1,0:T(8,128)(2,1)S(1)}, bf16[1024,128]{1,0:T(8,128)(2,1)S(1)}, u32[]{:S(2)}, u32[]{:S(2)}) collective-permute-start(bf16[1024,128]{1,0:T(8,128)(2,1)S(1)} %get-tuple-element.33), channel_id=1, source_target_pairs={{1,0},{2,1},{3,2},{4,3},{5,4},{6,5},{7,6},{8,7},{9,8},{10,9},{11,1... | collective-permute-start | bytes 786440 | tf_op jit(solution)/shard_map/ppermute | solution.py:351
  79.4 5.0 %near_second.1.near_ref = bf16[1024,1024]{1,0:T(8,128)(2,1)S(1)} custom-call(s32[8,2]{1,0:T(8,128)S(1)} %broadcast_subtract_fusion.named_ref, bf16[1024,6144]{1,0:T(8,128)(2,1)} %get-tuple-element.34.second_any, bf16[1024,6144]{1,0:T(8,128)(2,1)} %seeds.1.seed_any, f32[1,1024]{1,0:T(1,128)S(1)} %get-tuple-element.30.rinv_ref, ...), custom_call_target="tpu_custom_call" | custom-call | flops 2000000000 | bytes 1000000 | tf_op jit(solution)/shard_map/near_second/pallas_call | solution.py:436
  84.9 4.6 %all-to-all-done.3.recv_ref = bf16[16,96,128]{2,1,0:T(8,128)(2,1)S(1)} async-done(((bf16[16,96,128]{2,1,0:T(8,128)(2,1)}), bf16[16,96,128]{2,1,0:T(8,128)(2,1)S(1)}, u32[]{:S(2)}, u32[]{:S(2)}) %all-to-all-start.3) | async-done | bytes 393248 | tf_op jit(solution)/shard_map/all_to_all | solution.py:355
  89.5 2.0 %last.1 = bf16[1000,1024]{1,0:T(8,128)(2,1)} custom-call(bf16[16,96,128]{2,1,0:T(8,128)(2,1)S(1)} %all-to-all-done.3.recv_ref, s32[8,128]{1,0:T(8,128)S(1)} %copy-done.1, bf16[1024,128]{1,0:T(8,128)(2,1)S(1)} %collective-permute-done.2.next_ref, bf16[256,1024]{1,0:T(8,128)(2,1)S(1)} %get-tuple-element.29.w_ref, bf16[1024,1024]{1,0:T(8,128)(2,1)S(1)} %near_second.1.near_ref, ...), custom_call_target="tpu_custom_call" | custom-call | flops 1000000000 | bytes 1000000 | tf_op jit(solution)/shard_map/last/pallas_call | solution.py:444
  (16 shorter events, 1.9 us)
Async XLA Ops:
  0.0 34.5 %copy-start = (bf16[1024,1000]{0,1:T(8,128)(2,1)S(1)}, bf16[1024,1000]{0,1:T(8,128)(2,1)}, u32[]{:S(2)}) copy-start(bf16[1024,1000]{0,1:T(8,128)(2,1)} %param.10) | copy-start | bytes 6144004
  1.7 22.8 %all-to-all-start = ((s32[16,1,128]{2,1,0:T(1,128)}), s32[16,1,128]{2,1,0:T(1,128)S(1)}, u32[]{:S(2)}, u32[]{:S(2)}) async-start(s32[16,1,128]{2,1,0:T(1,128)} %get-tuple-element.20), calls=%async_computation | async-start | bytes 16384 | tf_op jit(solution)/shard_map/all_to_all | solution.py:355
  9.5 35.2 %copy-start.1 = (s32[8,128]{1,0:T(8,128)S(1)}, s32[8,128]{1,0:T(8,128)}, u32[]{:S(2)}) copy-start(s32[8,128]{1,0:T(8,128)} %get-tuple-element.22.place_ref) | copy-start | bytes 12292
  12.9 24.3 %collective-permute-start = (bf16[128,512]{1,0:T(8,128)(2,1)}, bf16[128,512]{1,0:T(8,128)(2,1)S(1)}, u32[]{:S(2)}, u32[]{:S(2)}) collective-permute-start(bf16[128,512]{1,0:T(8,128)(2,1)} %get-tuple-element.23), channel_id=1, source_target_pairs={{1,0},{2,1},{3,2},{4,3},{5,4},{6,5},{7,6},{8,7},{9,8},{10,9},{11,1... | collective-permute-start | bytes 393224 | tf_op jit(solution)/shard_map/ppermute | solution.py:351
  24.6 1.2 %copy-start.5 = (bf16[1024,512]{1,0:T(8,128)(2,1)S(1)}, bf16[1024,512]{1,0:T(8,128)(2,1)}, u32[]{:S(2)}) copy-start(bf16[1024,512]{1,0:T(8,128)(2,1)} %get-tuple-element.21.unit_ref) | copy-start | bytes 3145732
  27.0 17.8 %all-to-all-start.1 = ((bf16[16,48,128]{2,1,0:T(8,128)(2,1)}), bf16[16,48,128]{2,1,0:T(8,128)(2,1)S(1)}, u32[]{:S(2)}, u32[]{:S(2)}) async-start(bf16[16,48,128]{2,1,0:T(8,128)(2,1)} %gather_units.1), calls=%async_computation.1 | async-start | bytes 393216 | tf_op jit(solution)/shard_map/all_to_all | solution.py:355
  34.5 0.7 copy-start.2
  35.2 2.0 %copy-start.6 = (bf16[1024,512]{1,0:T(8,128)(2,1)S(1)}, bf16[1024,512]{1,0:T(8,128)(2,1)}, u32[]{:S(2)}) copy-start(bf16[1024,512]{1,0:T(8,128)(2,1)} %get-tuple-element.21.unit_ref) | copy-start | bytes 3145732
  49.5 17.7 %all-to-all-start.2 = ((bf16[16,96,128]{2,1,0:T(8,128)(2,1)}), bf16[16,96,128]{2,1,0:T(8,128)(2,1)S(1)}, u32[]{:S(2)}, u32[]{:S(2)}) async-start(bf16[16,96,128]{2,1,0:T(8,128)(2,1)} %get-tuple-element.27), calls=%async_computation.2 | async-start | bytes 786432 | tf_op jit(solution)/shard_map/all_to_all | solution.py:355
  53.0 9.9 %collective-permute-start.1 = (bf16[1024,128]{1,0:T(8,128)(2,1)S(1)}, bf16[1024,128]{1,0:T(8,128)(2,1)S(1)}, u32[]{:S(2)}, u32[]{:S(2)}) collective-permute-start(bf16[1024,128]{1,0:T(8,128)(2,1)S(1)} %get-tuple-element.28), channel_id=1, source_target_pairs={{1,0},{2,1},{3,2},{4,3},{5,4},{6,5},{7,6},{8,7},{9,8},{10,9},{11,1... | collective-permute-start | bytes 786440 | tf_op jit(solution)/shard_map/ppermute | solution.py:351
  62.9 0.7 copy-start.3
  67.2 1.0 %copy-start.4 = (bf16[1024,128]{1,0:T(8,128)(2,1)S(1)}, bf16[1024,128]{1,0:T(8,128)(2,1)}, u32[]{:S(2)}) copy-start(bf16[1024,128]{1,0:T(8,128)(2,1)} %copy-done.3) | copy-start | bytes 786436
  71.3 18.2 %all-to-all-start.3 = ((bf16[16,96,128]{2,1,0:T(8,128)(2,1)}), bf16[16,96,128]{2,1,0:T(8,128)(2,1)S(1)}, u32[]{:S(2)}, u32[]{:S(2)}) async-start(bf16[16,96,128]{2,1,0:T(8,128)(2,1)} %get-tuple-element.32), calls=%async_computation.3 | async-start | bytes 786432 | tf_op jit(solution)/shard_map/all_to_all | solution.py:355
  74.9 9.9 %collective-permute-start.2 = (bf16[1024,128]{1,0:T(8,128)(2,1)S(1)}, bf16[1024,128]{1,0:T(8,128)(2,1)S(1)}, u32[]{:S(2)}, u32[]{:S(2)}) collective-permute-start(bf16[1024,128]{1,0:T(8,128)(2,1)S(1)} %get-tuple-element.33), channel_id=1, source_target_pairs={{1,0},{2,1},{3,2},{4,3},{5,4},{6,5},{7,6},{8,7},{9,8},{10,9},{11,1... | collective-permute-start | bytes 786440 | tf_op jit(solution)/shard_map/ppermute | solution.py:351

commit v3 on v2

--- a/solution.py
+++ b/solution.py
@@ -15,9 +15,10 @@
 EXT = ROWS + BLK
 PAIR = 2 * BLK
 PAIRS = ROWS // PAIR
-UNIT_WIDE = 12 * D
 SCORE_WIDE = 6 * ROWS
+BASE_WIDE = 3 * ROWS
 WEIGHT_DEEP = 16 * TILES
+HALF = ROWS // 2
 
 alpha_mix = 0.8
 eps_norm = 1e-06
@@ -61,11 +62,12 @@
     return copies
 
 
-def fetched(source_ref, to_ref, sems):
+def moved(source_ref, to_ref, sems, pairs=range(PAIRS), source_at=0, to_at=0):
     made = []
-    for r in range(PAIRS):
-        cols = pl.ds(r * PAIR, PAIR)
-        made.append(pltpu.make_async_copy(source_ref.at[:, cols], to_ref.at[:, cols], sems.at[r]))
+    for r in pairs:
+        source = source_ref.at[:, pl.ds(r * PAIR + source_at, PAIR)]
+        to = to_ref.at[:, pl.ds(r * PAIR + to_at, PAIR)]
+        made.append(pltpu.make_async_copy(source, to, sems.at[r]))
     return started(made)
 
 
@@ -110,13 +112,19 @@
         head_ref[:, k * BLK : (k + 1) * BLK] = out[:BLK]
 
 
+def asked_columns(asked_ref, rows):
+    asked = jnp.broadcast_to(asked_ref[...].astype(F32), (GROUPS, rows, BLK))
+    lane, row = iota((GROUPS, rows, BLK), 2), iota((GROUPS, rows, BLK), 1)
+    return [
+        jnp.sum(jnp.where(lane == slot, asked, 0.0), axis=2, keepdims=True)
+        for slot in (row % 8, 8 + row % 4)
+    ]
+
+
 def request_rows(asked_ref):
-    asked = jnp.broadcast_to(asked_ref[...].astype(F32), (GROUPS, 8, BLK))
-    lane, row = iota((GROUPS, 8, BLK), 2), iota((GROUPS, 8, BLK), 1)
     node = iota((GROUPS, 8, ROWS), 2).astype(F32)
     made = []
-    for slot in (row, 8 + row % 4):
-        column = jnp.sum(jnp.where(lane == slot, asked, 0.0), axis=2, keepdims=True)
+    for column in asked_columns(asked_ref, 8):
         made.append(jnp.where(node == column, 1.0, 0.0).astype(BF16).reshape(BLK, ROWS))
     return jnp.concatenate(made, axis=0)
 
@@ -167,15 +175,9 @@
     return positive * positive * positive
 
 
-def near_body(
-    named_ref, unit_ref, next_ref, w_any, after_ref, degree_ref, unit_any, ext_ref, w_ref, sem, w_sem
-):
+def near_body(named_ref, unit_ref, next_ref, w_any, after_ref, degree_ref, ext_ref, w_ref, w_sem):
     ext_ref[:ROWS, :] = unit_ref[...]
     ext_ref[ROWS:, :] = next_ref[...]
-    kept = pltpu.make_async_copy(
-        ext_ref.at[pl.ds(0, ROWS), :], unit_any.at[:, pl.ds(0, D)], sem
-    )
-    kept.start()
     for r in range(TILES):
         own = ext_ref[r * BLK : (r + 1) * BLK, :]
         w = cube_pos(dot(own, own, NT))
@@ -195,7 +197,6 @@
         degree_ref[r : r + 1, :] = degree
     w_copy = pltpu.make_async_copy(w_ref, w_any.at[pl.ds(0, TILES)], w_sem)
     w_copy.start()
-    kept.wait()
     w_copy.wait()
 
 
@@ -215,13 +216,19 @@
     copy.wait()
 
 
+def gather_seeds_body(asked_ref, seed_any, send_ref, head_ref, seed_ref, sems):
+    arriving = moved(seed_any, seed_ref, sems)
+    rows = request_rows(asked_ref)
+    for copy in arriving:
+        copy.wait()
+    head_ref[...] = seed_ref[:, :BLK]
+    pack_rows(dot(rows, seed_ref[...], NT), CP // BLK, send_ref)
+
+
 def degree_body(
-    recv_ref, place_ref, asked_ref, unit_any, near_ref, after_ref, seed_any,
-    w_ref, rinv_ref, head_ref, send_ref, far_ref, unit_ref, seed_ref, first_ref, sem, sems,
+    recv_ref, place_ref, asked_ref, unit_ref, near_ref, after_ref, asked_seed_ref, seed_ref,
+    w_ref, rinv_ref, head_ref, send_ref, far_ref,
 ):
-    copy = pltpu.make_async_copy(unit_any.at[:, pl.ds(0, D)], unit_ref, sem)
-    copy.start()
-    arriving = fetched(seed_any, seed_ref, sems)
     low, high = placers(place_ref)
     for m in range(D // (4 * BLK)):
         deep = dot(high, received(recv_ref, 8 * D // BLK + 16 * m), TN)
@@ -232,7 +239,9 @@
                 part = flat[h * BLK : (h + 1) * BLK] + deep[(2 * j + h) * BLK :][:BLK]
                 far_ref[:, k * BLK : (k + 1) * BLK] = part.astype(BF16)
     far = far_ref[...]
-    copy.wait()
+    columns = asked_columns(asked_ref, 16)
+    node = iota((GROUPS, 16, BLK), 2).astype(F32)
+    found = [jnp.zeros((GROUPS, 16, BLK), F32) for _ in columns]
     for r in range(TILES):
         cols = slice(r * BLK, (r + 1) * BLK)
         w = cube_pos(dot(far, unit_ref[cols, :], NT))
@@ -240,12 +249,16 @@
         degree = near_ref[r : r + 1, :] + jnp.sum(w, axis=0, keepdims=True)
         rinv = lax.rsqrt(degree)
         rinv_ref[0:1, cols] = rinv
-        if r % 2 == 0:
-            arriving[r // 2].wait()
-        first_ref[:, cols] = (rinv * seed_ref[:, cols].astype(F32)).astype(BF16)
+        if r == 0:
+            head_ref[...] = (rinv * seed_ref[...].astype(F32)).astype(BF16)
+        spread = jnp.broadcast_to(rinv.reshape(1, 1, BLK), (GROUPS, 16, BLK))
+        for k, column in enumerate(columns):
+            found[k] = jnp.where(node + float(r * BLK) == column, spread, found[k])
     w_ref[BLK:, :] = after_ref[...]
-    head_ref[...] = first_ref[:, :BLK]
-    pack_rows(dot(request_rows(asked_ref), first_ref[...], NT), CP // BLK, send_ref)
+    weights = [jnp.sum(values, axis=2, keepdims=True) for values in found]
+    for k in range(6):
+        part = asked_seed_ref[:, 16 * k : 16 * (k + 1), :].astype(F32)
+        send_ref[:, 16 * k : 16 * (k + 1), :] = (weights[k // 4] * part).astype(BF16)
 
 
 def spread_near(named_ref, source_ref, w_ref, r):
@@ -261,35 +274,52 @@
 
 
 def near_first_body(
-    named_ref, seed_any, rinv_ref, w_any, out_ref, seed_ref, first_ref, w_ref, sems, w_sem
+    named_ref, seed_any, rinv_ref, w_any, low_ref, high_any,
+    seed_ref, first_ref, w_ref, high_ref, sems, w_sem, high_sem,
 ):
     w_copy = pltpu.make_async_copy(w_any.at[pl.ds(0, TILES)], w_ref, w_sem)
     w_copy.start()
-    arriving = fetched(seed_any, seed_ref, sems)
+    arriving = moved(seed_any, seed_ref, sems)
     for r in range(PAIRS):
         arriving[r].wait()
         cols = slice(r * PAIR, (r + 1) * PAIR)
         first_ref[:, cols] = (rinv_ref[0:1, cols] * seed_ref[:, cols].astype(F32)).astype(BF16)
     w_copy.wait()
-    for r in range(TILES):
+    for r in reversed(range(TILES)):
         cols = slice(r * BLK, (r + 1) * BLK)
         weight = rinv_ref[0:1, cols]
         total = spread_near(named_ref, first_ref, w_ref, r)
-        out_ref[:, cols] = (weight * mixed_near(total, weight, seed_ref[:, cols])).astype(BF16)
+        total = (weight * mixed_near(total, weight, seed_ref[:, cols])).astype(BF16)
+        if r < TILES // 2:
+            low_ref[:, cols] = total
+        else:
+            high_ref[:, r * BLK - HALF : (r + 1) * BLK - HALF] = total
+        if r == TILES // 2:
+            leaving = pltpu.make_async_copy(high_ref, high_any.at[:, pl.ds(0, HALF)], high_sem)
+            leaving.start()
+    leaving.wait()
 
 
 def near_second_body(
-    named_ref, second_any, seed_any, rinv_ref, w_any, out_ref,
-    seed_ref, second_ref, w_ref, sems, seed_sems, w_sem,
+    named_ref, second_any, seed_any, rinv_ref, w_any, low_ref, high_any,
+    seed_ref, second_ref, w_ref, high_ref, sems, seed_sems, w_sem, high_sem,
 ):
     arriving = started([pltpu.make_async_copy(w_any.at[pl.ds(0, TILES)], w_ref, w_sem)])
-    arriving += fetched(second_any, second_ref, sems) + fetched(seed_any, seed_ref, seed_sems)
+    arriving += moved(second_any, second_ref, sems) + moved(seed_any, seed_ref, seed_sems)
     for copy in arriving:
         copy.wait()
-    for r in range(TILES):
+    for r in reversed(range(TILES)):
         cols = slice(r * BLK, (r + 1) * BLK)
         total = spread_near(named_ref, second_ref, w_ref, r)
-        out_ref[:, cols] = mixed_near(total, rinv_ref[0:1, cols], seed_ref[:, cols]).astype(BF16)
+        total = mixed_near(total, rinv_ref[0:1, cols], seed_ref[:, cols])
+        if r < TILES // 2:
+            low_ref[:, cols] = total
+        else:
+            high_ref[:, r * BLK - HALF : (r + 1) * BLK - HALF] = total
+        if r == TILES // 2:
+            leaving = pltpu.make_async_copy(high_ref, high_any.at[:, pl.ds(0, HALF)], high_sem)
+            leaving.start()
+    leaving.wait()
 
 
 def far_scores(recv_ref, place_ref, next_ref, far_ref):
@@ -307,21 +337,26 @@
 
 
 def second_body(
-    recv_ref, place_ref, asked_ref, next_ref, w_ref, near_ref, rinv_ref,
-    second_any, head_ref, send_ref, far_ref, second_ref, sems,
+    recv_ref, place_ref, asked_ref, next_ref, w_ref, low_ref, high_any, rinv_ref,
+    second_any, head_ref, send_ref, far_ref, high_ref, second_ref, high_sem, sems,
 ):
+    arriving = pltpu.make_async_copy(high_any.at[:, pl.ds(0, HALF)], high_ref, high_sem)
+    arriving.start()
     far_scores(recv_ref, place_ref, next_ref, far_ref)
     leaving = []
     for r in range(PAIRS):
         cols = slice(r * PAIR, (r + 1) * PAIR)
         total = dot(far_ref[...], w_ref[:, cols])
         weight = rinv_ref[0:1, cols]
-        total = near_ref[:, cols].astype(F32) + (alpha_mix * weight * weight) * total
+        if r == PAIRS // 2:
+            arriving.wait()
+        if r < PAIRS // 2:
+            base = low_ref[:, cols]
+        else:
+            base = high_ref[:, r * PAIR - HALF : (r + 1) * PAIR - HALF]
+        total = base.astype(F32) + (alpha_mix * weight * weight) * total
         second_ref[:, cols] = total.astype(BF16)
-        at = pl.ds(r * PAIR, PAIR)
-        leaving += started(
-            [pltpu.make_async_copy(second_ref.at[:, at], second_any.at[:, at], sems.at[r])]
-        )
+        leaving += moved(second_ref, second_any, sems, [r])
     head_ref[...] = second_ref[:, :BLK]
     pack_rows(dot(request_rows(asked_ref), second_ref[...], NT), CP // BLK, send_ref)
     for copy in leaving:
@@ -329,19 +364,24 @@
 
 
 def last_body(
-    recv_ref, place_ref, next_ref, w_ref, near_ref, rinv_ref, out_any, far_ref, out_ref, sems
+    recv_ref, place_ref, next_ref, w_ref, low_ref, high_any, rinv_ref,
+    out_any, far_ref, high_ref, out_ref, high_sem, sems,
 ):
+    arriving = pltpu.make_async_copy(high_any.at[:, pl.ds(0, HALF)], high_ref, high_sem)
+    arriving.start()
     far_scores(recv_ref, place_ref, next_ref, far_ref)
     leaving = []
     for r in range(PAIRS):
         cols = slice(r * PAIR, (r + 1) * PAIR)
         total = dot(far_ref[:C, :], w_ref[:, cols])
-        total = near_ref[:C, cols].astype(F32) + (alpha_mix * rinv_ref[0:1, cols]) * total
-        out_ref[:, cols] = total.astype(BF16)
-        at = pl.ds(r * PAIR, PAIR)
-        leaving += started(
-            [pltpu.make_async_copy(out_ref.at[:, at], out_any.at[:, at], sems.at[r])]
-        )
+        if r == PAIRS // 2:
+            arriving.wait()
+        if r < PAIRS // 2:
+            base = low_ref[:C, cols]
+        else:
+            base = high_ref[:C, r * PAIR - HALF : (r + 1) * PAIR - HALF]
+        out_ref[:, cols] = (base + (alpha_mix * rinv_ref[0:1, cols]) * total).astype(BF16)
+        leaving += moved(out_ref, out_any, sems, [r])
     for copy in leaving:
         copy.wait()
 
@@ -383,72 +423,71 @@
     next_units = passed_back(head)
     (send,) = call(gather_units_body, "gather_units", [((GROUPS, 48, BLK), BF16)], "vv")(asked, units)
     far_units = exchanged(send)
-    near_w, after_w, near_degree, unit_wide = call(
+    near_w, after_w, near_degree = call(
         near_body,
         "near",
-        [
-            ((WEIGHT_DEEP, 3 * BLK, BLK), BF16),
-            ((BLK, ROWS), BF16),
-            ((TILES, BLK), F32),
-            ((ROWS, UNIT_WIDE), BF16),
-        ],
+        [((WEIGHT_DEEP, 3 * BLK, BLK), BF16), ((BLK, ROWS), BF16), ((TILES, BLK), F32)],
         "svv",
-        "hvvh",
-        scratch=[pltpu.VMEM((EXT, D), BF16), near_w_scratch, sem, sem],
+        "hvv",
+        scratch=[pltpu.VMEM((EXT, D), BF16), near_w_scratch, sem],
     )(named, units, next_units)
-    scores_shape = ((CP, ROWS), BF16)
     wide_shape = ((CP, SCORE_WIDE), BF16)
     (seeds,) = call(
         seed_body, "seeds", [wide_shape], "vv", "h", scratch=[plane, sem], nbytes=4 * 10**6
     )(labels.reshape(1, ROWS), jnp.transpose(prior))
-    head_send = [((CP, BLK), BF16), ((GROUPS, 96, BLK), BF16)]
+    head_shape, send_shape = ((CP, BLK), BF16), ((GROUPS, 96, BLK), BF16)
+    asked_seeds, seed_head = call(
+        gather_seeds_body, "gather_seeds", [send_shape, head_shape], "vh", scratch=[plane, sems]
+    )(asked, seeds)
     w, rinv, head, send = call(
         degree_body,
         "degree",
-        [((2 * BLK, ROWS), BF16), ((1, ROWS), F32)] + head_send,
-        "vvvhvvh",
-        scratch=[
-            pltpu.VMEM((BLK, D), BF16), pltpu.VMEM((ROWS, D), BF16), plane, plane, sem, sems
-        ],
+        [((2 * BLK, ROWS), BF16), ((1, ROWS), F32), head_shape, send_shape],
+        "vvvvvvvv",
+        scratch=[pltpu.VMEM((BLK, D), BF16)],
         limit=50,
-    )(far_units, place, asked, unit_wide, near_degree, after_w, seeds)
+    )(far_units, place, asked, units, near_degree, after_w, asked_seeds, seed_head)
     recv = exchanged(send)
     next_head = passed_back(head)
-    (near,) = call(
+    low, high = call(
         near_first_body,
         "near_first",
-        [scores_shape],
+        [((CP, HALF), BF16), wide_shape],
         "shvh",
-        scratch=[plane, plane, near_w_scratch, sems, sem],
+        "vh",
+        scratch=[plane, plane, near_w_scratch, pltpu.VMEM((CP, HALF), BF16), sems, sem, sem],
         flops=2 * 10**9,
     )(named, seeds, rinv, near_w)
     second, head, send = call(
         second_body,
         "second",
-        [wide_shape] + head_send,
-        "vvvvvvv",
+        [wide_shape, head_shape, send_shape],
+        "vvvvvvhv",
         "hvv",
-        scratch=[far_scratch, plane, sems],
+        scratch=[far_scratch, pltpu.VMEM((CP, HALF), BF16), plane, sem, sems],
         limit=50,
-    )(recv, place, asked, next_head, w, near, rinv)
+    )(recv, place, asked, next_head, w, low, high, rinv)
     recv = exchanged(send)
     next_head = passed_back(head)
-    (near,) = call(
+    low, high = call(
         near_second_body,
         "near_second",
-        [scores_shape],
+        [((CP, HALF), F32), ((CP, BASE_WIDE), F32)],
         "shhvh",
-        scratch=[plane, plane, near_w_scratch, sems, sems, sem],
+        "vh",
+        scratch=[plane, plane, near_w_scratch, pltpu.VMEM((CP, HALF), F32), sems, sems, sem, sem],
         flops=2 * 10**9,
     )(named, second, seeds, rinv, near_w)
     (out,) = call(
         last_body,
         "last",
         [((C, ROWS), BF16)],
-        "vvvvvv",
+        "vvvvvhv",
         "h",
-        scratch=[far_scratch, pltpu.VMEM((C, ROWS), BF16), sems],
-    )(recv, place, next_head, w, near, rinv)
+        scratch=[
+            far_scratch, pltpu.VMEM((CP, HALF), F32), pltpu.VMEM((C, ROWS), BF16), sem, sems
+        ],
+    )(recv, place, next_head, w, low, high, rinv)
     return jnp.transpose(out)
 
 

time: 92.3 us -> 92.1 us (level)
  Pallas kernels: 30.1 us -> 34 us
  waiting for transfers between devices: 17 us -> 13.8 us
  local copies, waits for them, and re-layouts: 4.33 us -> 2.68 us
    pallas_call x5 -> x6, Pallas kernels: 19.2 us -> 23.2 us  [the longest x1 5.92 us: local(): call(near_second_body, 'near_second', [((CP, HALF), F32), ((CP, BASE_WIDE...]
    all_to_all x4, waiting for transfers between devices: 13.1 us -> 11.1 us  [exchanged(): lax.all_to_all(block, 'group', split_axis=0, concat_axis=0, tiled=True)]
    unnamed x15 -> x13, local copies, waits for them, and re-layouts: 4.33 us -> 2.68 us
    all_to_all x4, starting transfers between devices: 22.3 us -> 23.5 us  [exchanged(): lax.all_to_all(block, 'group', split_axis=0, concat_axis=0, tiled=True)]
    ppermute x3, waiting for transfers between devices: 3.83 us -> 2.7 us  [passed_back(): return lax.ppermute(block, 'node', [(i, i - 1) for i in range(1, size)])]
  transfers between devices with their start and end apart: 7 -> 7, of which waited for: 5 -> 5; matrix products, arithmetic and copies ran while one was open for 1% -> 1% of each run, Pallas kernels for 20% -> 25%
where the time goes in v3:
time: 92.1 us; the launch traced here: 91.4 us
  starting transfers between devices  40.6 us (44%)
  Pallas kernels  34 us (37%)
  waiting for transfers between devices  13.8 us (15%)
  local copies, waits for them, and re-layouts  2.68 us (3%)
    all_to_all x4, starting transfers between devices, exchanged(): lax.all_to_all(block, 'group', split_axis=0, concat_axis=0, tiled=True)  23.5 us
    ppermute x3, starting transfers between devices, passed_back(): return lax.ppermute(block, 'node', [(i, i - 1) for i in range(1, size)])  17.1 us
    all_to_all x4, waiting for transfers between devices, exchanged(): lax.all_to_all(block, 'group', split_axis=0, concat_axis=0, tiled=True)  11.1 us
    pallas_call x1, Pallas kernels, local(): call(near_second_body, 'near_second', [((CP, HALF), F32), ((CP, BASE_WIDE...  5.92 us
    pallas_call x1, Pallas kernels, local(): call(near_first_body, 'near_first', [((CP, HALF), BF16), wide_shape], 'sh...  5.15 us
    pallas_call x1, Pallas kernels, local(): call(last_body, 'last', [((C, ROWS), BF16)], 'vvvvvhv', 'h', scratch=[far...  4.06 us
    pallas_call x1, Pallas kernels, local(): call(second_body, 'second', [wide_shape, head_shape, send_shape], 'vvvvvv...  3.75 us
    pallas_call x1, Pallas kernels, local(): call(unit_body, 'units', [((ROWS, D), BF16), ((BLK, D), BF16)], 'vv', nby...  3.31 us
  transfers between devices with their start and end apart: 7, of which 5 were waited for; matrix products, arithmetic and copies ran while one was open for 1% of the time, Pallas kernels for 25%

profile of v3, /device:TPU:7, one launch (start us, length us, event | category | flops | bytes accessed | tf_op | source)
XLA Modules:
  0.0 91.4 jit_solution(12011217837423224548)
XLA Ops:
  0.0 1.7 %index.1 = (s32[16,1,128]{2,1,0:T(1,128)}, s32[8,128]{1,0:T(8,128)}) custom-call(s32[1,128]{1,0:T(1,128)} %bitcast.7, s32[1,128]{1,0:T(1,128)} %bitcast.8), custom_call_target="tpu_custom_call" | custom-call | flops 1000000000 | bytes 1000000 | tf_op jit(solution)/shard_map/index/pallas_call | solution.py:406
  1.7 7.8 %all-to-all-start = ((s32[16,1,128]{2,1,0:T(1,128)}), s32[16,1,128]{2,1,0:T(1,128)S(1)}, u32[]{:S(2)}, u32[]{:S(2)}) async-start(s32[16,1,128]{2,1,0:T(1,128)} %get-tuple-element.25), calls=%async_computation | async-start | bytes 16384 | tf_op jit(solution)/shard_map/all_to_all | solution.py:395
  9.5 3.3 %units.1 = (bf16[1024,512]{1,0:T(8,128)(2,1)}, bf16[128,512]{1,0:T(8,128)(2,1)}) custom-call(bf16[1024,512]{1,0:T(8,128)(2,1)} %desc_ref.1, f32[4,1024]{1,0:T(4,128)} %scales_ref.1), custom_call_target="tpu_custom_call" | custom-call | flops 1000000000 | bytes 4000000 | tf_op jit(solution)/shard_map/units/pallas_call | solution.py:415
  12.9 10.9 %collective-permute-start = (bf16[128,512]{1,0:T(8,128)(2,1)}, bf16[128,512]{1,0:T(8,128)(2,1)S(1)}, u32[]{:S(2)}, u32[]{:S(2)}) collective-permute-start(bf16[128,512]{1,0:T(8,128)(2,1)} %get-tuple-element.28), channel_id=1, source_target_pairs={{1,0},{2,1},{3,2},{4,3},{5,4},{6,5},{7,6},{8,7},{9,8},{10,9},{11,1... | collective-permute-start | bytes 393224 | tf_op jit(solution)/shard_map/ppermute | solution.py:391
  23.8 0.8 copy.8
  24.6 1.2 %copy-done.3 = bf16[1024,512]{1,0:T(8,128)(2,1)S(1)} copy-done((bf16[1024,512]{1,0:T(8,128)(2,1)S(1)}, bf16[1024,512]{1,0:T(8,128)(2,1)}, u32[]{:S(2)}) %copy-start.3) | copy-done | bytes 1048600
  25.8 1.2 %gather_units.1 = bf16[16,48,128]{2,1,0:T(8,128)(2,1)} custom-call(s32[16,1,128]{2,1,0:T(1,128)S(1)} %all-to-all-done.asked_ref, bf16[1024,512]{1,0:T(8,128)(2,1)S(1)} %copy-done.3), custom_call_target="tpu_custom_call" | custom-call | flops 1000000000 | bytes 1000000 | tf_op jit(solution)/shard_map/gather_units/pallas_call | solution.py:424
  27.0 7.5 %all-to-all-start.1 = ((bf16[16,48,128]{2,1,0:T(8,128)(2,1)}), bf16[16,48,128]{2,1,0:T(8,128)(2,1)S(1)}, u32[]{:S(2)}, u32[]{:S(2)}) async-start(bf16[16,48,128]{2,1,0:T(8,128)(2,1)} %gather_units.1), calls=%async_computation.1 | async-start | bytes 393216 | tf_op jit(solution)/shard_map/all_to_all | solution.py:395
  35.2 2.0 %seeds.1.seed_any = bf16[1024,6144]{1,0:T(8,128)(2,1)} custom-call(s32[1,1024]{1,0:T(1,128)S(1)} %bitcast.6, bf16[1000,1024]{1,0:T(8,128)(2,1)S(1)} %bitcast.5), custom_call_target="tpu_custom_call" | custom-call | flops 1000000000 | bytes 4000000 | tf_op jit(solution)/shard_map/seeds/pallas_call | solution.py:435
  37.2 2.5 %gather_seeds.1 = (bf16[16,96,128]{2,1,0:T(8,128)(2,1)S(1)}, bf16[1024,128]{1,0:T(8,128)(2,1)S(1)}) custom-call(s32[16,1,128]{2,1,0:T(1,128)S(1)} %all-to-all-done.asked_ref, bf16[1024,6144]{1,0:T(8,128)(2,1)} %seeds.1.seed_any), custom_call_target="tpu_custom_call" | custom-call | flops 1000000000 | bytes 1000000 | tf_op jit(solution)/shard_map/gather_seeds/pallas_call | solution.py:439
  39.7 2.6 %near.1 = (bf16[128,384,128]{2,1,0:T(8,128)(2,1)}, bf16[128,1024]{1,0:T(8,128)(2,1)S(1)}, f32[8,128]{1,0:T(8,128)S(1)}) custom-call(s32[8,2]{1,0:T(8,128)S(1)} %broadcast_subtract_fusion.named_ref, bf16[1024,512]{1,0:T(8,128)(2,1)S(1)} %copy-done.4, bf16[128,512]{1,0:T(8,128)(2,1)S(1)} %collective-permute-done.next_ref), custom_call_target="tpu_custom_call" | custom-call | flops 1000000000 | bytes 1000000 | tf_op jit(solution)/shard_map/near/pallas_call | solution.py:426
  42.3 2.5 %all-to-all-done.1.recv_ref = bf16[16,48,128]{2,1,0:T(8,128)(2,1)S(1)} async-done(((bf16[16,48,128]{2,1,0:T(8,128)(2,1)}), bf16[16,48,128]{2,1,0:T(8,128)(2,1)S(1)}, u32[]{:S(2)}, u32[]{:S(2)}) %all-to-all-start.1) | async-done | bytes 196640 | tf_op jit(solution)/shard_map/all_to_all | solution.py:395
  44.8 1.9 %degree.1 = (bf16[256,1024]{1,0:T(8,128)(2,1)S(1)}, f32[1,1024]{1,0:T(1,128)S(1)}, bf16[1024,128]{1,0:T(8,128)(2,1)S(1)}, bf16[16,96,128]{2,1,0:T(8,128)(2,1)}) custom-call(bf16[16,48,128]{2,1,0:T(8,128)(2,1)S(1)} %all-to-all-done.1.recv_ref, s32[8,128]{1,0:T(8,128)S(1)} %copy-done.1, s32[16,1,128]{2,1,0:T(1,128)S(1)} %all-to-all-done.asked_ref, ...), custom_call_target="tpu_custom_call" | custom-call | flops 1000000000 | bytes 1000000 | tf_op jit(solution)/shard_map/degree/pallas_call | solution.py:442
  46.7 4.8 %all-to-all-start.2 = ((bf16[16,96,128]{2,1,0:T(8,128)(2,1)}), bf16[16,96,128]{2,1,0:T(8,128)(2,1)S(1)}, u32[]{:S(2)}, u32[]{:S(2)}) async-start(bf16[16,96,128]{2,1,0:T(8,128)(2,1)} %get-tuple-element.33), calls=%async_computation.2 | async-start | bytes 786432 | tf_op jit(solution)/shard_map/all_to_all | solution.py:395
  51.4 2.2 %collective-permute-start.1 = (bf16[1024,128]{1,0:T(8,128)(2,1)S(1)}, bf16[1024,128]{1,0:T(8,128)(2,1)S(1)}, u32[]{:S(2)}, u32[]{:S(2)}) collective-permute-start(bf16[1024,128]{1,0:T(8,128)(2,1)S(1)} %get-tuple-element.34), channel_id=1, source_target_pairs={{1,0},{2,1},{3,2},{4,3},{5,4},{6,5},{7,6},{8,7},{9,8},{10,9},{11,1... | collective-permute-start | bytes 786440 | tf_op jit(solution)/shard_map/ppermute | solution.py:391
  53.6 5.2 %near_first.1 = (bf16[1024,512]{1,0:T(8,128)(2,1)S(1)}, bf16[1024,6144]{1,0:T(8,128)(2,1)}) custom-call(s32[8,2]{1,0:T(8,128)S(1)} %broadcast_subtract_fusion.named_ref, bf16[1024,6144]{1,0:T(8,128)(2,1)} %seeds.1.seed_any, f32[1,1024]{1,0:T(1,128)S(1)} %get-tuple-element.36.rinv_ref, bf16[128,384,128]{2,1,0:T(8,128)(2,1)} %get-tuple-element.37.w_any), custom_call_target="tpu_custom_call" | custom-call | flops 2000000000 | bytes 1000000 | tf_op jit(solution)/shard_map/near_first/pallas_call | solution.py:452
  58.8 2.4 %collective-permute-done.1.next_ref = bf16[1024,128]{1,0:T(8,128)(2,1)S(1)} collective-permute-done((bf16[1024,128]{1,0:T(8,128)(2,1)S(1)}, bf16[1024,128]{1,0:T(8,128)(2,1)S(1)}, u32[]{:S(2)}, u32[]{:S(2)}) %collective-permute-start.1) | collective-permute-done | bytes 262176 | tf_op jit(solution)/shard_map/ppermute | solution.py:391
  61.2 4.8 %all-to-all-done.2.recv_ref = bf16[16,96,128]{2,1,0:T(8,128)(2,1)S(1)} async-done(((bf16[16,96,128]{2,1,0:T(8,128)(2,1)}), bf16[16,96,128]{2,1,0:T(8,128)(2,1)S(1)}, u32[]{:S(2)}, u32[]{:S(2)}) %all-to-all-start.2) | async-done | bytes 393248 | tf_op jit(solution)/shard_map/all_to_all | solution.py:395
  66.0 3.7 %second.1 = (bf16[1024,6144]{1,0:T(8,128)(2,1)}, bf16[1024,128]{1,0:T(8,128)(2,1)S(1)}, bf16[16,96,128]{2,1,0:T(8,128)(2,1)}) custom-call(bf16[16,96,128]{2,1,0:T(8,128)(2,1)S(1)} %all-to-all-done.2.recv_ref, s32[8,128]{1,0:T(8,128)S(1)} %copy-done.1, s32[16,1,128]{2,1,0:T(1,128)S(1)} %all-to-all-done.asked_ref, ...), custom_call_target="tpu_custom_call" | custom-call | flops 1000000000 | bytes 1000000 | tf_op jit(solution)/shard_map/second/pallas_call | solution.py:461
  69.7 3.5 %all-to-all-start.3 = ((bf16[16,96,128]{2,1,0:T(8,128)(2,1)}), bf16[16,96,128]{2,1,0:T(8,128)(2,1)S(1)}, u32[]{:S(2)}, u32[]{:S(2)}) async-start(bf16[16,96,128]{2,1,0:T(8,128)(2,1)} %get-tuple-element.40), calls=%async_computation.3 | async-start | bytes 786432 | tf_op jit(solution)/shard_map/all_to_all | solution.py:395
  73.2 4.0 %collective-permute-start.2 = (bf16[1024,128]{1,0:T(8,128)(2,1)S(1)}, bf16[1024,128]{1,0:T(8,128)(2,1)S(1)}, u32[]{:S(2)}, u32[]{:S(2)}) collective-permute-start(bf16[1024,128]{1,0:T(8,128)(2,1)S(1)} %get-tuple-element.41), channel_id=1, source_target_pairs={{1,0},{2,1},{3,2},{4,3},{5,4},{6,5},{7,6},{8,7},{9,8},{10,9},{11,1... | collective-permute-start | bytes 786440 | tf_op jit(solution)/shard_map/ppermute | solution.py:391
  77.2 5.9 %near_second.1 = (f32[1024,512]{1,0:T(8,128)S(1)}, f32[1024,3072]{1,0:T(8,128)}) custom-call(s32[8,2]{1,0:T(8,128)S(1)} %broadcast_subtract_fusion.named_ref, bf16[1024,6144]{1,0:T(8,128)(2,1)} %get-tuple-element.42.second_any, bf16[1024,6144]{1,0:T(8,128)(2,1)} %seeds.1.seed_any, f32[1,1024]{1,0:T(1,128)S(1)} %get-tuple-element.36.rinv_ref, ...), custom_call_target="tpu_custom_call" | custom-call | flops 2000000000 | bytes 1000000 | tf_op jit(solution)/shard_map/near_second/pallas_call | solution.py:472
  83.4 3.8 %all-to-all-done.3.recv_ref = bf16[16,96,128]{2,1,0:T(8,128)(2,1)S(1)} async-done(((bf16[16,96,128]{2,1,0:T(8,128)(2,1)}), bf16[16,96,128]{2,1,0:T(8,128)(2,1)S(1)}, u32[]{:S(2)}, u32[]{:S(2)}) %all-to-all-start.3) | async-done | bytes 393248 | tf_op jit(solution)/shard_map/all_to_all | solution.py:395
  87.2 4.1 %last.1 = bf16[1000,1024]{1,0:T(8,128)(2,1)} custom-call(bf16[16,96,128]{2,1,0:T(8,128)(2,1)S(1)} %all-to-all-done.3.recv_ref, s32[8,128]{1,0:T(8,128)S(1)} %copy-done.1, bf16[1024,128]{1,0:T(8,128)(2,1)S(1)} %collective-permute-done.2.next_ref, bf16[256,1024]{1,0:T(8,128)(2,1)S(1)} %get-tuple-element.35.w_ref, f32[1024,512]{1,0:T(8,128)S(1)} %get-tuple-element.43.low_ref, ...), custom_call_target="tpu_custom_call" | custom-call | flops 1000000000 | bytes 1000000 | tf_op jit(solution)/shard_map/last/pallas_call | solution.py:481
  (15 shorter events, 1.0 us)
Async XLA Ops:
  0.0 34.5 %copy-start = (bf16[1024,1000]{0,1:T(8,128)(2,1)S(1)}, bf16[1024,1000]{0,1:T(8,128)(2,1)}, u32[]{:S(2)}) copy-start(bf16[1024,1000]{0,1:T(8,128)(2,1)} %param.10) | copy-start | bytes 6144004
  1.7 22.8 %all-to-all-start = ((s32[16,1,128]{2,1,0:T(1,128)}), s32[16,1,128]{2,1,0:T(1,128)S(1)}, u32[]{:S(2)}, u32[]{:S(2)}) async-start(s32[16,1,128]{2,1,0:T(1,128)} %get-tuple-element.25), calls=%async_computation | async-start | bytes 16384 | tf_op jit(solution)/shard_map/all_to_all | solution.py:395
  12.9 26.8 %collective-permute-start = (bf16[128,512]{1,0:T(8,128)(2,1)}, bf16[128,512]{1,0:T(8,128)(2,1)S(1)}, u32[]{:S(2)}, u32[]{:S(2)}) collective-permute-start(bf16[128,512]{1,0:T(8,128)(2,1)} %get-tuple-element.28), channel_id=1, source_target_pairs={{1,0},{2,1},{3,2},{4,3},{5,4},{6,5},{7,6},{8,7},{9,8},{10,9},{11,1... | collective-permute-start | bytes 393224 | tf_op jit(solution)/shard_map/ppermute | solution.py:391
  24.6 1.2 %copy-start.3 = (bf16[1024,512]{1,0:T(8,128)(2,1)S(1)}, bf16[1024,512]{1,0:T(8,128)(2,1)}, u32[]{:S(2)}) copy-start(bf16[1024,512]{1,0:T(8,128)(2,1)} %get-tuple-element.26.unit_ref) | copy-start | bytes 3145732
  27.0 17.8 %all-to-all-start.1 = ((bf16[16,48,128]{2,1,0:T(8,128)(2,1)}), bf16[16,48,128]{2,1,0:T(8,128)(2,1)S(1)}, u32[]{:S(2)}, u32[]{:S(2)}) async-start(bf16[16,48,128]{2,1,0:T(8,128)(2,1)} %gather_units.1), calls=%async_computation.1 | async-start | bytes 393216 | tf_op jit(solution)/shard_map/all_to_all | solution.py:395
  34.5 0.7 copy-start.2
  35.2 4.5 %copy-start.4 = (bf16[1024,512]{1,0:T(8,128)(2,1)S(1)}, bf16[1024,512]{1,0:T(8,128)(2,1)}, u32[]{:S(2)}) copy-start(bf16[1024,512]{1,0:T(8,128)(2,1)} %get-tuple-element.26.unit_ref) | copy-start | bytes 3145732
  35.2 9.6 %copy-start.1 = (s32[8,128]{1,0:T(8,128)S(1)}, s32[8,128]{1,0:T(8,128)}, u32[]{:S(2)}) copy-start(s32[8,128]{1,0:T(8,128)} %get-tuple-element.27.place_ref) | copy-start | bytes 12292
  37.2 7.6 %copy-start.5 = (bf16[1024,512]{1,0:T(8,128)(2,1)S(1)}, bf16[1024,512]{1,0:T(8,128)(2,1)}, u32[]{:S(2)}) copy-start(bf16[1024,512]{1,0:T(8,128)(2,1)} %get-tuple-element.26.unit_ref) | copy-start | bytes 3145732
  46.7 19.3 %all-to-all-start.2 = ((bf16[16,96,128]{2,1,0:T(8,128)(2,1)}), bf16[16,96,128]{2,1,0:T(8,128)(2,1)S(1)}, u32[]{:S(2)}, u32[]{:S(2)}) async-start(bf16[16,96,128]{2,1,0:T(8,128)(2,1)} %get-tuple-element.33), calls=%async_computation.2 | async-start | bytes 786432 | tf_op jit(solution)/shard_map/all_to_all | solution.py:395
  51.4 9.8 %collective-permute-start.1 = (bf16[1024,128]{1,0:T(8,128)(2,1)S(1)}, bf16[1024,128]{1,0:T(8,128)(2,1)S(1)}, u32[]{:S(2)}, u32[]{:S(2)}) collective-permute-start(bf16[1024,128]{1,0:T(8,128)(2,1)S(1)} %get-tuple-element.34), channel_id=1, source_target_pairs={{1,0},{2,1},{3,2},{4,3},{5,4},{6,5},{7,6},{8,7},{9,8},{10,9},{11,1... | collective-permute-start | bytes 786440 | tf_op jit(solution)/shard_map/ppermute | solution.py:391
  69.7 17.5 %all-to-all-start.3 = ((bf16[16,96,128]{2,1,0:T(8,128)(2,1)}), bf16[16,96,128]{2,1,0:T(8,128)(2,1)S(1)}, u32[]{:S(2)}, u32[]{:S(2)}) async-start(bf16[16,96,128]{2,1,0:T(8,128)(2,1)} %get-tuple-element.40), calls=%async_computation.3 | async-start | bytes 786432 | tf_op jit(solution)/shard_map/all_to_all | solution.py:395
  73.2 10.2 %collective-permute-start.2 = (bf16[1024,128]{1,0:T(8,128)(2,1)S(1)}, bf16[1024,128]{1,0:T(8,128)(2,1)S(1)}, u32[]{:S(2)}, u32[]{:S(2)}) collective-permute-start(bf16[1024,128]{1,0:T(8,128)(2,1)S(1)} %get-tuple-element.41), channel_id=1, source_target_pairs={{1,0},{2,1},{3,2},{4,3},{5,4},{6,5},{7,6},{8,7},{9,8},{10,9},{11,1... | collective-permute-start | bytes 786440 | tf_op jit(solution)/shard_map/ppermute | solution.py:391

commit v4 on v3

--- a/solution.py
+++ b/solution.py
@@ -15,8 +15,8 @@
 EXT = ROWS + BLK
 PAIR = 2 * BLK
 PAIRS = ROWS // PAIR
-SCORE_WIDE = 6 * ROWS
-BASE_WIDE = 3 * ROWS
+SCORE_DEEP = 24
+BASE_DEEP = 12
 WEIGHT_DEEP = 16 * TILES
 HALF = ROWS // 2
 
@@ -62,13 +62,25 @@
     return copies
 
 
-def moved(source_ref, to_ref, sems, pairs=range(PAIRS), source_at=0, to_at=0):
-    made = []
-    for r in pairs:
-        source = source_ref.at[:, pl.ds(r * PAIR + source_at, PAIR)]
-        to = to_ref.at[:, pl.ds(r * PAIR + to_at, PAIR)]
-        made.append(pltpu.make_async_copy(source, to, sems.at[r]))
-    return started(made)
+def arriving_pairs(pairs_any, to_ref, sems, count=PAIRS):
+    return started(
+        [
+            pltpu.make_async_copy(
+                pairs_any.at[r], to_ref.at[:, pl.ds(r * PAIR, PAIR)], sems.at[r]
+            )
+            for r in range(count)
+        ]
+    )
+
+
+def leaving_pair(from_ref, pairs_any, sems, r):
+    return started(
+        [
+            pltpu.make_async_copy(
+                from_ref.at[:, pl.ds(r * PAIR, PAIR)], pairs_any.at[r], sems.at[r]
+            )
+        ]
+    )
 
 
 def index_body(group_any, row_any, wanted_ref, place_ref, group_ref, row_ref, sems):
@@ -200,7 +212,7 @@
     w_copy.wait()
 
 
-def seed_body(labels_ref, prior_ref, seed_any, seed_ref, sem):
+def seed_body(labels_ref, prior_ref, seed_any, seed_ref, sems):
     labels = labels_ref[...]
     for k in range(CP // BLK):
         size = min(BLK, C - k * BLK)
@@ -211,13 +223,15 @@
         if size < BLK:
             seed = jnp.concatenate([seed, jnp.zeros((BLK - size, ROWS), F32)], axis=0)
         seed_ref[k * BLK : (k + 1) * BLK, :] = seed.astype(BF16)
-    copy = pltpu.make_async_copy(seed_ref, seed_any.at[:, pl.ds(0, ROWS)], sem)
-    copy.start()
-    copy.wait()
+    leaving = []
+    for r in range(PAIRS):
+        leaving += leaving_pair(seed_ref, seed_any, sems, r)
+    for copy in leaving:
+        copy.wait()
 
 
 def gather_seeds_body(asked_ref, seed_any, send_ref, head_ref, seed_ref, sems):
-    arriving = moved(seed_any, seed_ref, sems)
+    arriving = arriving_pairs(seed_any, seed_ref, sems)
     rows = request_rows(asked_ref)
     for copy in arriving:
         copy.wait()
@@ -275,16 +289,17 @@
 
 def near_first_body(
     named_ref, seed_any, rinv_ref, w_any, low_ref, high_any,
-    seed_ref, first_ref, w_ref, high_ref, sems, w_sem, high_sem,
+    seed_ref, first_ref, w_ref, high_ref, sems, w_sem, high_sems,
 ):
     w_copy = pltpu.make_async_copy(w_any.at[pl.ds(0, TILES)], w_ref, w_sem)
     w_copy.start()
-    arriving = moved(seed_any, seed_ref, sems)
+    arriving = arriving_pairs(seed_any, seed_ref, sems)
     for r in range(PAIRS):
         arriving[r].wait()
         cols = slice(r * PAIR, (r + 1) * PAIR)
         first_ref[:, cols] = (rinv_ref[0:1, cols] * seed_ref[:, cols].astype(F32)).astype(BF16)
     w_copy.wait()
+    leaving = []
     for r in reversed(range(TILES)):
         cols = slice(r * BLK, (r + 1) * BLK)
         weight = rinv_ref[0:1, cols]
@@ -294,20 +309,22 @@
             low_ref[:, cols] = total
         else:
             high_ref[:, r * BLK - HALF : (r + 1) * BLK - HALF] = total
-        if r == TILES // 2:
-            leaving = pltpu.make_async_copy(high_ref, high_any.at[:, pl.ds(0, HALF)], high_sem)
-            leaving.start()
-    leaving.wait()
+        if r >= TILES // 2 and r % 2 == 0:
+            leaving += leaving_pair(high_ref, high_any, high_sems, (r - TILES // 2) // 2)
+    for copy in leaving:
+        copy.wait()
 
 
 def near_second_body(
     named_ref, second_any, seed_any, rinv_ref, w_any, low_ref, high_any,
-    seed_ref, second_ref, w_ref, high_ref, sems, seed_sems, w_sem, high_sem,
+    seed_ref, second_ref, w_ref, high_ref, sems, seed_sems, w_sem, high_sems,
 ):
     arriving = started([pltpu.make_async_copy(w_any.at[pl.ds(0, TILES)], w_ref, w_sem)])
-    arriving += moved(second_any, second_ref, sems) + moved(seed_any, seed_ref, seed_sems)
+    arriving += arriving_pairs(second_any, second_ref, sems)
+    arriving += arriving_pairs(seed_any, seed_ref, seed_sems)
     for copy in arriving:
         copy.wait()
+    leaving = []
     for r in reversed(range(TILES)):
         cols = slice(r * BLK, (r + 1) * BLK)
         total = spread_near(named_ref, second_ref, w_ref, r)
@@ -316,10 +333,10 @@
             low_ref[:, cols] = total
         else:
             high_ref[:, r * BLK - HALF : (r + 1) * BLK - HALF] = total
-        if r == TILES // 2:
-            leaving = pltpu.make_async_copy(high_ref, high_any.at[:, pl.ds(0, HALF)], high_sem)
-            leaving.start()
-    leaving.wait()
+        if r >= TILES // 2 and r % 2 == 0:
+            leaving += leaving_pair(high_ref, high_any, high_sems, (r - TILES // 2) // 2)
+    for copy in leaving:
+        copy.wait()
 
 
 def far_scores(recv_ref, place_ref, next_ref, far_ref):
@@ -338,25 +355,24 @@
 
 def second_body(
     recv_ref, place_ref, asked_ref, next_ref, w_ref, low_ref, high_any, rinv_ref,
-    second_any, head_ref, send_ref, far_ref, high_ref, second_ref, high_sem, sems,
+    second_any, head_ref, send_ref, far_ref, high_ref, second_ref, high_sems, sems,
 ):
-    arriving = pltpu.make_async_copy(high_any.at[:, pl.ds(0, HALF)], high_ref, high_sem)
-    arriving.start()
+    arriving = arriving_pairs(high_any, high_ref, high_sems, PAIRS // 2)
     far_scores(recv_ref, place_ref, next_ref, far_ref)
     leaving = []
     for r in range(PAIRS):
         cols = slice(r * PAIR, (r + 1) * PAIR)
         total = dot(far_ref[...], w_ref[:, cols])
         weight = rinv_ref[0:1, cols]
-        if r == PAIRS // 2:
-            arriving.wait()
+        if r >= PAIRS // 2:
+            arriving[r - PAIRS // 2].wait()
         if r < PAIRS // 2:
             base = low_ref[:, cols]
         else:
             base = high_ref[:, r * PAIR - HALF : (r + 1) * PAIR - HALF]
         total = base.astype(F32) + (alpha_mix * weight * weight) * total
         second_ref[:, cols] = total.astype(BF16)
-        leaving += moved(second_ref, second_any, sems, [r])
+        leaving += leaving_pair(second_ref, second_any, sems, r)
     head_ref[...] = second_ref[:, :BLK]
     pack_rows(dot(request_rows(asked_ref), second_ref[...], NT), CP // BLK, send_ref)
     for copy in leaving:
@@ -365,23 +381,25 @@
 
 def last_body(
     recv_ref, place_ref, next_ref, w_ref, low_ref, high_any, rinv_ref,
-    out_any, far_ref, high_ref, out_ref, high_sem, sems,
+    out_any, far_ref, high_ref, out_ref, high_sems, sems,
 ):
-    arriving = pltpu.make_async_copy(high_any.at[:, pl.ds(0, HALF)], high_ref, high_sem)
-    arriving.start()
+    arriving = arriving_pairs(high_any, high_ref, high_sems, PAIRS // 2)
     far_scores(recv_ref, place_ref, next_ref, far_ref)
     leaving = []
     for r in range(PAIRS):
         cols = slice(r * PAIR, (r + 1) * PAIR)
         total = dot(far_ref[:C, :], w_ref[:, cols])
-        if r == PAIRS // 2:
-            arriving.wait()
+        if r >= PAIRS // 2:
+            arriving[r - PAIRS // 2].wait()
         if r < PAIRS // 2:
             base = low_ref[:C, cols]
         else:
             base = high_ref[:C, r * PAIR - HALF : (r + 1) * PAIR - HALF]
         out_ref[:, cols] = (base + (alpha_mix * rinv_ref[0:1, cols]) * total).astype(BF16)
-        leaving += moved(out_ref, out_any, sems, [r])
+        at = pl.ds(r * PAIR, PAIR)
+        leaving += started(
+            [pltpu.make_async_copy(out_ref.at[:, at], out_any.at[:, at], sems.at[r])]
+        )
     for copy in leaving:
         copy.wait()
 
@@ -418,7 +436,6 @@
         [((ROWS, D), BF16), ((BLK, D), BF16)],
         "vv",
         nbytes=4 * 10**6,
-        limit=60,
     )(desc, scales)
     next_units = passed_back(head)
     (send,) = call(gather_units_body, "gather_units", [((GROUPS, 48, BLK), BF16)], "vv")(asked, units)
@@ -431,9 +448,9 @@
         "hvv",
         scratch=[pltpu.VMEM((EXT, D), BF16), near_w_scratch, sem],
     )(named, units, next_units)
-    wide_shape = ((CP, SCORE_WIDE), BF16)
+    wide_shape = ((SCORE_DEEP, CP, PAIR), BF16)
     (seeds,) = call(
-        seed_body, "seeds", [wide_shape], "vv", "h", scratch=[plane, sem], nbytes=4 * 10**6
+        seed_body, "seeds", [wide_shape], "vv", "h", scratch=[plane, sems], nbytes=4 * 10**6
     )(labels.reshape(1, ROWS), jnp.transpose(prior))
     head_shape, send_shape = ((CP, BLK), BF16), ((GROUPS, 96, BLK), BF16)
     asked_seeds, seed_head = call(
@@ -455,7 +472,7 @@
         [((CP, HALF), BF16), wide_shape],
         "shvh",
         "vh",
-        scratch=[plane, plane, near_w_scratch, pltpu.VMEM((CP, HALF), BF16), sems, sem, sem],
+        scratch=[plane, plane, near_w_scratch, pltpu.VMEM((CP, HALF), BF16), sems, sem, sems],
         flops=2 * 10**9,
     )(named, seeds, rinv, near_w)
     second, head, send = call(
@@ -464,7 +481,7 @@
         [wide_shape, head_shape, send_shape],
         "vvvvvvhv",
         "hvv",
-        scratch=[far_scratch, pltpu.VMEM((CP, HALF), BF16), plane, sem, sems],
+        scratch=[far_scratch, pltpu.VMEM((CP, HALF), BF16), plane, sems, sems],
         limit=50,
     )(recv, place, asked, next_head, w, low, high, rinv)
     recv = exchanged(send)
@@ -472,10 +489,10 @@
     low, high = call(
         near_second_body,
         "near_second",
-        [((CP, HALF), F32), ((CP, BASE_WIDE), F32)],
+        [((CP, HALF), F32), ((BASE_DEEP, CP, PAIR), F32)],
         "shhvh",
         "vh",
-        scratch=[plane, plane, near_w_scratch, pltpu.VMEM((CP, HALF), F32), sems, sems, sem, sem],
+        scratch=[plane, plane, near_w_scratch, pltpu.VMEM((CP, HALF), F32), sems, sems, sem, sems],
         flops=2 * 10**9,
     )(named, second, seeds, rinv, near_w)
     (out,) = call(
@@ -485,7 +502,7 @@
         "vvvvvhv",
         "h",
         scratch=[
-            far_scratch, pltpu.VMEM((CP, HALF), F32), pltpu.VMEM((C, ROWS), BF16), sem, sems
+            far_scratch, pltpu.VMEM((CP, HALF), F32), pltpu.VMEM((C, ROWS), BF16), sems, sems
         ],
     )(recv, place, next_head, w, low, high, rinv)
     return jnp.transpose(out)

time: 92.1 us -> 91 us (0.988)
  Pallas kernels: 34 us -> 31.1 us
  waiting for transfers between devices: 13.8 us -> 15 us
    pallas_call x1, Pallas kernels: 3.31 us -> 1.11 us  [local(): call(unit_body, 'units', [((ROWS, D), BF16), ((BLK, D), BF16)], 'vv', nby...]
    ppermute x3, waiting for transfers between devices: 2.7 us -> 3.77 us  [passed_back(): return lax.ppermute(block, 'node', [(i, i - 1) for i in range(1, size)])]
    unnamed x13 -> x17, local copies, waits for them, and re-layouts: 2.68 us -> 3.4 us
  transfers between devices with their start and end apart: 7 -> 7, of which waited for: 5 -> 5; matrix products, arithmetic and copies ran while one was open for 1% -> 1% of each run, Pallas kernels for 25% -> 21%
where the time goes in v4:
time: 91 us; the launch traced here: 90.3 us
  starting transfers between devices  40.5 us (45%)
  Pallas kernels  31.1 us (34%)
  waiting for transfers between devices  15 us (16%)
  local copies, waits for them, and re-layouts  3.4 us (4%)
    all_to_all x4, starting transfers between devices, exchanged(): lax.all_to_all(block, 'group', split_axis=0, concat_axis=0, tiled=True)  23.4 us
    ppermute x3, starting transfers between devices, passed_back(): return lax.ppermute(block, 'node', [(i, i - 1) for i in range(1, size)])  17.1 us
    all_to_all x4, waiting for transfers between devices, exchanged(): lax.all_to_all(block, 'group', split_axis=0, concat_axis=0, tiled=True)  11.2 us
    pallas_call x1, Pallas kernels, local(): call(near_second_body, 'near_second', [((CP, HALF), F32), ((BASE_DEEP, CP...  5.51 us
    pallas_call x1, Pallas kernels, local(): call(near_first_body, 'near_first', [((CP, HALF), BF16), wide_shape], 'sh...  4.5 us
    pallas_call x1, Pallas kernels, local(): call(second_body, 'second', [wide_shape, head_shape, send_shape], 'vvvvvv...  4.35 us
    pallas_call x1, Pallas kernels, local(): call(last_body, 'last', [((C, ROWS), BF16)], 'vvvvvhv', 'h', scratch=[far...  3.9 us
    ppermute x3, waiting for transfers between devices, passed_back(): return lax.ppermute(block, 'node', [(i, i - 1) for i in range(1, size)])  3.77 us
  transfers between devices with their start and end apart: 7, of which 5 were waited for; matrix products, arithmetic and copies ran while one was open for 1% of the time, Pallas kernels for 21%

profile of v4, /device:TPU:7, one launch (start us, length us, event | category | flops | bytes accessed | tf_op | source)
XLA Modules:
  0.0 90.3 jit_solution(1026710111801400003)
XLA Ops:
  0.0 1.7 %index.1 = (s32[16,1,128]{2,1,0:T(1,128)}, s32[8,128]{1,0:T(8,128)}) custom-call(s32[1,128]{1,0:T(1,128)} %bitcast.7, s32[1,128]{1,0:T(1,128)} %bitcast.8), custom_call_target="tpu_custom_call" | custom-call | flops 1000000000 | bytes 1000000 | tf_op jit(solution)/shard_map/index/pallas_call | solution.py:424
  1.7 7.8 %all-to-all-start = ((s32[16,1,128]{2,1,0:T(1,128)}), s32[16,1,128]{2,1,0:T(1,128)S(1)}, u32[]{:S(2)}, u32[]{:S(2)}) async-start(s32[16,1,128]{2,1,0:T(1,128)} %get-tuple-element.25), calls=%async_computation | async-start | bytes 16384 | tf_op jit(solution)/shard_map/all_to_all | solution.py:413
  9.6 1.2 %copy-done.3 = bf16[1024,512]{1,0:T(8,128)(2,1)S(1)} copy-done((bf16[1024,512]{1,0:T(8,128)(2,1)S(1)}, bf16[1024,512]{1,0:T(8,128)(2,1)}, u32[]{:S(2)}) %copy-start.3) | copy-done | bytes 1048600
  11.5 1.1 %units.1 = (bf16[1024,512]{1,0:T(8,128)(2,1)S(1)}, bf16[128,512]{1,0:T(8,128)(2,1)S(1)}) custom-call(bf16[1024,512]{1,0:T(8,128)(2,1)S(1)} %copy-done.3, f32[4,1024]{1,0:T(4,128)S(1)} %copy-done.4), custom_call_target="tpu_custom_call" | custom-call | flops 1000000000 | bytes 4000000 | tf_op jit(solution)/shard_map/units/pallas_call | solution.py:433
  12.6 11.0 %collective-permute-start = (bf16[128,512]{1,0:T(8,128)(2,1)S(1)}, bf16[128,512]{1,0:T(8,128)(2,1)S(1)}, u32[]{:S(2)}, u32[]{:S(2)}) collective-permute-start(bf16[128,512]{1,0:T(8,128)(2,1)S(1)} %get-tuple-element.28), channel_id=1, source_target_pairs={{1,0},{2,1},{3,2},{4,3},{5,4},{6,5},{7,6},{8,7},{9,8},{10,9},{11,1... | collective-permute-start | bytes 393224 | tf_op jit(solution)/shard_map/ppermute | solution.py:409
  23.6 0.8 copy.8
  24.3 1.2 %gather_units.1 = bf16[16,48,128]{2,1,0:T(8,128)(2,1)} custom-call(s32[16,1,128]{2,1,0:T(1,128)S(1)} %all-to-all-done.asked_ref, bf16[1024,512]{1,0:T(8,128)(2,1)S(1)} %get-tuple-element.26.unit_ref), custom_call_target="tpu_custom_call" | custom-call | flops 1000000000 | bytes 1000000 | tf_op jit(solution)/shard_map/gather_units/pallas_call | solution.py:441
  25.5 7.5 %all-to-all-start.1 = ((bf16[16,48,128]{2,1,0:T(8,128)(2,1)}), bf16[16,48,128]{2,1,0:T(8,128)(2,1)S(1)}, u32[]{:S(2)}, u32[]{:S(2)}) async-start(bf16[16,48,128]{2,1,0:T(8,128)(2,1)} %gather_units.1), calls=%async_computation.1 | async-start | bytes 393216 | tf_op jit(solution)/shard_map/all_to_all | solution.py:413
  33.7 2.0 %seeds.1.seed_any = bf16[24,1024,256]{2,1,0:T(8,128)(2,1)} custom-call(s32[1,1024]{1,0:T(1,128)S(1)} %bitcast.6, bf16[1000,1024]{1,0:T(8,128)(2,1)S(1)} %bitcast.5), custom_call_target="tpu_custom_call" | custom-call | flops 1000000000 | bytes 4000000 | tf_op jit(solution)/shard_map/seeds/pallas_call | solution.py:452
  35.7 2.5 %gather_seeds.1 = (bf16[16,96,128]{2,1,0:T(8,128)(2,1)S(1)}, bf16[1024,128]{1,0:T(8,128)(2,1)S(1)}) custom-call(s32[16,1,128]{2,1,0:T(1,128)S(1)} %all-to-all-done.asked_ref, bf16[24,1024,256]{2,1,0:T(8,128)(2,1)} %seeds.1.seed_any), custom_call_target="tpu_custom_call" | custom-call | flops 1000000000 | bytes 1000000 | tf_op jit(solution)/shard_map/gather_seeds/pallas_call | solution.py:456
  38.2 2.5 %near.1 = (bf16[128,384,128]{2,1,0:T(8,128)(2,1)}, bf16[128,1024]{1,0:T(8,128)(2,1)S(1)}, f32[8,128]{1,0:T(8,128)S(1)}) custom-call(s32[8,2]{1,0:T(8,128)S(1)} %broadcast_subtract_fusion.named_ref, bf16[1024,512]{1,0:T(8,128)(2,1)S(1)} %copy-done.6, bf16[128,512]{1,0:T(8,128)(2,1)S(1)} %collective-permute-done.next_ref), custom_call_target="tpu_custom_call" | custom-call | flops 1000000000 | bytes 1000000 | tf_op jit(solution)/shard_map/near/pallas_call | solution.py:443
  40.7 2.6 %all-to-all-done.1.recv_ref = bf16[16,48,128]{2,1,0:T(8,128)(2,1)S(1)} async-done(((bf16[16,48,128]{2,1,0:T(8,128)(2,1)}), bf16[16,48,128]{2,1,0:T(8,128)(2,1)S(1)}, u32[]{:S(2)}, u32[]{:S(2)}) %all-to-all-start.1) | async-done | bytes 196640 | tf_op jit(solution)/shard_map/all_to_all | solution.py:413
  43.4 1.9 %degree.1 = (bf16[256,1024]{1,0:T(8,128)(2,1)S(1)}, f32[1,1024]{1,0:T(1,128)S(1)}, bf16[1024,128]{1,0:T(8,128)(2,1)S(1)}, bf16[16,96,128]{2,1,0:T(8,128)(2,1)}) custom-call(bf16[16,48,128]{2,1,0:T(8,128)(2,1)S(1)} %all-to-all-done.1.recv_ref, s32[8,128]{1,0:T(8,128)S(1)} %copy-done.1, s32[16,1,128]{2,1,0:T(1,128)S(1)} %all-to-all-done.asked_ref, ...), custom_call_target="tpu_custom_call" | custom-call | flops 1000000000 | bytes 1000000 | tf_op jit(solution)/shard_map/degree/pallas_call | solution.py:459
  45.2 4.6 %all-to-all-start.2 = ((bf16[16,96,128]{2,1,0:T(8,128)(2,1)}), bf16[16,96,128]{2,1,0:T(8,128)(2,1)S(1)}, u32[]{:S(2)}, u32[]{:S(2)}) async-start(bf16[16,96,128]{2,1,0:T(8,128)(2,1)} %get-tuple-element.33), calls=%async_computation.2 | async-start | bytes 786432 | tf_op jit(solution)/shard_map/all_to_all | solution.py:413
  49.8 2.2 %collective-permute-start.1 = (bf16[1024,128]{1,0:T(8,128)(2,1)S(1)}, bf16[1024,128]{1,0:T(8,128)(2,1)S(1)}, u32[]{:S(2)}, u32[]{:S(2)}) collective-permute-start(bf16[1024,128]{1,0:T(8,128)(2,1)S(1)} %get-tuple-element.34), channel_id=1, source_target_pairs={{1,0},{2,1},{3,2},{4,3},{5,4},{6,5},{7,6},{8,7},{9,8},{10,9},{11,1... | collective-permute-start | bytes 786440 | tf_op jit(solution)/shard_map/ppermute | solution.py:409
  52.1 4.5 %near_first.1 = (bf16[1024,512]{1,0:T(8,128)(2,1)S(1)}, bf16[24,1024,256]{2,1,0:T(8,128)(2,1)}) custom-call(s32[8,2]{1,0:T(8,128)S(1)} %broadcast_subtract_fusion.named_ref, bf16[24,1024,256]{2,1,0:T(8,128)(2,1)} %seeds.1.seed_any, f32[1,1024]{1,0:T(1,128)S(1)} %get-tuple-element.36.rinv_ref, bf16[128,384,128]{2,1,0:T(8,128)(2,1)} %get-tuple-element.37.w_any), custom_call_target="tpu_custom_call" | custom-call | flops 2000000000 | bytes 1000000 | tf_op jit(solution)/shard_map/near_first/pallas_call | solution.py:469
  56.6 3.0 %collective-permute-done.1.next_ref = bf16[1024,128]{1,0:T(8,128)(2,1)S(1)} collective-permute-done((bf16[1024,128]{1,0:T(8,128)(2,1)S(1)}, bf16[1024,128]{1,0:T(8,128)(2,1)S(1)}, u32[]{:S(2)}, u32[]{:S(2)}) %collective-permute-start.1) | collective-permute-done | bytes 262176 | tf_op jit(solution)/shard_map/ppermute | solution.py:409
  59.6 4.8 %all-to-all-done.2.recv_ref = bf16[16,96,128]{2,1,0:T(8,128)(2,1)S(1)} async-done(((bf16[16,96,128]{2,1,0:T(8,128)(2,1)}), bf16[16,96,128]{2,1,0:T(8,128)(2,1)S(1)}, u32[]{:S(2)}, u32[]{:S(2)}) %all-to-all-start.2) | async-done | bytes 393248 | tf_op jit(solution)/shard_map/all_to_all | solution.py:413
  64.4 4.3 %second.1 = (bf16[24,1024,256]{2,1,0:T(8,128)(2,1)}, bf16[1024,128]{1,0:T(8,128)(2,1)S(1)}, bf16[16,96,128]{2,1,0:T(8,128)(2,1)}) custom-call(bf16[16,96,128]{2,1,0:T(8,128)(2,1)S(1)} %all-to-all-done.2.recv_ref, s32[8,128]{1,0:T(8,128)S(1)} %copy-done.1, s32[16,1,128]{2,1,0:T(1,128)S(1)} %all-to-all-done.asked_ref, ...), custom_call_target="tpu_custom_call" | custom-call | flops 1000000000 | bytes 1000000 | tf_op jit(solution)/shard_map/second/pallas_call | solution.py:478
  68.8 3.5 %all-to-all-start.3 = ((bf16[16,96,128]{2,1,0:T(8,128)(2,1)}), bf16[16,96,128]{2,1,0:T(8,128)(2,1)S(1)}, u32[]{:S(2)}, u32[]{:S(2)}) async-start(bf16[16,96,128]{2,1,0:T(8,128)(2,1)} %get-tuple-element.40), calls=%async_computation.3 | async-start | bytes 786432 | tf_op jit(solution)/shard_map/all_to_all | solution.py:413
  72.2 4.0 %collective-permute-start.2 = (bf16[1024,128]{1,0:T(8,128)(2,1)S(1)}, bf16[1024,128]{1,0:T(8,128)(2,1)S(1)}, u32[]{:S(2)}, u32[]{:S(2)}) collective-permute-start(bf16[1024,128]{1,0:T(8,128)(2,1)S(1)} %get-tuple-element.41), channel_id=1, source_target_pairs={{1,0},{2,1},{3,2},{4,3},{5,4},{6,5},{7,6},{8,7},{9,8},{10,9},{11,1... | collective-permute-start | bytes 786440 | tf_op jit(solution)/shard_map/ppermute | solution.py:409
  76.2 5.5 %near_second.1 = (f32[1024,512]{1,0:T(8,128)S(1)}, f32[12,1024,256]{2,1,0:T(8,128)}) custom-call(s32[8,2]{1,0:T(8,128)S(1)} %broadcast_subtract_fusion.named_ref, bf16[24,1024,256]{2,1,0:T(8,128)(2,1)} %get-tuple-element.42.second_any, bf16[24,1024,256]{2,1,0:T(8,128)(2,1)} %seeds.1.seed_any, f32[1,1024]{1,0:T(1,128)S(1)} %get-tuple-element.36.rinv_ref, ...), custom_call_target="tpu_custom_call" | custom-call | flops 2000000000 | bytes 1000000 | tf_op jit(solution)/shard_map/near_second/pallas_call | solution.py:489
  82.4 3.8 %all-to-all-done.3.recv_ref = bf16[16,96,128]{2,1,0:T(8,128)(2,1)S(1)} async-done(((bf16[16,96,128]{2,1,0:T(8,128)(2,1)}), bf16[16,96,128]{2,1,0:T(8,128)(2,1)S(1)}, u32[]{:S(2)}, u32[]{:S(2)}) %all-to-all-start.3) | async-done | bytes 393248 | tf_op jit(solution)/shard_map/all_to_all | solution.py:413
  86.2 3.9 %last.1 = bf16[1000,1024]{1,0:T(8,128)(2,1)} custom-call(bf16[16,96,128]{2,1,0:T(8,128)(2,1)S(1)} %all-to-all-done.3.recv_ref, s32[8,128]{1,0:T(8,128)S(1)} %copy-done.1, bf16[1024,128]{1,0:T(8,128)(2,1)S(1)} %collective-permute-done.2.next_ref, bf16[256,1024]{1,0:T(8,128)(2,1)S(1)} %get-tuple-element.35.w_ref, f32[1024,512]{1,0:T(8,128)S(1)} %get-tuple-element.43.low_ref, ...), custom_call_target="tpu_custom_call" | custom-call | flops 1000000000 | bytes 1000000 | tf_op jit(solution)/shard_map/last/pallas_call | solution.py:498
  (19 shorter events, 2.2 us)
Async XLA Ops:
  0.0 33.0 %copy-start = (bf16[1024,1000]{0,1:T(8,128)(2,1)S(1)}, bf16[1024,1000]{0,1:T(8,128)(2,1)}, u32[]{:S(2)}) copy-start(bf16[1024,1000]{0,1:T(8,128)(2,1)} %param.10) | copy-start | bytes 6144004
  1.7 22.6 %all-to-all-start = ((s32[16,1,128]{2,1,0:T(1,128)}), s32[16,1,128]{2,1,0:T(1,128)S(1)}, u32[]{:S(2)}, u32[]{:S(2)}) async-start(s32[16,1,128]{2,1,0:T(1,128)} %get-tuple-element.25), calls=%async_computation | async-start | bytes 16384 | tf_op jit(solution)/shard_map/all_to_all | solution.py:413
  9.5 1.2 %copy-start.3 = (bf16[1024,512]{1,0:T(8,128)(2,1)S(1)}, bf16[1024,512]{1,0:T(8,128)(2,1)}, u32[]{:S(2)}) copy-start(bf16[1024,512]{1,0:T(8,128)(2,1)} %desc_ref.1) | copy-start | bytes 3145732
  10.8 0.7 copy-start.4
  12.6 12.9 %copy-start.5 = (bf16[1024,512]{1,0:T(8,128)(2,1)}, bf16[1024,512]{1,0:T(8,128)(2,1)S(1)}, u32[]{:S(2)}) copy-start(bf16[1024,512]{1,0:T(8,128)(2,1)S(1)} %get-tuple-element.26.unit_ref) | copy-start | bytes 3145732
  12.6 25.6 %collective-permute-start = (bf16[128,512]{1,0:T(8,128)(2,1)S(1)}, bf16[128,512]{1,0:T(8,128)(2,1)S(1)}, u32[]{:S(2)}, u32[]{:S(2)}) collective-permute-start(bf16[128,512]{1,0:T(8,128)(2,1)S(1)} %get-tuple-element.28), channel_id=1, source_target_pairs={{1,0},{2,1},{3,2},{4,3},{5,4},{6,5},{7,6},{8,7},{9,8},{10,9},{11,1... | collective-permute-start | bytes 393224 | tf_op jit(solution)/shard_map/ppermute | solution.py:409
  25.5 17.8 %all-to-all-start.1 = ((bf16[16,48,128]{2,1,0:T(8,128)(2,1)}), bf16[16,48,128]{2,1,0:T(8,128)(2,1)S(1)}, u32[]{:S(2)}, u32[]{:S(2)}) async-start(bf16[16,48,128]{2,1,0:T(8,128)(2,1)} %gather_units.1), calls=%async_computation.1 | async-start | bytes 393216 | tf_op jit(solution)/shard_map/all_to_all | solution.py:413
  33.0 0.7 copy-start.2
  33.7 4.5 %copy-start.6 = (bf16[1024,512]{1,0:T(8,128)(2,1)S(1)}, bf16[1024,512]{1,0:T(8,128)(2,1)}, u32[]{:S(2)}) copy-start(bf16[1024,512]{1,0:T(8,128)(2,1)} %copy-done.5) | copy-start | bytes 3145732
  33.7 9.6 %copy-start.1 = (s32[8,128]{1,0:T(8,128)S(1)}, s32[8,128]{1,0:T(8,128)}, u32[]{:S(2)}) copy-start(s32[8,128]{1,0:T(8,128)} %get-tuple-element.27.place_ref) | copy-start | bytes 12292
  35.7 7.7 %copy-start.7 = (bf16[1024,512]{1,0:T(8,128)(2,1)S(1)}, bf16[1024,512]{1,0:T(8,128)(2,1)}, u32[]{:S(2)}) copy-start(bf16[1024,512]{1,0:T(8,128)(2,1)} %copy-done.5) | copy-start | bytes 3145732
  45.2 19.2 %all-to-all-start.2 = ((bf16[16,96,128]{2,1,0:T(8,128)(2,1)}), bf16[16,96,128]{2,1,0:T(8,128)(2,1)S(1)}, u32[]{:S(2)}, u32[]{:S(2)}) async-start(bf16[16,96,128]{2,1,0:T(8,128)(2,1)} %get-tuple-element.33), calls=%async_computation.2 | async-start | bytes 786432 | tf_op jit(solution)/shard_map/all_to_all | solution.py:413
  49.8 9.8 %collective-permute-start.1 = (bf16[1024,128]{1,0:T(8,128)(2,1)S(1)}, bf16[1024,128]{1,0:T(8,128)(2,1)S(1)}, u32[]{:S(2)}, u32[]{:S(2)}) collective-permute-start(bf16[1024,128]{1,0:T(8,128)(2,1)S(1)} %get-tuple-element.34), channel_id=1, source_target_pairs={{1,0},{2,1},{3,2},{4,3},{5,4},{6,5},{7,6},{8,7},{9,8},{10,9},{11,1... | collective-permute-start | bytes 786440 | tf_op jit(solution)/shard_map/ppermute | solution.py:409
  68.8 17.5 %all-to-all-start.3 = ((bf16[16,96,128]{2,1,0:T(8,128)(2,1)}), bf16[16,96,128]{2,1,0:T(8,128)(2,1)S(1)}, u32[]{:S(2)}, u32[]{:S(2)}) async-start(bf16[16,96,128]{2,1,0:T(8,128)(2,1)} %get-tuple-element.40), calls=%async_computation.3 | async-start | bytes 786432 | tf_op jit(solution)/shard_map/all_to_all | solution.py:413
  72.2 10.2 %collective-permute-start.2 = (bf16[1024,128]{1,0:T(8,128)(2,1)S(1)}, bf16[1024,128]{1,0:T(8,128)(2,1)S(1)}, u32[]{:S(2)}, u32[]{:S(2)}) collective-permute-start(bf16[1024,128]{1,0:T(8,128)(2,1)S(1)} %get-tuple-element.41), channel_id=1, source_target_pairs={{1,0},{2,1},{3,2},{4,3},{5,4},{6,5},{7,6},{8,7},{9,8},{10,9},{11,1... | collective-permute-start | bytes 786440 | tf_op jit(solution)/shard_map/ppermute | solution.py:409

commit v5 on v4

--- a/solution.py
+++ b/solution.py
@@ -16,9 +16,7 @@
 PAIR = 2 * BLK
 PAIRS = ROWS // PAIR
 SCORE_DEEP = 24
-BASE_DEEP = 12
 WEIGHT_DEEP = 16 * TILES
-HALF = ROWS // 2
 
 alpha_mix = 0.8
 eps_norm = 1e-06
@@ -212,37 +210,38 @@
     w_copy.wait()
 
 
-def seed_body(labels_ref, prior_ref, seed_any, seed_ref, sems):
-    labels = labels_ref[...]
-    for k in range(CP // BLK):
-        size = min(BLK, C - k * BLK)
-        prior = prior_ref[k * BLK : k * BLK + size, :].astype(F32)
-        classes = iota((size, ROWS), 0) + k * BLK
-        hot = jnp.where(classes == labels, 1.0, 0.0)
-        seed = jnp.where(labels >= 0, hot, prior)
-        if size < BLK:
-            seed = jnp.concatenate([seed, jnp.zeros((BLK - size, ROWS), F32)], axis=0)
-        seed_ref[k * BLK : (k + 1) * BLK, :] = seed.astype(BF16)
+def seed_body(
+    asked_ref, labels_ref, prior_any, send_ref, head_ref, seed_any,
+    prior_ref, seed_ref, in_sems, sems,
+):
+    arriving = []
+    for r in range(PAIRS):
+        at = pl.ds(r * PAIR, PAIR)
+        arriving += started(
+            [pltpu.make_async_copy(prior_any.at[:, at], prior_ref.at[:, at], in_sems.at[r])]
+        )
+    rows = request_rows(asked_ref)
+    seed_ref[CP - 32 :, :] = jnp.zeros((32, ROWS), BF16)
     leaving = []
     for r in range(PAIRS):
+        cols = slice(r * PAIR, (r + 1) * PAIR)
+        labels = labels_ref[:, cols]
+        arriving[r].wait()
+        hot = jnp.where(iota((C, PAIR), 0) == labels, 1.0, 0.0)
+        seed = jnp.where(labels >= 0, hot, prior_ref[:, cols].astype(F32))
+        seed_ref[:C, cols] = seed.astype(BF16)
         leaving += leaving_pair(seed_ref, seed_any, sems, r)
+    head_ref[...] = seed_ref[:, :BLK]
+    pack_rows(dot(rows, seed_ref[...], NT), CP // BLK, send_ref)
     for copy in leaving:
         copy.wait()
 
 
-def gather_seeds_body(asked_ref, seed_any, send_ref, head_ref, seed_ref, sems):
-    arriving = arriving_pairs(seed_any, seed_ref, sems)
-    rows = request_rows(asked_ref)
-    for copy in arriving:
-        copy.wait()
-    head_ref[...] = seed_ref[:, :BLK]
-    pack_rows(dot(rows, seed_ref[...], NT), CP // BLK, send_ref)
-
-
 def degree_body(
     recv_ref, place_ref, asked_ref, unit_ref, near_ref, after_ref, asked_seed_ref, seed_ref,
-    w_ref, rinv_ref, head_ref, send_ref, far_ref,
+    w_any, rinv_ref, head_ref, send_ref, far_ref, w_ref, w_sem,
 ):
+    w_ref[BLK:, :] = after_ref[...]
     low, high = placers(place_ref)
     for m in range(D // (4 * BLK)):
         deep = dot(high, received(recv_ref, 8 * D // BLK + 16 * m), TN)
@@ -268,11 +267,13 @@
         spread = jnp.broadcast_to(rinv.reshape(1, 1, BLK), (GROUPS, 16, BLK))
         for k, column in enumerate(columns):
             found[k] = jnp.where(node + float(r * BLK) == column, spread, found[k])
-    w_ref[BLK:, :] = after_ref[...]
+    w_copy = pltpu.make_async_copy(w_ref, w_any.at[0], w_sem)
+    w_copy.start()
     weights = [jnp.sum(values, axis=2, keepdims=True) for values in found]
     for k in range(6):
         part = asked_seed_ref[:, 16 * k : 16 * (k + 1), :].astype(F32)
         send_ref[:, 16 * k : 16 * (k + 1), :] = (weights[k // 4] * part).astype(BF16)
+    w_copy.wait()
 
 
 def spread_near(named_ref, source_ref, w_ref, r):
@@ -287,10 +288,7 @@
     return (alpha_mix * weight) * total + (1.0 - alpha_mix) * seed.astype(F32)
 
 
-def near_first_body(
-    named_ref, seed_any, rinv_ref, w_any, low_ref, high_any,
-    seed_ref, first_ref, w_ref, high_ref, sems, w_sem, high_sems,
-):
+def near_first_body(named_ref, seed_any, rinv_ref, w_any, base_ref, seed_ref, first_ref, w_ref, sems, w_sem):
     w_copy = pltpu.make_async_copy(w_any.at[pl.ds(0, TILES)], w_ref, w_sem)
     w_copy.start()
     arriving = arriving_pairs(seed_any, seed_ref, sems)
@@ -299,44 +297,28 @@
         cols = slice(r * PAIR, (r + 1) * PAIR)
         first_ref[:, cols] = (rinv_ref[0:1, cols] * seed_ref[:, cols].astype(F32)).astype(BF16)
     w_copy.wait()
-    leaving = []
-    for r in reversed(range(TILES)):
+    for r in range(TILES):
         cols = slice(r * BLK, (r + 1) * BLK)
         weight = rinv_ref[0:1, cols]
         total = spread_near(named_ref, first_ref, w_ref, r)
-        total = (weight * mixed_near(total, weight, seed_ref[:, cols])).astype(BF16)
-        if r < TILES // 2:
-            low_ref[:, cols] = total
-        else:
-            high_ref[:, r * BLK - HALF : (r + 1) * BLK - HALF] = total
-        if r >= TILES // 2 and r % 2 == 0:
-            leaving += leaving_pair(high_ref, high_any, high_sems, (r - TILES // 2) // 2)
-    for copy in leaving:
-        copy.wait()
+        base_ref[:, cols] = (weight * mixed_near(total, weight, seed_ref[:, cols])).astype(BF16)
 
 
 def near_second_body(
-    named_ref, second_any, seed_any, rinv_ref, w_any, low_ref, high_any,
-    seed_ref, second_ref, w_ref, high_ref, sems, seed_sems, w_sem, high_sems,
+    named_ref, second_any, seed_any, rinv_ref, w_any, base_ref,
+    second_ref, seed_ref, w_ref, sems, seed_sems, w_sem,
 ):
-    arriving = started([pltpu.make_async_copy(w_any.at[pl.ds(0, TILES)], w_ref, w_sem)])
-    arriving += arriving_pairs(second_any, second_ref, sems)
-    arriving += arriving_pairs(seed_any, seed_ref, seed_sems)
+    arriving = arriving_pairs(second_any, second_ref, sems)
+    arriving += started([pltpu.make_async_copy(w_any.at[pl.ds(0, TILES)], w_ref, w_sem)])
+    seeds = arriving_pairs(seed_any, seed_ref, seed_sems)
     for copy in arriving:
         copy.wait()
-    leaving = []
-    for r in reversed(range(TILES)):
+    for r in range(TILES):
         cols = slice(r * BLK, (r + 1) * BLK)
         total = spread_near(named_ref, second_ref, w_ref, r)
-        total = mixed_near(total, rinv_ref[0:1, cols], seed_ref[:, cols])
-        if r < TILES // 2:
-            low_ref[:, cols] = total
-        else:
-            high_ref[:, r * BLK - HALF : (r + 1) * BLK - HALF] = total
-        if r >= TILES // 2 and r % 2 == 0:
-            leaving += leaving_pair(high_ref, high_any, high_sems, (r - TILES // 2) // 2)
-    for copy in leaving:
-        copy.wait()
+        if r % 2 == 0:
+            seeds[r // 2].wait()
+        base_ref[:, cols] = mixed_near(total, rinv_ref[0:1, cols], seed_ref[:, cols]).astype(BF16)
 
 
 def far_scores(recv_ref, place_ref, next_ref, far_ref):
@@ -354,23 +336,19 @@
 
 
 def second_body(
-    recv_ref, place_ref, asked_ref, next_ref, w_ref, low_ref, high_any, rinv_ref,
-    second_any, head_ref, send_ref, far_ref, high_ref, second_ref, high_sems, sems,
+    recv_ref, place_ref, asked_ref, next_ref, w_any, base_ref, rinv_ref,
+    second_any, head_ref, send_ref, far_ref, w_ref, second_ref, w_sem, sems,
 ):
-    arriving = arriving_pairs(high_any, high_ref, high_sems, PAIRS // 2)
+    w_copy = pltpu.make_async_copy(w_any.at[0], w_ref, w_sem)
+    w_copy.start()
     far_scores(recv_ref, place_ref, next_ref, far_ref)
+    w_copy.wait()
     leaving = []
     for r in range(PAIRS):
         cols = slice(r * PAIR, (r + 1) * PAIR)
         total = dot(far_ref[...], w_ref[:, cols])
         weight = rinv_ref[0:1, cols]
-        if r >= PAIRS // 2:
-            arriving[r - PAIRS // 2].wait()
-        if r < PAIRS // 2:
-            base = low_ref[:, cols]
-        else:
-            base = high_ref[:, r * PAIR - HALF : (r + 1) * PAIR - HALF]
-        total = base.astype(F32) + (alpha_mix * weight * weight) * total
+        total = base_ref[:, cols].astype(F32) + (alpha_mix * weight * weight) * total
         second_ref[:, cols] = total.astype(BF16)
         leaving += leaving_pair(second_ref, second_any, sems, r)
     head_ref[...] = second_ref[:, :BLK]
@@ -380,22 +358,19 @@
 
 
 def last_body(
-    recv_ref, place_ref, next_ref, w_ref, low_ref, high_any, rinv_ref,
-    out_any, far_ref, high_ref, out_ref, high_sems, sems,
+    recv_ref, place_ref, next_ref, w_any, base_ref, rinv_ref,
+    out_any, far_ref, w_ref, out_ref, w_sem, sems,
 ):
-    arriving = arriving_pairs(high_any, high_ref, high_sems, PAIRS // 2)
+    w_copy = pltpu.make_async_copy(w_any.at[0], w_ref, w_sem)
+    w_copy.start()
     far_scores(recv_ref, place_ref, next_ref, far_ref)
+    w_copy.wait()
     leaving = []
     for r in range(PAIRS):
         cols = slice(r * PAIR, (r + 1) * PAIR)
         total = dot(far_ref[:C, :], w_ref[:, cols])
-        if r >= PAIRS // 2:
-            arriving[r - PAIRS // 2].wait()
-        if r < PAIRS // 2:
-            base = low_ref[:C, cols]
-        else:
-            base = high_ref[:C, r * PAIR - HALF : (r + 1) * PAIR - HALF]
-        out_ref[:, cols] = (base + (alpha_mix * rinv_ref[0:1, cols]) * total).astype(BF16)
+        total = base_ref[:C, cols].astype(F32) + (alpha_mix * rinv_ref[0:1, cols]) * total
+        out_ref[:, cols] = total.astype(BF16)
         at = pl.ds(r * PAIR, PAIR)
         leaving += started(
             [pltpu.make_async_copy(out_ref.at[:, at], out_any.at[:, at], sems.at[r])]
@@ -420,6 +395,7 @@
     row_vector = pltpu.VMEM((1, BLK), jnp.int32)
     plane = pltpu.VMEM((CP, ROWS), BF16)
     far_scratch = pltpu.VMEM((CP, 2 * BLK), BF16)
+    w_scratch = pltpu.VMEM((2 * BLK, ROWS), BF16)
     near_w_scratch = pltpu.VMEM((TILES, 3 * BLK, BLK), BF16)
     wanted, place = call(
         index_body,
@@ -449,62 +425,64 @@
         scratch=[pltpu.VMEM((EXT, D), BF16), near_w_scratch, sem],
     )(named, units, next_units)
     wide_shape = ((SCORE_DEEP, CP, PAIR), BF16)
-    (seeds,) = call(
-        seed_body, "seeds", [wide_shape], "vv", "h", scratch=[plane, sems], nbytes=4 * 10**6
-    )(labels.reshape(1, ROWS), jnp.transpose(prior))
     head_shape, send_shape = ((CP, BLK), BF16), ((GROUPS, 96, BLK), BF16)
-    asked_seeds, seed_head = call(
-        gather_seeds_body, "gather_seeds", [send_shape, head_shape], "vh", scratch=[plane, sems]
-    )(asked, seeds)
+    asked_seeds, seed_head, seeds = call(
+        seed_body,
+        "seeds",
+        [send_shape, head_shape, wide_shape],
+        "vvh",
+        "vvh",
+        scratch=[pltpu.VMEM((C, ROWS), BF16), plane, sems, sems],
+        flops=2 * 10**9,
+        limit=53,
+    )(asked, labels.reshape(1, ROWS), jnp.transpose(prior))
     w, rinv, head, send = call(
         degree_body,
         "degree",
-        [((2 * BLK, ROWS), BF16), ((1, ROWS), F32), head_shape, send_shape],
+        [((SCORE_DEEP, 2 * BLK, ROWS), BF16), ((1, ROWS), F32), head_shape, send_shape],
         "vvvvvvvv",
-        scratch=[pltpu.VMEM((BLK, D), BF16)],
+        "hvvv",
+        scratch=[pltpu.VMEM((BLK, D), BF16), w_scratch, sem],
         limit=50,
     )(far_units, place, asked, units, near_degree, after_w, asked_seeds, seed_head)
     recv = exchanged(send)
     next_head = passed_back(head)
-    low, high = call(
+    scores_shape = ((CP, ROWS), BF16)
+    (base,) = call(
         near_first_body,
         "near_first",
-        [((CP, HALF), BF16), wide_shape],
+        [scores_shape],
         "shvh",
-        "vh",
-        scratch=[plane, plane, near_w_scratch, pltpu.VMEM((CP, HALF), BF16), sems, sem, sems],
+        scratch=[plane, plane, near_w_scratch, sems, sem],
         flops=2 * 10**9,
     )(named, seeds, rinv, near_w)
     second, head, send = call(
         second_body,
         "second",
         [wide_shape, head_shape, send_shape],
-        "vvvvvvhv",
+        "vvvvhvv",
         "hvv",
-        scratch=[far_scratch, pltpu.VMEM((CP, HALF), BF16), plane, sems, sems],
+        scratch=[far_scratch, w_scratch, plane, sem, sems],
         limit=50,
-    )(recv, place, asked, next_head, w, low, high, rinv)
+    )(recv, place, asked, next_head, w, base, rinv)
     recv = exchanged(send)
     next_head = passed_back(head)
-    low, high = call(
+    (base,) = call(
         near_second_body,
         "near_second",
-        [((CP, HALF), F32), ((BASE_DEEP, CP, PAIR), F32)],
+        [scores_shape],
         "shhvh",
-        "vh",
-        scratch=[plane, plane, near_w_scratch, pltpu.VMEM((CP, HALF), F32), sems, sems, sem, sems],
+        scratch=[plane, plane, near_w_scratch, sems, sems, sem],
         flops=2 * 10**9,
     )(named, second, seeds, rinv, near_w)
     (out,) = call(
         last_body,
         "last",
         [((C, ROWS), BF16)],
-        "vvvvvhv",
+        "vvvhvv",
         "h",
-        scratch=[
-            far_scratch, pltpu.VMEM((CP, HALF), F32), pltpu.VMEM((C, ROWS), BF16), sems, sems
-        ],
-    )(recv, place, next_head, w, low, high, rinv)
+        scratch=[far_scratch, w_scratch, pltpu.VMEM((C, ROWS), BF16), sem, sems],
+    )(recv, place, next_head, w, base, rinv)
     return jnp.transpose(out)
 
 

time: 91 us -> 89.2 us (0.980)
  starting transfers between devices: 40.5 us -> 39.3 us
  Pallas kernels: 31.1 us -> 30 us
    all_to_all x4, starting transfers between devices: 23.4 us -> 22.2 us  [exchanged(): lax.all_to_all(block, 'group', split_axis=0, concat_axis=0, tiled=True)]
    pallas_call x7 -> x6, Pallas kernels: 24.5 us -> 23.6 us  [the longest x1 6.42 us: local(): call(near_second_body, 'near_second', [scores_shape], 'shhvh', scratch=[p...]
    unnamed x17 -> x9, local copies, waits for them, and re-layouts: 3.4 us -> 3.38 us
  transfers between devices with their start and end apart: 7 -> 7, of which waited for: 5 -> 4; matrix products, arithmetic and copies ran while one was open for 1% -> 1% of each run, Pallas kernels for 21% -> 21%
where the time goes in v5:
time: 89.2 us; the launch traced here: 88.4 us
  starting transfers between devices  39.3 us (44%)
  Pallas kernels  30 us (34%)
  waiting for transfers between devices  15.4 us (17%)
  local copies, waits for them, and re-layouts  3.38 us (4%)
    all_to_all x4, starting transfers between devices, exchanged(): lax.all_to_all(block, 'group', split_axis=0, concat_axis=0, tiled=True)  22.2 us
    ppermute x3, starting transfers between devices, passed_back(): return lax.ppermute(block, 'node', [(i, i - 1) for i in range(1, size)])  17.1 us
    all_to_all x4, waiting for transfers between devices, exchanged(): lax.all_to_all(block, 'group', split_axis=0, concat_axis=0, tiled=True)  12.1 us
    pallas_call x1, Pallas kernels, local(): call(near_second_body, 'near_second', [scores_shape], 'shhvh', scratch=[p...  6.42 us
    pallas_call x1, Pallas kernels, local(): call(near_first_body, 'near_first', [scores_shape], 'shvh', scratch=[plan...  4.37 us
    pallas_call x1, Pallas kernels, local(): call(second_body, 'second', [wide_shape, head_shape, send_shape], 'vvvvhv...  3.94 us
    unnamed x9, local copies, waits for them, and re-layouts  3.38 us
    ppermute x3, waiting for transfers between devices, passed_back(): return lax.ppermute(block, 'node', [(i, i - 1) for i in range(1, size)])  3.34 us
  transfers between devices with their start and end apart: 7, of which 4 were waited for; matrix products, arithmetic and copies ran while one was open for 1% of the time, Pallas kernels for 21%

profile of v5, /device:TPU:7, one launch (start us, length us, event | category | flops | bytes accessed | tf_op | source)
XLA Modules:
  0.0 88.4 jit_solution(8580356118130882027)
XLA Ops:
  0.0 1.6 %index.1 = (s32[16,1,128]{2,1,0:T(1,128)}, s32[8,128]{1,0:T(8,128)}) custom-call(s32[1,128]{1,0:T(1,128)} %bitcast.7, s32[1,128]{1,0:T(1,128)} %bitcast.8), custom_call_target="tpu_custom_call" | custom-call | flops 1000000000 | bytes 1000000 | tf_op jit(solution)/shard_map/index/pallas_call | solution.py:400
  1.6 7.8 %all-to-all-start = ((s32[16,1,128]{2,1,0:T(1,128)}), s32[16,1,128]{2,1,0:T(1,128)S(1)}, u32[]{:S(2)}, u32[]{:S(2)}) async-start(s32[16,1,128]{2,1,0:T(1,128)} %get-tuple-element.22), calls=%async_computation | async-start | bytes 16384 | tf_op jit(solution)/shard_map/all_to_all | solution.py:388
  9.4 1.2 %copy-done.1 = bf16[1024,512]{1,0:T(8,128)(2,1)S(1)} copy-done((bf16[1024,512]{1,0:T(8,128)(2,1)S(1)}, bf16[1024,512]{1,0:T(8,128)(2,1)}, u32[]{:S(2)}) %copy-start.1) | copy-done | bytes 1048600
  10.6 0.7 copy-done.2
  11.4 1.1 %units.1 = (bf16[1024,512]{1,0:T(8,128)(2,1)S(1)}, bf16[128,512]{1,0:T(8,128)(2,1)S(1)}) custom-call(bf16[1024,512]{1,0:T(8,128)(2,1)S(1)} %copy-done.1, f32[4,1024]{1,0:T(4,128)S(1)} %copy-done.2), custom_call_target="tpu_custom_call" | custom-call | flops 1000000000 | bytes 4000000 | tf_op jit(solution)/shard_map/units/pallas_call | solution.py:409
  12.5 11.0 %collective-permute-start = (bf16[128,512]{1,0:T(8,128)(2,1)S(1)}, bf16[128,512]{1,0:T(8,128)(2,1)S(1)}, u32[]{:S(2)}, u32[]{:S(2)}) collective-permute-start(bf16[128,512]{1,0:T(8,128)(2,1)S(1)} %get-tuple-element.25), channel_id=1, source_target_pairs={{1,0},{2,1},{3,2},{4,3},{5,4},{6,5},{7,6},{8,7},{9,8},{10,9},{11,1... | collective-permute-start | bytes 393224 | tf_op jit(solution)/shard_map/ppermute | solution.py:384
  23.4 0.8 copy.8
  24.2 1.2 %gather_units.1 = bf16[16,48,128]{2,1,0:T(8,128)(2,1)} custom-call(s32[16,1,128]{2,1,0:T(1,128)S(1)} %all-to-all-done.asked_ref, bf16[1024,512]{1,0:T(8,128)(2,1)S(1)} %get-tuple-element.23.unit_ref), custom_call_target="tpu_custom_call" | custom-call | flops 1000000000 | bytes 1000000 | tf_op jit(solution)/shard_map/gather_units/pallas_call | solution.py:417
  25.4 7.5 %all-to-all-start.1 = ((bf16[16,48,128]{2,1,0:T(8,128)(2,1)}), bf16[16,48,128]{2,1,0:T(8,128)(2,1)S(1)}, u32[]{:S(2)}, u32[]{:S(2)}) async-start(bf16[16,48,128]{2,1,0:T(8,128)(2,1)} %gather_units.1), calls=%async_computation.1 | async-start | bytes 393216 | tf_op jit(solution)/shard_map/all_to_all | solution.py:388
  33.6 3.1 %seeds.1 = (bf16[16,96,128]{2,1,0:T(8,128)(2,1)S(1)}, bf16[1024,128]{1,0:T(8,128)(2,1)S(1)}, bf16[24,1024,256]{2,1,0:T(8,128)(2,1)}) custom-call(s32[16,1,128]{2,1,0:T(1,128)S(1)} %all-to-all-done.asked_ref, s32[1,1024]{1,0:T(1,128)S(1)} %bitcast.5, bf16[1000,1024]{1,0:T(8,128)(2,1)} %bitcast.6), custom_call_target="tpu_custom_call" | custom-call | flops 2000000000 | bytes 1000000 | tf_op jit(solution)/shard_map/seeds/pallas_call | solution.py:429
  36.7 2.5 %near.1 = (bf16[128,384,128]{2,1,0:T(8,128)(2,1)}, bf16[128,1024]{1,0:T(8,128)(2,1)S(1)}, f32[8,128]{1,0:T(8,128)S(1)}) custom-call(s32[8,2]{1,0:T(8,128)S(1)} %broadcast_subtract_fusion.named_ref, bf16[1024,512]{1,0:T(8,128)(2,1)S(1)} %get-tuple-element.23.unit_ref, bf16[128,512]{1,0:T(8,128)(2,1)S(1)} %collective-permute-done.next_ref), custom_call_target="tpu_custom_call" | custom-call | flops 1000000000 | bytes 1000000 | tf_op jit(solution)/shard_map/near/pallas_call | solution.py:419
  39.2 4.0 %all-to-all-done.1.recv_ref = bf16[16,48,128]{2,1,0:T(8,128)(2,1)S(1)} async-done(((bf16[16,48,128]{2,1,0:T(8,128)(2,1)}), bf16[16,48,128]{2,1,0:T(8,128)(2,1)S(1)}, u32[]{:S(2)}, u32[]{:S(2)}) %all-to-all-start.1) | async-done | bytes 196640 | tf_op jit(solution)/shard_map/all_to_all | solution.py:388
  43.2 2.7 %degree.1 = (bf16[24,256,1024]{2,1,0:T(8,128)(2,1)}, f32[1,1024]{1,0:T(1,128)S(1)}, bf16[1024,128]{1,0:T(8,128)(2,1)S(1)}, bf16[16,96,128]{2,1,0:T(8,128)(2,1)}) custom-call(bf16[16,48,128]{2,1,0:T(8,128)(2,1)S(1)} %all-to-all-done.1.recv_ref, s32[8,128]{1,0:T(8,128)S(1)} %copy-done, s32[16,1,128]{2,1,0:T(1,128)S(1)} %all-to-all-done.asked_ref, ...), custom_call_target="tpu_custom_call" | custom-call | flops 1000000000 | bytes 1000000 | tf_op jit(solution)/shard_map/degree/pallas_call | solution.py:439
  45.9 3.5 %all-to-all-start.2 = ((bf16[16,96,128]{2,1,0:T(8,128)(2,1)}), bf16[16,96,128]{2,1,0:T(8,128)(2,1)S(1)}, u32[]{:S(2)}, u32[]{:S(2)}) async-start(bf16[16,96,128]{2,1,0:T(8,128)(2,1)} %get-tuple-element.30), calls=%async_computation.2 | async-start | bytes 786432 | tf_op jit(solution)/shard_map/all_to_all | solution.py:388
  49.3 2.2 %collective-permute-start.1 = (bf16[1024,128]{1,0:T(8,128)(2,1)S(1)}, bf16[1024,128]{1,0:T(8,128)(2,1)S(1)}, u32[]{:S(2)}, u32[]{:S(2)}) collective-permute-start(bf16[1024,128]{1,0:T(8,128)(2,1)S(1)} %get-tuple-element.31), channel_id=1, source_target_pairs={{1,0},{2,1},{3,2},{4,3},{5,4},{6,5},{7,6},{8,7},{9,8},{10,9},{11,1... | collective-permute-start | bytes 786440 | tf_op jit(solution)/shard_map/ppermute | solution.py:384
  51.5 4.4 %near_first.1.base_ref = bf16[1024,1024]{1,0:T(8,128)(2,1)S(1)} custom-call(s32[8,2]{1,0:T(8,128)S(1)} %broadcast_subtract_fusion.named_ref, bf16[24,1024,256]{2,1,0:T(8,128)(2,1)} %get-tuple-element.33.seed_any, f32[1,1024]{1,0:T(1,128)S(1)} %get-tuple-element.34.rinv_ref, bf16[128,384,128]{2,1,0:T(8,128)(2,1)} %get-tuple-element.35.w_any), custom_call_target="tpu_custom_call" | custom-call | flops 2000000000 | bytes 1000000 | tf_op jit(solution)/shard_map/near_first/pallas_call | solution.py:451
  55.9 3.3 %collective-permute-done.1.next_ref = bf16[1024,128]{1,0:T(8,128)(2,1)S(1)} collective-permute-done((bf16[1024,128]{1,0:T(8,128)(2,1)S(1)}, bf16[1024,128]{1,0:T(8,128)(2,1)S(1)}, u32[]{:S(2)}, u32[]{:S(2)}) %collective-permute-start.1) | collective-permute-done | bytes 262176 | tf_op jit(solution)/shard_map/ppermute | solution.py:384
  59.2 4.5 %all-to-all-done.2.recv_ref = bf16[16,96,128]{2,1,0:T(8,128)(2,1)S(1)} async-done(((bf16[16,96,128]{2,1,0:T(8,128)(2,1)}), bf16[16,96,128]{2,1,0:T(8,128)(2,1)S(1)}, u32[]{:S(2)}, u32[]{:S(2)}) %all-to-all-start.2) | async-done | bytes 393248 | tf_op jit(solution)/shard_map/all_to_all | solution.py:388
  63.7 3.9 %second.1 = (bf16[24,1024,256]{2,1,0:T(8,128)(2,1)}, bf16[1024,128]{1,0:T(8,128)(2,1)S(1)}, bf16[16,96,128]{2,1,0:T(8,128)(2,1)}) custom-call(bf16[16,96,128]{2,1,0:T(8,128)(2,1)S(1)} %all-to-all-done.2.recv_ref, s32[8,128]{1,0:T(8,128)S(1)} %copy-done, s32[16,1,128]{2,1,0:T(1,128)S(1)} %all-to-all-done.asked_ref, ...), custom_call_target="tpu_custom_call" | custom-call | flops 1000000000 | bytes 1000000 | tf_op jit(solution)/shard_map/second/pallas_call | solution.py:459
  67.7 3.5 %all-to-all-start.3 = ((bf16[16,96,128]{2,1,0:T(8,128)(2,1)}), bf16[16,96,128]{2,1,0:T(8,128)(2,1)S(1)}, u32[]{:S(2)}, u32[]{:S(2)}) async-start(bf16[16,96,128]{2,1,0:T(8,128)(2,1)} %get-tuple-element.36), calls=%async_computation.3 | async-start | bytes 786432 | tf_op jit(solution)/shard_map/all_to_all | solution.py:388
  71.2 3.9 %collective-permute-start.2 = (bf16[1024,128]{1,0:T(8,128)(2,1)S(1)}, bf16[1024,128]{1,0:T(8,128)(2,1)S(1)}, u32[]{:S(2)}, u32[]{:S(2)}) collective-permute-start(bf16[1024,128]{1,0:T(8,128)(2,1)S(1)} %get-tuple-element.37), channel_id=1, source_target_pairs={{1,0},{2,1},{3,2},{4,3},{5,4},{6,5},{7,6},{8,7},{9,8},{10,9},{11,1... | collective-permute-start | bytes 786440 | tf_op jit(solution)/shard_map/ppermute | solution.py:384
  75.1 6.4 %near_second.1.base_ref = bf16[1024,1024]{1,0:T(8,128)(2,1)S(1)} custom-call(s32[8,2]{1,0:T(8,128)S(1)} %broadcast_subtract_fusion.named_ref, bf16[24,1024,256]{2,1,0:T(8,128)(2,1)} %get-tuple-element.38.second_any, bf16[24,1024,256]{2,1,0:T(8,128)(2,1)} %get-tuple-element.33.seed_any, f32[1,1024]{1,0:T(1,128)S(1)} %get-tuple-element.34.rinv_ref, ...), custom_call_target="tpu_custom_call" | custom-call | flops 2000000000 | bytes 1000000 | tf_op jit(solution)/shard_map/near_second/pallas_call | solution.py:470
  81.5 3.6 %all-to-all-done.3.recv_ref = bf16[16,96,128]{2,1,0:T(8,128)(2,1)S(1)} async-done(((bf16[16,96,128]{2,1,0:T(8,128)(2,1)}), bf16[16,96,128]{2,1,0:T(8,128)(2,1)S(1)}, u32[]{:S(2)}, u32[]{:S(2)}) %all-to-all-start.3) | async-done | bytes 393248 | tf_op jit(solution)/shard_map/all_to_all | solution.py:388
  85.2 3.0 %last.1 = bf16[1000,1024]{1,0:T(8,128)(2,1)} custom-call(bf16[16,96,128]{2,1,0:T(8,128)(2,1)S(1)} %all-to-all-done.3.recv_ref, s32[8,128]{1,0:T(8,128)S(1)} %copy-done, bf16[1024,128]{1,0:T(8,128)(2,1)S(1)} %collective-permute-done.2.next_ref, bf16[24,256,1024]{2,1,0:T(8,128)(2,1)} %get-tuple-element.32.w_any, bf16[1024,1024]{1,0:T(8,128)(2,1)S(1)} %near_second.1.base_ref, ...), custom_call_target="tpu_custom_call" | custom-call | flops 1000000000 | bytes 1000000 | tf_op jit(solution)/shard_map/last/pallas_call | solution.py:478
  (10 shorter events, 0.7 us)
Async XLA Ops:
  1.6 41.6 %copy-start = (s32[8,128]{1,0:T(8,128)S(1)}, s32[8,128]{1,0:T(8,128)}, u32[]{:S(2)}) copy-start(s32[8,128]{1,0:T(8,128)} %get-tuple-element.24.place_ref) | copy-start | bytes 12292
  1.6 22.6 %all-to-all-start = ((s32[16,1,128]{2,1,0:T(1,128)}), s32[16,1,128]{2,1,0:T(1,128)S(1)}, u32[]{:S(2)}, u32[]{:S(2)}) async-start(s32[16,1,128]{2,1,0:T(1,128)} %get-tuple-element.22), calls=%async_computation | async-start | bytes 16384 | tf_op jit(solution)/shard_map/all_to_all | solution.py:388
  9.4 1.2 %copy-start.1 = (bf16[1024,512]{1,0:T(8,128)(2,1)S(1)}, bf16[1024,512]{1,0:T(8,128)(2,1)}, u32[]{:S(2)}) copy-start(bf16[1024,512]{1,0:T(8,128)(2,1)} %desc_ref.1) | copy-start | bytes 3145732
  10.6 0.7 copy-start.2
  12.5 24.2 %collective-permute-start = (bf16[128,512]{1,0:T(8,128)(2,1)S(1)}, bf16[128,512]{1,0:T(8,128)(2,1)S(1)}, u32[]{:S(2)}, u32[]{:S(2)}) collective-permute-start(bf16[128,512]{1,0:T(8,128)(2,1)S(1)} %get-tuple-element.25), channel_id=1, source_target_pairs={{1,0},{2,1},{3,2},{4,3},{5,4},{6,5},{7,6},{8,7},{9,8},{10,9},{11,1... | collective-permute-start | bytes 393224 | tf_op jit(solution)/shard_map/ppermute | solution.py:384
  25.4 17.8 %all-to-all-start.1 = ((bf16[16,48,128]{2,1,0:T(8,128)(2,1)}), bf16[16,48,128]{2,1,0:T(8,128)(2,1)S(1)}, u32[]{:S(2)}, u32[]{:S(2)}) async-start(bf16[16,48,128]{2,1,0:T(8,128)(2,1)} %gather_units.1), calls=%async_computation.1 | async-start | bytes 393216 | tf_op jit(solution)/shard_map/all_to_all | solution.py:388
  32.9 0.7 copy-start.3
  45.9 17.9 %all-to-all-start.2 = ((bf16[16,96,128]{2,1,0:T(8,128)(2,1)}), bf16[16,96,128]{2,1,0:T(8,128)(2,1)S(1)}, u32[]{:S(2)}, u32[]{:S(2)}) async-start(bf16[16,96,128]{2,1,0:T(8,128)(2,1)} %get-tuple-element.30), calls=%async_computation.2 | async-start | bytes 786432 | tf_op jit(solution)/shard_map/all_to_all | solution.py:388
  49.3 9.9 %collective-permute-start.1 = (bf16[1024,128]{1,0:T(8,128)(2,1)S(1)}, bf16[1024,128]{1,0:T(8,128)(2,1)S(1)}, u32[]{:S(2)}, u32[]{:S(2)}) collective-permute-start(bf16[1024,128]{1,0:T(8,128)(2,1)S(1)} %get-tuple-element.31), channel_id=1, source_target_pairs={{1,0},{2,1},{3,2},{4,3},{5,4},{6,5},{7,6},{8,7},{9,8},{10,9},{11,1... | collective-permute-start | bytes 786440 | tf_op jit(solution)/shard_map/ppermute | solution.py:384
  67.7 17.5 %all-to-all-start.3 = ((bf16[16,96,128]{2,1,0:T(8,128)(2,1)}), bf16[16,96,128]{2,1,0:T(8,128)(2,1)S(1)}, u32[]{:S(2)}, u32[]{:S(2)}) async-start(bf16[16,96,128]{2,1,0:T(8,128)(2,1)} %get-tuple-element.36), calls=%async_computation.3 | async-start | bytes 786432 | tf_op jit(solution)/shard_map/all_to_all | solution.py:388
  71.2 10.4 %collective-permute-start.2 = (bf16[1024,128]{1,0:T(8,128)(2,1)S(1)}, bf16[1024,128]{1,0:T(8,128)(2,1)S(1)}, u32[]{:S(2)}, u32[]{:S(2)}) collective-permute-start(bf16[1024,128]{1,0:T(8,128)(2,1)S(1)} %get-tuple-element.37), channel_id=1, source_target_pairs={{1,0},{2,1},{3,2},{4,3},{5,4},{6,5},{7,6},{8,7},{9,8},{10,9},{11,1... | collective-permute-start | bytes 786440 | tf_op jit(solution)/shard_map/ppermute | solution.py:384

commit v6 on v5

--- a/solution.py
+++ b/solution.py
@@ -16,6 +16,7 @@
 PAIR = 2 * BLK
 PAIRS = ROWS // PAIR
 SCORE_DEEP = 24
+LOW = ROWS - PAIR
 WEIGHT_DEEP = 16 * TILES
 
 alpha_mix = 0.8
@@ -106,7 +107,7 @@
     place_ref[1:2, :] = slot
 
 
-def unit_body(desc_ref, scales_ref, unit_ref, head_ref):
+def unit_body(desc_ref, scales_ref, unit_ref):
     columns = jnp.transpose(jnp.concatenate([scales_ref[...], scales_ref[...]], axis=0))
     parts = []
     total = None
@@ -117,9 +118,7 @@
         total = square if total is None else total + square
     inv = lax.rsqrt(jnp.sum(total, axis=1, keepdims=True) + eps_norm)
     for k in range(D // BLK):
-        out = (parts[k] * inv).astype(BF16)
-        unit_ref[:, k * BLK : (k + 1) * BLK] = out
-        head_ref[:, k * BLK : (k + 1) * BLK] = out[:BLK]
+        unit_ref[:, k * BLK : (k + 1) * BLK] = (parts[k] * inv).astype(BF16)
 
 
 def asked_columns(asked_ref, rows):
@@ -176,7 +175,8 @@
     return recv_ref[:, at : at + 16, :].reshape(2 * BLK, BLK)
 
 
-def gather_units_body(asked_ref, unit_ref, send_ref):
+def gather_units_body(asked_ref, unit_ref, send_ref, head_ref):
+    head_ref[...] = unit_ref[:BLK, :]
     pack_rows(dot(request_rows(asked_ref), unit_ref[...]), D // BLK, send_ref)
 
 
@@ -239,7 +239,7 @@
 
 def degree_body(
     recv_ref, place_ref, asked_ref, unit_ref, near_ref, after_ref, asked_seed_ref, seed_ref,
-    w_any, rinv_ref, head_ref, send_ref, far_ref, w_ref, w_sem,
+    w_ref, rinv_ref, head_ref, send_ref, far_ref,
 ):
     w_ref[BLK:, :] = after_ref[...]
     low, high = placers(place_ref)
@@ -267,13 +267,10 @@
         spread = jnp.broadcast_to(rinv.reshape(1, 1, BLK), (GROUPS, 16, BLK))
         for k, column in enumerate(columns):
             found[k] = jnp.where(node + float(r * BLK) == column, spread, found[k])
-    w_copy = pltpu.make_async_copy(w_ref, w_any.at[0], w_sem)
-    w_copy.start()
     weights = [jnp.sum(values, axis=2, keepdims=True) for values in found]
     for k in range(6):
         part = asked_seed_ref[:, 16 * k : 16 * (k + 1), :].astype(F32)
         send_ref[:, 16 * k : 16 * (k + 1), :] = (weights[k // 4] * part).astype(BF16)
-    w_copy.wait()
 
 
 def spread_near(named_ref, source_ref, w_ref, r):
@@ -288,7 +285,17 @@
     return (alpha_mix * weight) * total + (1.0 - alpha_mix) * seed.astype(F32)
 
 
-def near_first_body(named_ref, seed_any, rinv_ref, w_any, base_ref, seed_ref, first_ref, w_ref, sems, w_sem):
+def put_base(total, r, low_ref, high_ref):
+    if r * BLK < LOW:
+        low_ref[:, r * BLK : (r + 1) * BLK] = total.astype(BF16)
+    else:
+        high_ref[:, r * BLK - LOW : (r + 1) * BLK - LOW] = total.astype(BF16)
+
+
+def near_first_body(
+    named_ref, seed_any, rinv_ref, w_any, low_ref, high_any,
+    seed_ref, first_ref, w_ref, high_ref, sems, w_sem, high_sem,
+):
     w_copy = pltpu.make_async_copy(w_any.at[pl.ds(0, TILES)], w_ref, w_sem)
     w_copy.start()
     arriving = arriving_pairs(seed_any, seed_ref, sems)
@@ -301,12 +308,15 @@
         cols = slice(r * BLK, (r + 1) * BLK)
         weight = rinv_ref[0:1, cols]
         total = spread_near(named_ref, first_ref, w_ref, r)
-        base_ref[:, cols] = (weight * mixed_near(total, weight, seed_ref[:, cols])).astype(BF16)
+        put_base(weight * mixed_near(total, weight, seed_ref[:, cols]), r, low_ref, high_ref)
+    copy = pltpu.make_async_copy(high_ref, high_any.at[0], high_sem)
+    copy.start()
+    copy.wait()
 
 
 def near_second_body(
-    named_ref, second_any, seed_any, rinv_ref, w_any, base_ref,
-    second_ref, seed_ref, w_ref, sems, seed_sems, w_sem,
+    named_ref, second_any, seed_any, rinv_ref, w_any, low_ref, high_any,
+    second_ref, seed_ref, w_ref, high_ref, sems, seed_sems, w_sem, high_sem,
 ):
     arriving = arriving_pairs(second_any, second_ref, sems)
     arriving += started([pltpu.make_async_copy(w_any.at[pl.ds(0, TILES)], w_ref, w_sem)])
@@ -318,7 +328,10 @@
         total = spread_near(named_ref, second_ref, w_ref, r)
         if r % 2 == 0:
             seeds[r // 2].wait()
-        base_ref[:, cols] = mixed_near(total, rinv_ref[0:1, cols], seed_ref[:, cols]).astype(BF16)
+        put_base(mixed_near(total, rinv_ref[0:1, cols], seed_ref[:, cols]), r, low_ref, high_ref)
+    copy = pltpu.make_async_copy(high_ref, high_any.at[0], high_sem)
+    copy.start()
+    copy.wait()
 
 
 def far_scores(recv_ref, place_ref, next_ref, far_ref):
@@ -336,19 +349,21 @@
 
 
 def second_body(
-    recv_ref, place_ref, asked_ref, next_ref, w_any, base_ref, rinv_ref,
-    second_any, head_ref, send_ref, far_ref, w_ref, second_ref, w_sem, sems,
+    recv_ref, place_ref, asked_ref, next_ref, w_ref, low_ref, high_any, rinv_ref,
+    second_any, head_ref, send_ref, far_ref, high_ref, second_ref, high_sem, sems,
 ):
-    w_copy = pltpu.make_async_copy(w_any.at[0], w_ref, w_sem)
-    w_copy.start()
+    arriving = pltpu.make_async_copy(high_any.at[0], high_ref, high_sem)
+    arriving.start()
     far_scores(recv_ref, place_ref, next_ref, far_ref)
-    w_copy.wait()
     leaving = []
     for r in range(PAIRS):
         cols = slice(r * PAIR, (r + 1) * PAIR)
         total = dot(far_ref[...], w_ref[:, cols])
         weight = rinv_ref[0:1, cols]
-        total = base_ref[:, cols].astype(F32) + (alpha_mix * weight * weight) * total
+        if r == PAIRS - 1:
+            arriving.wait()
+        base = low_ref[:, cols] if r < PAIRS - 1 else high_ref[...]
+        total = base.astype(F32) + (alpha_mix * weight * weight) * total
         second_ref[:, cols] = total.astype(BF16)
         leaving += leaving_pair(second_ref, second_any, sems, r)
     head_ref[...] = second_ref[:, :BLK]
@@ -358,18 +373,20 @@
 
 
 def last_body(
-    recv_ref, place_ref, next_ref, w_any, base_ref, rinv_ref,
-    out_any, far_ref, w_ref, out_ref, w_sem, sems,
+    recv_ref, place_ref, next_ref, w_ref, low_ref, high_any, rinv_ref,
+    out_any, far_ref, high_ref, out_ref, high_sem, sems,
 ):
-    w_copy = pltpu.make_async_copy(w_any.at[0], w_ref, w_sem)
-    w_copy.start()
+    arriving = pltpu.make_async_copy(high_any.at[0], high_ref, high_sem)
+    arriving.start()
     far_scores(recv_ref, place_ref, next_ref, far_ref)
-    w_copy.wait()
     leaving = []
     for r in range(PAIRS):
         cols = slice(r * PAIR, (r + 1) * PAIR)
         total = dot(far_ref[:C, :], w_ref[:, cols])
-        total = base_ref[:C, cols].astype(F32) + (alpha_mix * rinv_ref[0:1, cols]) * total
+        if r == PAIRS - 1:
+            arriving.wait()
+        base = low_ref[:C, cols] if r < PAIRS - 1 else high_ref[:C, :]
+        total = base.astype(F32) + (alpha_mix * rinv_ref[0:1, cols]) * total
         out_ref[:, cols] = total.astype(BF16)
         at = pl.ds(r * PAIR, PAIR)
         leaving += started(
@@ -395,7 +412,8 @@
     row_vector = pltpu.VMEM((1, BLK), jnp.int32)
     plane = pltpu.VMEM((CP, ROWS), BF16)
     far_scratch = pltpu.VMEM((CP, 2 * BLK), BF16)
-    w_scratch = pltpu.VMEM((2 * BLK, ROWS), BF16)
+    last_pair = pltpu.VMEM((CP, PAIR), BF16)
+    base_shapes = [((CP, LOW), BF16), ((SCORE_DEEP, CP, PAIR), BF16)]
     near_w_scratch = pltpu.VMEM((TILES, 3 * BLK, BLK), BF16)
     wanted, place = call(
         index_body,
@@ -406,16 +424,15 @@
         limit=60,
     )(cross_group.reshape(1, BLK), cross_row.reshape(1, BLK))
     asked = exchanged(wanted)
-    units, head = call(
-        unit_body,
-        "units",
-        [((ROWS, D), BF16), ((BLK, D), BF16)],
+    (units,) = call(unit_body, "units", [((ROWS, D), BF16)], "vv", nbytes=4 * 10**6)(desc, scales)
+    send, head = call(
+        gather_units_body,
+        "gather_units",
+        [((GROUPS, 48, BLK), BF16), ((BLK, D), BF16)],
         "vv",
-        nbytes=4 * 10**6,
-    )(desc, scales)
+    )(asked, units)
+    far_units = exchanged(send)
     next_units = passed_back(head)
-    (send,) = call(gather_units_body, "gather_units", [((GROUPS, 48, BLK), BF16)], "vv")(asked, units)
-    far_units = exchanged(send)
     near_w, after_w, near_degree = call(
         near_body,
         "near",
@@ -439,50 +456,50 @@
     w, rinv, head, send = call(
         degree_body,
         "degree",
-        [((SCORE_DEEP, 2 * BLK, ROWS), BF16), ((1, ROWS), F32), head_shape, send_shape],
+        [((2 * BLK, ROWS), BF16), ((1, ROWS), F32), head_shape, send_shape],
         "vvvvvvvv",
-        "hvvv",
-        scratch=[pltpu.VMEM((BLK, D), BF16), w_scratch, sem],
+        scratch=[pltpu.VMEM((BLK, D), BF16)],
         limit=50,
     )(far_units, place, asked, units, near_degree, after_w, asked_seeds, seed_head)
     recv = exchanged(send)
     next_head = passed_back(head)
-    scores_shape = ((CP, ROWS), BF16)
-    (base,) = call(
+    low, high = call(
         near_first_body,
         "near_first",
-        [scores_shape],
+        base_shapes,
         "shvh",
-        scratch=[plane, plane, near_w_scratch, sems, sem],
+        "vh",
+        scratch=[plane, plane, near_w_scratch, last_pair, sems, sem, sem],
         flops=2 * 10**9,
     )(named, seeds, rinv, near_w)
     second, head, send = call(
         second_body,
         "second",
         [wide_shape, head_shape, send_shape],
-        "vvvvhvv",
+        "vvvvvvhv",
         "hvv",
-        scratch=[far_scratch, w_scratch, plane, sem, sems],
+        scratch=[far_scratch, last_pair, plane, sem, sems],
         limit=50,
-    )(recv, place, asked, next_head, w, base, rinv)
+    )(recv, place, asked, next_head, w, low, high, rinv)
     recv = exchanged(send)
     next_head = passed_back(head)
-    (base,) = call(
+    low, high = call(
         near_second_body,
         "near_second",
-        [scores_shape],
+        base_shapes,
         "shhvh",
-        scratch=[plane, plane, near_w_scratch, sems, sems, sem],
+        "vh",
+        scratch=[plane, plane, near_w_scratch, last_pair, sems, sems, sem, sem],
         flops=2 * 10**9,
     )(named, second, seeds, rinv, near_w)
     (out,) = call(
         last_body,
         "last",
         [((C, ROWS), BF16)],
-        "vvvhvv",
+        "vvvvvhv",
         "h",
-        scratch=[far_scratch, w_scratch, pltpu.VMEM((C, ROWS), BF16), sem, sems],
-    )(recv, place, next_head, w, base, rinv)
+        scratch=[far_scratch, last_pair, pltpu.VMEM((C, ROWS), BF16), sem, sems],
+    )(recv, place, next_head, w, low, high, rinv)
     return jnp.transpose(out)
 
 

time: 89.2 us -> 88.6 us (level)
  waiting for transfers between devices: 15.4 us -> 8.03 us
  starting transfers between devices: 39.3 us -> 46.5 us
    ppermute x3, starting transfers between devices: 17.1 us -> 22.8 us  [passed_back(): return lax.ppermute(block, 'node', [(i, i - 1) for i in range(1, size)])]
    all_to_all x4, waiting for transfers between devices: 12.1 us -> 7.6 us  [exchanged(): lax.all_to_all(block, 'group', split_axis=0, concat_axis=0, tiled=True)]
    ppermute x3, waiting for transfers between devices: 3.34 us -> 0.43 us  [passed_back(): return lax.ppermute(block, 'node', [(i, i - 1) for i in range(1, size)])]
    all_to_all x4, starting transfers between devices: 22.2 us -> 23.6 us  [exchanged(): lax.all_to_all(block, 'group', split_axis=0, concat_axis=0, tiled=True)]
  transfers between devices with their start and end apart: 7 -> 7, of which waited for: 4 -> 4; matrix products, arithmetic and copies ran while one was open for 1% -> 1% of each run, Pallas kernels for 21% -> 22%
where the time goes in v6:
time: 88.6 us; the launch traced here: 87.8 us
  starting transfers between devices  46.5 us (52%)
  Pallas kernels  29.6 us (33%)
  waiting for transfers between devices  8.03 us (9%)
  local copies, waits for them, and re-layouts  3.38 us (4%)
    all_to_all x4, starting transfers between devices, exchanged(): lax.all_to_all(block, 'group', split_axis=0, concat_axis=0, tiled=True)  23.6 us
    ppermute x3, starting transfers between devices, passed_back(): return lax.ppermute(block, 'node', [(i, i - 1) for i in range(1, size)])  22.8 us
    all_to_all x4, waiting for transfers between devices, exchanged(): lax.all_to_all(block, 'group', split_axis=0, concat_axis=0, tiled=True)  7.6 us
    pallas_call x1, Pallas kernels, local(): call(near_second_body, 'near_second', base_shapes, 'shhvh', 'vh', scratch...  7.09 us
    pallas_call x1, Pallas kernels, local(): call(near_first_body, 'near_first', base_shapes, 'shvh', 'vh', scratch=[p...  5.19 us
    pallas_call x1, Pallas kernels, local(): call(second_body, 'second', [wide_shape, head_shape, send_shape], 'vvvvvv...  3.47 us
    unnamed x9, local copies, waits for them, and re-layouts  3.38 us
    pallas_call x1, Pallas kernels, local(): call(seed_body, 'seeds', [send_shape, head_shape, wide_shape], 'vvh', 'vv...  3.13 us
  transfers between devices with their start and end apart: 7, of which 4 were waited for; matrix products, arithmetic and copies ran while one was open for 1% of the time, Pallas kernels for 22%

profile of v6, /device:TPU:7, one launch (start us, length us, event | category | flops | bytes accessed | tf_op | source)
XLA Modules:
  0.0 87.8 jit_solution(5571169817866742885)
XLA Ops:
  0.0 1.6 %index.1 = (s32[16,1,128]{2,1,0:T(1,128)}, s32[8,128]{1,0:T(8,128)}) custom-call(s32[1,128]{1,0:T(1,128)} %bitcast.7, s32[1,128]{1,0:T(1,128)} %bitcast.8), custom_call_target="tpu_custom_call" | custom-call | flops 1000000000 | bytes 1000000 | tf_op jit(solution)/shard_map/index/pallas_call | solution.py:418
  1.6 7.8 %all-to-all-start = ((s32[16,1,128]{2,1,0:T(1,128)}), s32[16,1,128]{2,1,0:T(1,128)S(1)}, u32[]{:S(2)}, u32[]{:S(2)}) async-start(s32[16,1,128]{2,1,0:T(1,128)} %get-tuple-element.26), calls=%async_computation | async-start | bytes 16384 | tf_op jit(solution)/shard_map/all_to_all | solution.py:405
  9.4 1.2 %copy-done.1 = bf16[1024,512]{1,0:T(8,128)(2,1)S(1)} copy-done((bf16[1024,512]{1,0:T(8,128)(2,1)S(1)}, bf16[1024,512]{1,0:T(8,128)(2,1)}, u32[]{:S(2)}) %copy-start.1) | copy-done | bytes 1048600
  10.6 0.7 copy-done.2
  11.4 1.1 %units.1.unit_ref = bf16[1024,512]{1,0:T(8,128)(2,1)S(1)} custom-call(bf16[1024,512]{1,0:T(8,128)(2,1)S(1)} %copy-done.1, f32[4,1024]{1,0:T(4,128)S(1)} %copy-done.2), custom_call_target="tpu_custom_call" | custom-call | flops 1000000000 | bytes 4000000 | tf_op jit(solution)/shard_map/units/pallas_call | solution.py:427
  12.5 0.8 copy.8
  13.2 3.1 %all-to-all-done.asked_ref = s32[16,1,128]{2,1,0:T(1,128)S(1)} async-done(((s32[16,1,128]{2,1,0:T(1,128)}), s32[16,1,128]{2,1,0:T(1,128)S(1)}, u32[]{:S(2)}, u32[]{:S(2)}) %all-to-all-start) | async-done | bytes 8224 | tf_op jit(solution)/shard_map/all_to_all | solution.py:405
  16.4 1.2 %gather_units.1 = (bf16[16,48,128]{2,1,0:T(8,128)(2,1)}, bf16[128,512]{1,0:T(8,128)(2,1)S(1)}) custom-call(s32[16,1,128]{2,1,0:T(1,128)S(1)} %all-to-all-done.asked_ref, bf16[1024,512]{1,0:T(8,128)(2,1)S(1)} %units.1.unit_ref), custom_call_target="tpu_custom_call" | custom-call | flops 1000000000 | bytes 1000000 | tf_op jit(solution)/shard_map/gather_units/pallas_call | solution.py:428
  17.5 4.1 %all-to-all-start.1 = ((bf16[16,48,128]{2,1,0:T(8,128)(2,1)}), bf16[16,48,128]{2,1,0:T(8,128)(2,1)S(1)}, u32[]{:S(2)}, u32[]{:S(2)}) async-start(bf16[16,48,128]{2,1,0:T(8,128)(2,1)} %get-tuple-element.27), calls=%async_computation.1 | async-start | bytes 393216 | tf_op jit(solution)/shard_map/all_to_all | solution.py:405
  21.6 11.0 %collective-permute-start = (bf16[128,512]{1,0:T(8,128)(2,1)S(1)}, bf16[128,512]{1,0:T(8,128)(2,1)S(1)}, u32[]{:S(2)}, u32[]{:S(2)}) collective-permute-start(bf16[128,512]{1,0:T(8,128)(2,1)S(1)} %get-tuple-element.29), channel_id=1, source_target_pairs={{1,0},{2,1},{3,2},{4,3},{5,4},{6,5},{7,6},{8,7},{9,8},{10,9},{11,1... | collective-permute-start | bytes 393224 | tf_op jit(solution)/shard_map/ppermute | solution.py:401
  32.6 0.7 copy-done.3
  33.3 3.1 %seeds.1 = (bf16[16,96,128]{2,1,0:T(8,128)(2,1)S(1)}, bf16[1024,128]{1,0:T(8,128)(2,1)S(1)}, bf16[24,1024,256]{2,1,0:T(8,128)(2,1)}) custom-call(s32[16,1,128]{2,1,0:T(1,128)S(1)} %all-to-all-done.asked_ref, s32[1,1024]{1,0:T(1,128)S(1)} %bitcast.5, bf16[1000,1024]{1,0:T(8,128)(2,1)} %bitcast.6), custom_call_target="tpu_custom_call" | custom-call | flops 2000000000 | bytes 1000000 | tf_op jit(solution)/shard_map/seeds/pallas_call | solution.py:446
  36.5 2.5 %near.1 = (bf16[128,384,128]{2,1,0:T(8,128)(2,1)}, bf16[128,1024]{1,0:T(8,128)(2,1)S(1)}, f32[8,128]{1,0:T(8,128)S(1)}) custom-call(s32[8,2]{1,0:T(8,128)S(1)} %broadcast_subtract_fusion.named_ref, bf16[1024,512]{1,0:T(8,128)(2,1)S(1)} %units.1.unit_ref, bf16[128,512]{1,0:T(8,128)(2,1)S(1)} %collective-permute-done.next_ref), custom_call_target="tpu_custom_call" | custom-call | flops 1000000000 | bytes 1000000 | tf_op jit(solution)/shard_map/near/pallas_call | solution.py:436
  39.0 1.9 %degree.1 = (bf16[256,1024]{1,0:T(8,128)(2,1)S(1)}, f32[1,1024]{1,0:T(1,128)S(1)}, bf16[1024,128]{1,0:T(8,128)(2,1)S(1)}, bf16[16,96,128]{2,1,0:T(8,128)(2,1)}) custom-call(bf16[16,48,128]{2,1,0:T(8,128)(2,1)S(1)} %all-to-all-done.1.recv_ref, s32[8,128]{1,0:T(8,128)S(1)} %copy-done, s32[16,1,128]{2,1,0:T(1,128)S(1)} %all-to-all-done.asked_ref, ...), custom_call_target="tpu_custom_call" | custom-call | flops 1000000000 | bytes 1000000 | tf_op jit(solution)/shard_map/degree/pallas_call | solution.py:456
  40.9 7.5 %all-to-all-start.2 = ((bf16[16,96,128]{2,1,0:T(8,128)(2,1)}), bf16[16,96,128]{2,1,0:T(8,128)(2,1)S(1)}, u32[]{:S(2)}, u32[]{:S(2)}) async-start(bf16[16,96,128]{2,1,0:T(8,128)(2,1)} %get-tuple-element.34), calls=%async_computation.2 | async-start | bytes 786432 | tf_op jit(solution)/shard_map/all_to_all | solution.py:405
  48.3 5.4 %collective-permute-start.1 = (bf16[1024,128]{1,0:T(8,128)(2,1)S(1)}, bf16[1024,128]{1,0:T(8,128)(2,1)S(1)}, u32[]{:S(2)}, u32[]{:S(2)}) collective-permute-start(bf16[1024,128]{1,0:T(8,128)(2,1)S(1)} %get-tuple-element.35), channel_id=1, source_target_pairs={{1,0},{2,1},{3,2},{4,3},{5,4},{6,5},{7,6},{8,7},{9,8},{10,9},{11,1... | collective-permute-start | bytes 786440 | tf_op jit(solution)/shard_map/ppermute | solution.py:401
  53.8 5.2 %near_first.1 = (bf16[1024,768]{1,0:T(8,128)(2,1)S(1)}, bf16[24,1024,256]{2,1,0:T(8,128)(2,1)}) custom-call(s32[8,2]{1,0:T(8,128)S(1)} %broadcast_subtract_fusion.named_ref, bf16[24,1024,256]{2,1,0:T(8,128)(2,1)} %get-tuple-element.37.seed_any, f32[1,1024]{1,0:T(1,128)S(1)} %get-tuple-element.38.rinv_ref, bf16[128,384,128]{2,1,0:T(8,128)(2,1)} %get-tuple-element.39.w_any), custom_call_target="tpu_custom_call" | custom-call | flops 2000000000 | bytes 1000000 | tf_op jit(solution)/shard_map/near_first/pallas_call | solution.py:466
  59.4 3.5 %all-to-all-done.2.recv_ref = bf16[16,96,128]{2,1,0:T(8,128)(2,1)S(1)} async-done(((bf16[16,96,128]{2,1,0:T(8,128)(2,1)}), bf16[16,96,128]{2,1,0:T(8,128)(2,1)S(1)}, u32[]{:S(2)}, u32[]{:S(2)}) %all-to-all-start.2) | async-done | bytes 393248 | tf_op jit(solution)/shard_map/all_to_all | solution.py:405
  62.9 3.5 %second.1 = (bf16[24,1024,256]{2,1,0:T(8,128)(2,1)}, bf16[1024,128]{1,0:T(8,128)(2,1)S(1)}, bf16[16,96,128]{2,1,0:T(8,128)(2,1)}) custom-call(bf16[16,96,128]{2,1,0:T(8,128)(2,1)S(1)} %all-to-all-done.2.recv_ref, s32[8,128]{1,0:T(8,128)S(1)} %copy-done, s32[16,1,128]{2,1,0:T(1,128)S(1)} %all-to-all-done.asked_ref, ...), custom_call_target="tpu_custom_call" | custom-call | flops 1000000000 | bytes 1000000 | tf_op jit(solution)/shard_map/second/pallas_call | solution.py:475
  66.4 4.2 %all-to-all-start.3 = ((bf16[16,96,128]{2,1,0:T(8,128)(2,1)}), bf16[16,96,128]{2,1,0:T(8,128)(2,1)S(1)}, u32[]{:S(2)}, u32[]{:S(2)}) async-start(bf16[16,96,128]{2,1,0:T(8,128)(2,1)} %get-tuple-element.42), calls=%async_computation.3 | async-start | bytes 786432 | tf_op jit(solution)/shard_map/all_to_all | solution.py:405
  70.6 6.4 %collective-permute-start.2 = (bf16[1024,128]{1,0:T(8,128)(2,1)S(1)}, bf16[1024,128]{1,0:T(8,128)(2,1)S(1)}, u32[]{:S(2)}, u32[]{:S(2)}) collective-permute-start(bf16[1024,128]{1,0:T(8,128)(2,1)S(1)} %get-tuple-element.43), channel_id=1, source_target_pairs={{1,0},{2,1},{3,2},{4,3},{5,4},{6,5},{7,6},{8,7},{9,8},{10,9},{11,1... | collective-permute-start | bytes 786440 | tf_op jit(solution)/shard_map/ppermute | solution.py:401
  77.1 7.1 %near_second.1 = (bf16[1024,768]{1,0:T(8,128)(2,1)S(1)}, bf16[24,1024,256]{2,1,0:T(8,128)(2,1)}) custom-call(s32[8,2]{1,0:T(8,128)S(1)} %broadcast_subtract_fusion.named_ref, bf16[24,1024,256]{2,1,0:T(8,128)(2,1)} %get-tuple-element.44.second_any, bf16[24,1024,256]{2,1,0:T(8,128)(2,1)} %get-tuple-element.37.seed_any, ...), custom_call_target="tpu_custom_call" | custom-call | flops 2000000000 | bytes 1000000 | tf_op jit(solution)/shard_map/near_second/pallas_call | solution.py:486
  84.2 1.0 %all-to-all-done.3.recv_ref = bf16[16,96,128]{2,1,0:T(8,128)(2,1)S(1)} async-done(((bf16[16,96,128]{2,1,0:T(8,128)(2,1)}), bf16[16,96,128]{2,1,0:T(8,128)(2,1)S(1)}, u32[]{:S(2)}, u32[]{:S(2)}) %all-to-all-start.3) | async-done | bytes 393248 | tf_op jit(solution)/shard_map/all_to_all | solution.py:405
  85.2 2.5 %last.1 = bf16[1000,1024]{1,0:T(8,128)(2,1)} custom-call(bf16[16,96,128]{2,1,0:T(8,128)(2,1)S(1)} %all-to-all-done.3.recv_ref, s32[8,128]{1,0:T(8,128)S(1)} %copy-done, bf16[1024,128]{1,0:T(8,128)(2,1)S(1)} %collective-permute-done.2.next_ref, bf16[256,1024]{1,0:T(8,128)(2,1)S(1)} %get-tuple-element.36.w_ref, ...), custom_call_target="tpu_custom_call" | custom-call | flops 1000000000 | bytes 1000000 | tf_op jit(solution)/shard_map/last/pallas_call | solution.py:495
  (10 shorter events, 0.5 us)
Async XLA Ops:
  1.6 37.4 %copy-start = (s32[8,128]{1,0:T(8,128)S(1)}, s32[8,128]{1,0:T(8,128)}, u32[]{:S(2)}) copy-start(s32[8,128]{1,0:T(8,128)} %get-tuple-element.28.place_ref) | copy-start | bytes 12292
  1.6 14.7 %all-to-all-start = ((s32[16,1,128]{2,1,0:T(1,128)}), s32[16,1,128]{2,1,0:T(1,128)S(1)}, u32[]{:S(2)}, u32[]{:S(2)}) async-start(s32[16,1,128]{2,1,0:T(1,128)} %get-tuple-element.26), calls=%async_computation | async-start | bytes 16384 | tf_op jit(solution)/shard_map/all_to_all | solution.py:405
  9.4 1.2 %copy-start.1 = (bf16[1024,512]{1,0:T(8,128)(2,1)S(1)}, bf16[1024,512]{1,0:T(8,128)(2,1)}, u32[]{:S(2)}) copy-start(bf16[1024,512]{1,0:T(8,128)(2,1)} %desc_ref.1) | copy-start | bytes 3145732
  10.6 0.7 copy-start.2
  17.5 21.5 %all-to-all-start.1 = ((bf16[16,48,128]{2,1,0:T(8,128)(2,1)}), bf16[16,48,128]{2,1,0:T(8,128)(2,1)S(1)}, u32[]{:S(2)}, u32[]{:S(2)}) async-start(bf16[16,48,128]{2,1,0:T(8,128)(2,1)} %get-tuple-element.27), calls=%async_computation.1 | async-start | bytes 393216 | tf_op jit(solution)/shard_map/all_to_all | solution.py:405
  21.6 14.8 %collective-permute-start = (bf16[128,512]{1,0:T(8,128)(2,1)S(1)}, bf16[128,512]{1,0:T(8,128)(2,1)S(1)}, u32[]{:S(2)}, u32[]{:S(2)}) collective-permute-start(bf16[128,512]{1,0:T(8,128)(2,1)S(1)} %get-tuple-element.29), channel_id=1, source_target_pairs={{1,0},{2,1},{3,2},{4,3},{5,4},{6,5},{7,6},{8,7},{9,8},{10,9},{11,1... | collective-permute-start | bytes 393224 | tf_op jit(solution)/shard_map/ppermute | solution.py:401
  32.6 0.7 copy-start.3
  40.9 22.0 %all-to-all-start.2 = ((bf16[16,96,128]{2,1,0:T(8,128)(2,1)}), bf16[16,96,128]{2,1,0:T(8,128)(2,1)S(1)}, u32[]{:S(2)}, u32[]{:S(2)}) async-start(bf16[16,96,128]{2,1,0:T(8,128)(2,1)} %get-tuple-element.34), calls=%async_computation.2 | async-start | bytes 786432 | tf_op jit(solution)/shard_map/all_to_all | solution.py:405
  48.3 11.1 %collective-permute-start.1 = (bf16[1024,128]{1,0:T(8,128)(2,1)S(1)}, bf16[1024,128]{1,0:T(8,128)(2,1)S(1)}, u32[]{:S(2)}, u32[]{:S(2)}) collective-permute-start(bf16[1024,128]{1,0:T(8,128)(2,1)S(1)} %get-tuple-element.35), channel_id=1, source_target_pairs={{1,0},{2,1},{3,2},{4,3},{5,4},{6,5},{7,6},{8,7},{9,8},{10,9},{11,1... | collective-permute-start | bytes 786440 | tf_op jit(solution)/shard_map/ppermute | solution.py:401
  66.4 18.8 %all-to-all-start.3 = ((bf16[16,96,128]{2,1,0:T(8,128)(2,1)}), bf16[16,96,128]{2,1,0:T(8,128)(2,1)S(1)}, u32[]{:S(2)}, u32[]{:S(2)}) async-start(bf16[16,96,128]{2,1,0:T(8,128)(2,1)} %get-tuple-element.42), calls=%async_computation.3 | async-start | bytes 786432 | tf_op jit(solution)/shard_map/all_to_all | solution.py:405
  70.6 13.5 %collective-permute-start.2 = (bf16[1024,128]{1,0:T(8,128)(2,1)S(1)}, bf16[1024,128]{1,0:T(8,128)(2,1)S(1)}, u32[]{:S(2)}, u32[]{:S(2)}) collective-permute-start(bf16[1024,128]{1,0:T(8,128)(2,1)S(1)} %get-tuple-element.43), channel_id=1, source_target_pairs={{1,0},{2,1},{3,2},{4,3},{5,4},{6,5},{7,6},{8,7},{9,8},{10,9},{11,1... | collective-permute-start | bytes 786440 | tf_op jit(solution)/shard_map/ppermute | solution.py:401

commit v7 on v6

--- a/solution.py
+++ b/solution.py
@@ -107,7 +107,7 @@
     place_ref[1:2, :] = slot
 
 
-def unit_body(desc_ref, scales_ref, unit_ref):
+def unit_body(desc_ref, scales_ref, unit_ref, head_ref):
     columns = jnp.transpose(jnp.concatenate([scales_ref[...], scales_ref[...]], axis=0))
     parts = []
     total = None
@@ -118,7 +118,9 @@
         total = square if total is None else total + square
     inv = lax.rsqrt(jnp.sum(total, axis=1, keepdims=True) + eps_norm)
     for k in range(D // BLK):
-        unit_ref[:, k * BLK : (k + 1) * BLK] = (parts[k] * inv).astype(BF16)
+        out = (parts[k] * inv).astype(BF16)
+        unit_ref[:, k * BLK : (k + 1) * BLK] = out
+        head_ref[:, k * BLK : (k + 1) * BLK] = out[:BLK]
 
 
 def asked_columns(asked_ref, rows):
@@ -175,8 +177,7 @@
     return recv_ref[:, at : at + 16, :].reshape(2 * BLK, BLK)
 
 
-def gather_units_body(asked_ref, unit_ref, send_ref, head_ref):
-    head_ref[...] = unit_ref[:BLK, :]
+def gather_units_body(asked_ref, unit_ref, send_ref):
     pack_rows(dot(request_rows(asked_ref), unit_ref[...]), D // BLK, send_ref)
 
 
@@ -424,15 +425,12 @@
         limit=60,
     )(cross_group.reshape(1, BLK), cross_row.reshape(1, BLK))
     asked = exchanged(wanted)
-    (units,) = call(unit_body, "units", [((ROWS, D), BF16)], "vv", nbytes=4 * 10**6)(desc, scales)
-    send, head = call(
-        gather_units_body,
-        "gather_units",
-        [((GROUPS, 48, BLK), BF16), ((BLK, D), BF16)],
-        "vv",
-    )(asked, units)
+    units, head = call(
+        unit_body, "units", [((ROWS, D), BF16), ((BLK, D), BF16)], "vv", nbytes=4 * 10**6
+    )(desc, scales)
+    next_units = passed_back(head)
+    (send,) = call(gather_units_body, "gather_units", [((GROUPS, 48, BLK), BF16)], "vv")(asked, units)
     far_units = exchanged(send)
-    next_units = passed_back(head)
     near_w, after_w, near_degree = call(
         near_body,
         "near",

time: 88.6 us -> 87.3 us (0.985)
  starting transfers between devices: 46.5 us -> 39.3 us
  waiting for transfers between devices: 8.03 us -> 14 us
    ppermute x3, starting transfers between devices: 22.8 us -> 17.1 us  [passed_back(): return lax.ppermute(block, 'node', [(i, i - 1) for i in range(1, size)])]
    all_to_all x4, waiting for transfers between devices: 7.6 us -> 11.4 us  [exchanged(): lax.all_to_all(block, 'group', split_axis=0, concat_axis=0, tiled=True)]
    ppermute x3, waiting for transfers between devices: 0.43 us -> 2.54 us  [passed_back(): return lax.ppermute(block, 'node', [(i, i - 1) for i in range(1, size)])]
    all_to_all x4, starting transfers between devices: 23.6 us -> 22.2 us  [exchanged(): lax.all_to_all(block, 'group', split_axis=0, concat_axis=0, tiled=True)]
  transfers between devices with their start and end apart: 7 -> 7, of which waited for: 4 -> 4; matrix products, arithmetic and copies ran while one was open for 1% -> 1% of each run, Pallas kernels for 22% -> 23%
where the time goes in v7:
time: 87.3 us; the launch traced here: 86.5 us
  starting transfers between devices  39.3 us (45%)
  Pallas kernels  29.6 us (34%)
  waiting for transfers between devices  14 us (16%)
  local copies, waits for them, and re-layouts  3.38 us (4%)
    all_to_all x4, starting transfers between devices, exchanged(): lax.all_to_all(block, 'group', split_axis=0, concat_axis=0, tiled=True)  22.2 us
    ppermute x3, starting transfers between devices, passed_back(): return lax.ppermute(block, 'node', [(i, i - 1) for i in range(1, size)])  17.1 us
    all_to_all x4, waiting for transfers between devices, exchanged(): lax.all_to_all(block, 'group', split_axis=0, concat_axis=0, tiled=True)  11.4 us
    pallas_call x1, Pallas kernels, local(): call(near_second_body, 'near_second', base_shapes, 'shhvh', 'vh', scratch...  7.09 us
    pallas_call x1, Pallas kernels, local(): call(near_first_body, 'near_first', base_shapes, 'shvh', 'vh', scratch=[p...  5.17 us
    pallas_call x1, Pallas kernels, local(): call(second_body, 'second', [wide_shape, head_shape, send_shape], 'vvvvvv...  3.47 us
    unnamed x9, local copies, waits for them, and re-layouts  3.38 us
    pallas_call x1, Pallas kernels, local(): call(seed_body, 'seeds', [send_shape, head_shape, wide_shape], 'vvh', 'vv...  3.13 us
  transfers between devices with their start and end apart: 7, of which 4 were waited for; matrix products, arithmetic and copies ran while one was open for 1% of the time, Pallas kernels for 23%

profile of v7, /device:TPU:7, one launch (start us, length us, event | category | flops | bytes accessed | tf_op | source)
XLA Modules:
  0.0 86.5 jit_solution(8301732926196275246)
XLA Ops:
  0.0 1.6 %index.1 = (s32[16,1,128]{2,1,0:T(1,128)}, s32[8,128]{1,0:T(8,128)}) custom-call(s32[1,128]{1,0:T(1,128)} %bitcast.7, s32[1,128]{1,0:T(1,128)} %bitcast.8), custom_call_target="tpu_custom_call" | custom-call | flops 1000000000 | bytes 1000000 | tf_op jit(solution)/shard_map/index/pallas_call | solution.py:419
  1.6 7.8 %all-to-all-start = ((s32[16,1,128]{2,1,0:T(1,128)}), s32[16,1,128]{2,1,0:T(1,128)S(1)}, u32[]{:S(2)}, u32[]{:S(2)}) async-start(s32[16,1,128]{2,1,0:T(1,128)} %get-tuple-element.26), calls=%async_computation | async-start | bytes 16384 | tf_op jit(solution)/shard_map/all_to_all | solution.py:406
  9.4 1.2 %copy-done.1 = bf16[1024,512]{1,0:T(8,128)(2,1)S(1)} copy-done((bf16[1024,512]{1,0:T(8,128)(2,1)S(1)}, bf16[1024,512]{1,0:T(8,128)(2,1)}, u32[]{:S(2)}) %copy-start.1) | copy-done | bytes 1048600
  10.6 0.7 copy-done.2
  11.4 1.1 %units.1 = (bf16[1024,512]{1,0:T(8,128)(2,1)S(1)}, bf16[128,512]{1,0:T(8,128)(2,1)S(1)}) custom-call(bf16[1024,512]{1,0:T(8,128)(2,1)S(1)} %copy-done.1, f32[4,1024]{1,0:T(4,128)S(1)} %copy-done.2), custom_call_target="tpu_custom_call" | custom-call | flops 1000000000 | bytes 4000000 | tf_op jit(solution)/shard_map/units/pallas_call | solution.py:428
  12.5 11.0 %collective-permute-start = (bf16[128,512]{1,0:T(8,128)(2,1)S(1)}, bf16[128,512]{1,0:T(8,128)(2,1)S(1)}, u32[]{:S(2)}, u32[]{:S(2)}) collective-permute-start(bf16[128,512]{1,0:T(8,128)(2,1)S(1)} %get-tuple-element.29), channel_id=1, source_target_pairs={{1,0},{2,1},{3,2},{4,3},{5,4},{6,5},{7,6},{8,7},{9,8},{10,9},{11,1... | collective-permute-start | bytes 393224 | tf_op jit(solution)/shard_map/ppermute | solution.py:402
  23.4 0.8 copy.8
  24.2 1.2 %gather_units.1 = bf16[16,48,128]{2,1,0:T(8,128)(2,1)} custom-call(s32[16,1,128]{2,1,0:T(1,128)S(1)} %all-to-all-done.asked_ref, bf16[1024,512]{1,0:T(8,128)(2,1)S(1)} %get-tuple-element.27.unit_ref), custom_call_target="tpu_custom_call" | custom-call | flops 1000000000 | bytes 1000000 | tf_op jit(solution)/shard_map/gather_units/pallas_call | solution.py:432
  25.4 7.5 %all-to-all-start.1 = ((bf16[16,48,128]{2,1,0:T(8,128)(2,1)}), bf16[16,48,128]{2,1,0:T(8,128)(2,1)S(1)}, u32[]{:S(2)}, u32[]{:S(2)}) async-start(bf16[16,48,128]{2,1,0:T(8,128)(2,1)} %gather_units.1), calls=%async_computation.1 | async-start | bytes 393216 | tf_op jit(solution)/shard_map/all_to_all | solution.py:406
  33.6 3.1 %seeds.1 = (bf16[16,96,128]{2,1,0:T(8,128)(2,1)S(1)}, bf16[1024,128]{1,0:T(8,128)(2,1)S(1)}, bf16[24,1024,256]{2,1,0:T(8,128)(2,1)}) custom-call(s32[16,1,128]{2,1,0:T(1,128)S(1)} %all-to-all-done.asked_ref, s32[1,1024]{1,0:T(1,128)S(1)} %bitcast.5, bf16[1000,1024]{1,0:T(8,128)(2,1)} %bitcast.6), custom_call_target="tpu_custom_call" | custom-call | flops 2000000000 | bytes 1000000 | tf_op jit(solution)/shard_map/seeds/pallas_call | solution.py:444
  36.7 2.5 %near.1 = (bf16[128,384,128]{2,1,0:T(8,128)(2,1)}, bf16[128,1024]{1,0:T(8,128)(2,1)S(1)}, f32[8,128]{1,0:T(8,128)S(1)}) custom-call(s32[8,2]{1,0:T(8,128)S(1)} %broadcast_subtract_fusion.named_ref, bf16[1024,512]{1,0:T(8,128)(2,1)S(1)} %get-tuple-element.27.unit_ref, bf16[128,512]{1,0:T(8,128)(2,1)S(1)} %collective-permute-done.next_ref), custom_call_target="tpu_custom_call" | custom-call | flops 1000000000 | bytes 1000000 | tf_op jit(solution)/shard_map/near/pallas_call | solution.py:434
  39.2 3.9 %all-to-all-done.1.recv_ref = bf16[16,48,128]{2,1,0:T(8,128)(2,1)S(1)} async-done(((bf16[16,48,128]{2,1,0:T(8,128)(2,1)}), bf16[16,48,128]{2,1,0:T(8,128)(2,1)S(1)}, u32[]{:S(2)}, u32[]{:S(2)}) %all-to-all-start.1) | async-done | bytes 196640 | tf_op jit(solution)/shard_map/all_to_all | solution.py:406
  43.2 1.9 %degree.1 = (bf16[256,1024]{1,0:T(8,128)(2,1)S(1)}, f32[1,1024]{1,0:T(1,128)S(1)}, bf16[1024,128]{1,0:T(8,128)(2,1)S(1)}, bf16[16,96,128]{2,1,0:T(8,128)(2,1)}) custom-call(bf16[16,48,128]{2,1,0:T(8,128)(2,1)S(1)} %all-to-all-done.1.recv_ref, s32[8,128]{1,0:T(8,128)S(1)} %copy-done, s32[16,1,128]{2,1,0:T(1,128)S(1)} %all-to-all-done.asked_ref, ...), custom_call_target="tpu_custom_call" | custom-call | flops 1000000000 | bytes 1000000 | tf_op jit(solution)/shard_map/degree/pallas_call | solution.py:454
  45.1 3.5 %all-to-all-start.2 = ((bf16[16,96,128]{2,1,0:T(8,128)(2,1)}), bf16[16,96,128]{2,1,0:T(8,128)(2,1)S(1)}, u32[]{:S(2)}, u32[]{:S(2)}) async-start(bf16[16,96,128]{2,1,0:T(8,128)(2,1)} %get-tuple-element.34), calls=%async_computation.2 | async-start | bytes 786432 | tf_op jit(solution)/shard_map/all_to_all | solution.py:406
  48.5 2.2 %collective-permute-start.1 = (bf16[1024,128]{1,0:T(8,128)(2,1)S(1)}, bf16[1024,128]{1,0:T(8,128)(2,1)S(1)}, u32[]{:S(2)}, u32[]{:S(2)}) collective-permute-start(bf16[1024,128]{1,0:T(8,128)(2,1)S(1)} %get-tuple-element.35), channel_id=1, source_target_pairs={{1,0},{2,1},{3,2},{4,3},{5,4},{6,5},{7,6},{8,7},{9,8},{10,9},{11,1... | collective-permute-start | bytes 786440 | tf_op jit(solution)/shard_map/ppermute | solution.py:402
  50.7 5.2 %near_first.1 = (bf16[1024,768]{1,0:T(8,128)(2,1)S(1)}, bf16[24,1024,256]{2,1,0:T(8,128)(2,1)}) custom-call(s32[8,2]{1,0:T(8,128)S(1)} %broadcast_subtract_fusion.named_ref, bf16[24,1024,256]{2,1,0:T(8,128)(2,1)} %get-tuple-element.37.seed_any, f32[1,1024]{1,0:T(1,128)S(1)} %get-tuple-element.38.rinv_ref, bf16[128,384,128]{2,1,0:T(8,128)(2,1)} %get-tuple-element.39.w_any), custom_call_target="tpu_custom_call" | custom-call | flops 2000000000 | bytes 1000000 | tf_op jit(solution)/shard_map/near_first/pallas_call | solution.py:464
  55.9 2.5 %collective-permute-done.1.next_ref = bf16[1024,128]{1,0:T(8,128)(2,1)S(1)} collective-permute-done((bf16[1024,128]{1,0:T(8,128)(2,1)S(1)}, bf16[1024,128]{1,0:T(8,128)(2,1)S(1)}, u32[]{:S(2)}, u32[]{:S(2)}) %collective-permute-start.1) | collective-permute-done | bytes 262176 | tf_op jit(solution)/shard_map/ppermute | solution.py:402
  58.4 4.5 %all-to-all-done.2.recv_ref = bf16[16,96,128]{2,1,0:T(8,128)(2,1)S(1)} async-done(((bf16[16,96,128]{2,1,0:T(8,128)(2,1)}), bf16[16,96,128]{2,1,0:T(8,128)(2,1)S(1)}, u32[]{:S(2)}, u32[]{:S(2)}) %all-to-all-start.2) | async-done | bytes 393248 | tf_op jit(solution)/shard_map/all_to_all | solution.py:406
  62.9 3.5 %second.1 = (bf16[24,1024,256]{2,1,0:T(8,128)(2,1)}, bf16[1024,128]{1,0:T(8,128)(2,1)S(1)}, bf16[16,96,128]{2,1,0:T(8,128)(2,1)}) custom-call(bf16[16,96,128]{2,1,0:T(8,128)(2,1)S(1)} %all-to-all-done.2.recv_ref, s32[8,128]{1,0:T(8,128)S(1)} %copy-done, s32[16,1,128]{2,1,0:T(1,128)S(1)} %all-to-all-done.asked_ref, ...), custom_call_target="tpu_custom_call" | custom-call | flops 1000000000 | bytes 1000000 | tf_op jit(solution)/shard_map/second/pallas_call | solution.py:473
  66.4 3.5 %all-to-all-start.3 = ((bf16[16,96,128]{2,1,0:T(8,128)(2,1)}), bf16[16,96,128]{2,1,0:T(8,128)(2,1)S(1)}, u32[]{:S(2)}, u32[]{:S(2)}) async-start(bf16[16,96,128]{2,1,0:T(8,128)(2,1)} %get-tuple-element.42), calls=%async_computation.3 | async-start | bytes 786432 | tf_op jit(solution)/shard_map/all_to_all | solution.py:406
  69.9 3.9 %collective-permute-start.2 = (bf16[1024,128]{1,0:T(8,128)(2,1)S(1)}, bf16[1024,128]{1,0:T(8,128)(2,1)S(1)}, u32[]{:S(2)}, u32[]{:S(2)}) collective-permute-start(bf16[1024,128]{1,0:T(8,128)(2,1)S(1)} %get-tuple-element.43), channel_id=1, source_target_pairs={{1,0},{2,1},{3,2},{4,3},{5,4},{6,5},{7,6},{8,7},{9,8},{10,9},{11,1... | collective-permute-start | bytes 786440 | tf_op jit(solution)/shard_map/ppermute | solution.py:402
  73.8 7.1 %near_second.1 = (bf16[1024,768]{1,0:T(8,128)(2,1)S(1)}, bf16[24,1024,256]{2,1,0:T(8,128)(2,1)}) custom-call(s32[8,2]{1,0:T(8,128)S(1)} %broadcast_subtract_fusion.named_ref, bf16[24,1024,256]{2,1,0:T(8,128)(2,1)} %get-tuple-element.44.second_any, bf16[24,1024,256]{2,1,0:T(8,128)(2,1)} %get-tuple-element.37.seed_any, ...), custom_call_target="tpu_custom_call" | custom-call | flops 2000000000 | bytes 1000000 | tf_op jit(solution)/shard_map/near_second/pallas_call | solution.py:484
  80.9 3.0 %all-to-all-done.3.recv_ref = bf16[16,96,128]{2,1,0:T(8,128)(2,1)S(1)} async-done(((bf16[16,96,128]{2,1,0:T(8,128)(2,1)}), bf16[16,96,128]{2,1,0:T(8,128)(2,1)S(1)}, u32[]{:S(2)}, u32[]{:S(2)}) %all-to-all-start.3) | async-done | bytes 393248 | tf_op jit(solution)/shard_map/all_to_all | solution.py:406
  83.9 2.5 %last.1 = bf16[1000,1024]{1,0:T(8,128)(2,1)} custom-call(bf16[16,96,128]{2,1,0:T(8,128)(2,1)S(1)} %all-to-all-done.3.recv_ref, s32[8,128]{1,0:T(8,128)S(1)} %copy-done, bf16[1024,128]{1,0:T(8,128)(2,1)S(1)} %collective-permute-done.2.next_ref, bf16[256,1024]{1,0:T(8,128)(2,1)S(1)} %get-tuple-element.36.w_ref, ...), custom_call_target="tpu_custom_call" | custom-call | flops 1000000000 | bytes 1000000 | tf_op jit(solution)/shard_map/last/pallas_call | solution.py:493
  (10 shorter events, 0.7 us)
Async XLA Ops:
  1.6 41.6 %copy-start = (s32[8,128]{1,0:T(8,128)S(1)}, s32[8,128]{1,0:T(8,128)}, u32[]{:S(2)}) copy-start(s32[8,128]{1,0:T(8,128)} %get-tuple-element.28.place_ref) | copy-start | bytes 12292
  1.6 22.6 %all-to-all-start = ((s32[16,1,128]{2,1,0:T(1,128)}), s32[16,1,128]{2,1,0:T(1,128)S(1)}, u32[]{:S(2)}, u32[]{:S(2)}) async-start(s32[16,1,128]{2,1,0:T(1,128)} %get-tuple-element.26), calls=%async_computation | async-start | bytes 16384 | tf_op jit(solution)/shard_map/all_to_all | solution.py:406
  9.4 1.2 %copy-start.1 = (bf16[1024,512]{1,0:T(8,128)(2,1)S(1)}, bf16[1024,512]{1,0:T(8,128)(2,1)}, u32[]{:S(2)}) copy-start(bf16[1024,512]{1,0:T(8,128)(2,1)} %desc_ref.1) | copy-start | bytes 3145732
  10.6 0.7 copy-start.2
  12.5 24.2 %collective-permute-start = (bf16[128,512]{1,0:T(8,128)(2,1)S(1)}, bf16[128,512]{1,0:T(8,128)(2,1)S(1)}, u32[]{:S(2)}, u32[]{:S(2)}) collective-permute-start(bf16[128,512]{1,0:T(8,128)(2,1)S(1)} %get-tuple-element.29), channel_id=1, source_target_pairs={{1,0},{2,1},{3,2},{4,3},{5,4},{6,5},{7,6},{8,7},{9,8},{10,9},{11,1... | collective-permute-start | bytes 393224 | tf_op jit(solution)/shard_map/ppermute | solution.py:402
  25.4 17.8 %all-to-all-start.1 = ((bf16[16,48,128]{2,1,0:T(8,128)(2,1)}), bf16[16,48,128]{2,1,0:T(8,128)(2,1)S(1)}, u32[]{:S(2)}, u32[]{:S(2)}) async-start(bf16[16,48,128]{2,1,0:T(8,128)(2,1)} %gather_units.1), calls=%async_computation.1 | async-start | bytes 393216 | tf_op jit(solution)/shard_map/all_to_all | solution.py:406
  32.9 0.7 copy-start.3
  45.1 17.9 %all-to-all-start.2 = ((bf16[16,96,128]{2,1,0:T(8,128)(2,1)}), bf16[16,96,128]{2,1,0:T(8,128)(2,1)S(1)}, u32[]{:S(2)}, u32[]{:S(2)}) async-start(bf16[16,96,128]{2,1,0:T(8,128)(2,1)} %get-tuple-element.34), calls=%async_computation.2 | async-start | bytes 786432 | tf_op jit(solution)/shard_map/all_to_all | solution.py:406
  48.5 9.9 %collective-permute-start.1 = (bf16[1024,128]{1,0:T(8,128)(2,1)S(1)}, bf16[1024,128]{1,0:T(8,128)(2,1)S(1)}, u32[]{:S(2)}, u32[]{:S(2)}) collective-permute-start(bf16[1024,128]{1,0:T(8,128)(2,1)S(1)} %get-tuple-element.35), channel_id=1, source_target_pairs={{1,0},{2,1},{3,2},{4,3},{5,4},{6,5},{7,6},{8,7},{9,8},{10,9},{11,1... | collective-permute-start | bytes 786440 | tf_op jit(solution)/shard_map/ppermute | solution.py:402
  66.4 17.5 %all-to-all-start.3 = ((bf16[16,96,128]{2,1,0:T(8,128)(2,1)}), bf16[16,96,128]{2,1,0:T(8,128)(2,1)S(1)}, u32[]{:S(2)}, u32[]{:S(2)}) async-start(bf16[16,96,128]{2,1,0:T(8,128)(2,1)} %get-tuple-element.42), calls=%async_computation.3 | async-start | bytes 786432 | tf_op jit(solution)/shard_map/all_to_all | solution.py:406
  69.9 11.0 %collective-permute-start.2 = (bf16[1024,128]{1,0:T(8,128)(2,1)S(1)}, bf16[1024,128]{1,0:T(8,128)(2,1)S(1)}, u32[]{:S(2)}, u32[]{:S(2)}) collective-permute-start(bf16[1024,128]{1,0:T(8,128)(2,1)S(1)} %get-tuple-element.43), channel_id=1, source_target_pairs={{1,0},{2,1},{3,2},{4,3},{5,4},{6,5},{7,6},{8,7},{9,8},{10,9},{11,1... | collective-permute-start | bytes 786440 | tf_op jit(solution)/shard_map/ppermute | solution.py:402

commit v8 on v7

--- a/solution.py
+++ b/solution.py
@@ -196,7 +196,7 @@
         w_ref[r, :BLK, :] = w.astype(BF16)
         after = jnp.zeros((BLK, BLK), F32)
         for k in range(2):
-            tile = named_ref[r, k]
+            tile = named_ref[k, r]
             start = pl.multiple_of(tile * BLK, BLK)
             w = cube_pos(dot(ext_ref[pl.ds(start, BLK), :], own, NT))
             degree = degree + jnp.sum(w, axis=0, keepdims=True)
@@ -277,7 +277,7 @@
 def spread_near(named_ref, source_ref, w_ref, r):
     sources = [source_ref[:, r * BLK : (r + 1) * BLK]]
     for k in range(2):
-        start = pl.multiple_of(lax.rem(named_ref[r, k], TILES) * BLK, BLK)
+        start = pl.multiple_of(lax.rem(named_ref[k, r], TILES) * BLK, BLK)
         sources.append(source_ref[:, pl.ds(start, BLK)])
     return dot(jnp.concatenate(sources, axis=1), w_ref[r])
 
@@ -407,7 +407,7 @@
 
 
 def local(desc, scales, labels, prior, block_cols, cross_group, cross_row):
-    named = block_cols - lax.axis_index("node") * TILES
+    named = jnp.transpose(block_cols) - lax.axis_index("node") * TILES
     sem = pltpu.SemaphoreType.DMA
     sems = pltpu.SemaphoreType.DMA((PAIRS,))
     row_vector = pltpu.VMEM((1, BLK), jnp.int32)

time: 87.3 us -> 87.2 us (level)
    unnamed x9 -> x8, local copies, waits for them, and re-layouts: 3.38 us -> 2.63 us
where the time goes in v8:
time: 87.2 us; the launch traced here: 86.4 us
  starting transfers between devices  39.8 us (46%)
  Pallas kernels  29.5 us (34%)
  waiting for transfers between devices  13.5 us (15%)
  local copies, waits for them, and re-layouts  2.63 us (3%)
    all_to_all x4, starting transfers between devices, exchanged(): lax.all_to_all(block, 'group', split_axis=0, concat_axis=0, tiled=True)  22.7 us
    ppermute x3, starting transfers between devices, passed_back(): return lax.ppermute(block, 'node', [(i, i - 1) for i in range(1, size)])  17.1 us
    all_to_all x4, waiting for transfers between devices, exchanged(): lax.all_to_all(block, 'group', split_axis=0, concat_axis=0, tiled=True)  11.1 us
    pallas_call x1, Pallas kernels, local(): call(near_second_body, 'near_second', base_shapes, 'shhvh', 'vh', scratch...  7.05 us
    pallas_call x1, Pallas kernels, local(): call(near_first_body, 'near_first', base_shapes, 'shvh', 'vh', scratch=[p...  5.14 us
    pallas_call x1, Pallas kernels, local(): call(second_body, 'second', [wide_shape, head_shape, send_shape], 'vvvvvv...  3.48 us
    pallas_call x1, Pallas kernels, local(): call(seed_body, 'seeds', [send_shape, head_shape, wide_shape], 'vvh', 'vv...  3.13 us
    unnamed x8, local copies, waits for them, and re-layouts  2.63 us
  transfers between devices with their start and end apart: 7, of which 4 were waited for; matrix products, arithmetic and copies ran while one was open for 1% of the time, Pallas kernels for 23%

profile of v8, /device:TPU:7, one launch (start us, length us, event | category | flops | bytes accessed | tf_op | source)
XLA Modules:
  0.0 86.4 jit_solution(12098551060681807080)
XLA Ops:
  0.0 1.6 %index.1 = (s32[16,1,128]{2,1,0:T(1,128)}, s32[8,128]{1,0:T(8,128)}) custom-call(s32[1,128]{1,0:T(1,128)} %bitcast.9, s32[1,128]{1,0:T(1,128)} %bitcast.10), custom_call_target="tpu_custom_call" | custom-call | flops 1000000000 | bytes 1000000 | tf_op jit(solution)/shard_map/index/pallas_call | solution.py:419
  1.6 7.8 %all-to-all-start = ((s32[16,1,128]{2,1,0:T(1,128)}), s32[16,1,128]{2,1,0:T(1,128)S(1)}, u32[]{:S(2)}, u32[]{:S(2)}) async-start(s32[16,1,128]{2,1,0:T(1,128)} %get-tuple-element.26), calls=%async_computation | async-start | bytes 16384 | tf_op jit(solution)/shard_map/all_to_all | solution.py:406
  9.4 1.2 %copy-done.1 = bf16[1024,512]{1,0:T(8,128)(2,1)S(1)} copy-done((bf16[1024,512]{1,0:T(8,128)(2,1)S(1)}, bf16[1024,512]{1,0:T(8,128)(2,1)}, u32[]{:S(2)}) %copy-start.1) | copy-done | bytes 1048600
  10.6 0.7 copy-done.2
  11.4 1.1 %units.1 = (bf16[1024,512]{1,0:T(8,128)(2,1)S(1)}, bf16[128,512]{1,0:T(8,128)(2,1)S(1)}) custom-call(bf16[1024,512]{1,0:T(8,128)(2,1)S(1)} %copy-done.1, f32[4,1024]{1,0:T(4,128)S(1)} %copy-done.2), custom_call_target="tpu_custom_call" | custom-call | flops 1000000000 | bytes 4000000 | tf_op jit(solution)/shard_map/units/pallas_call | solution.py:428
  12.5 11.0 %collective-permute-start = (bf16[128,512]{1,0:T(8,128)(2,1)S(1)}, bf16[128,512]{1,0:T(8,128)(2,1)S(1)}, u32[]{:S(2)}, u32[]{:S(2)}) collective-permute-start(bf16[128,512]{1,0:T(8,128)(2,1)S(1)} %get-tuple-element.29), channel_id=1, source_target_pairs={{1,0},{2,1},{3,2},{4,3},{5,4},{6,5},{7,6},{8,7},{9,8},{10,9},{11,1... | collective-permute-start | bytes 393224 | tf_op jit(solution)/shard_map/ppermute | solution.py:402
  23.4 1.2 %gather_units.1 = bf16[16,48,128]{2,1,0:T(8,128)(2,1)} custom-call(s32[16,1,128]{2,1,0:T(1,128)S(1)} %all-to-all-done.asked_ref, bf16[1024,512]{1,0:T(8,128)(2,1)S(1)} %get-tuple-element.27.unit_ref), custom_call_target="tpu_custom_call" | custom-call | flops 1000000000 | bytes 1000000 | tf_op jit(solution)/shard_map/gather_units/pallas_call | solution.py:432
  24.6 7.5 %all-to-all-start.1 = ((bf16[16,48,128]{2,1,0:T(8,128)(2,1)}), bf16[16,48,128]{2,1,0:T(8,128)(2,1)S(1)}, u32[]{:S(2)}, u32[]{:S(2)}) async-start(bf16[16,48,128]{2,1,0:T(8,128)(2,1)} %gather_units.1), calls=%async_computation.1 | async-start | bytes 393216 | tf_op jit(solution)/shard_map/all_to_all | solution.py:406
  32.8 0.7 copy-done.3
  33.5 3.1 %seeds.1 = (bf16[16,96,128]{2,1,0:T(8,128)(2,1)S(1)}, bf16[1024,128]{1,0:T(8,128)(2,1)S(1)}, bf16[24,1024,256]{2,1,0:T(8,128)(2,1)}) custom-call(s32[16,1,128]{2,1,0:T(1,128)S(1)} %all-to-all-done.asked_ref, s32[1,1024]{1,0:T(1,128)S(1)} %bitcast.7, bf16[1000,1024]{1,0:T(8,128)(2,1)} %bitcast.8), custom_call_target="tpu_custom_call" | custom-call | flops 2000000000 | bytes 1000000 | tf_op jit(solution)/shard_map/seeds/pallas_call | solution.py:444
  36.6 2.5 %near.1 = (bf16[128,384,128]{2,1,0:T(8,128)(2,1)}, bf16[128,1024]{1,0:T(8,128)(2,1)S(1)}, f32[8,128]{1,0:T(8,128)S(1)}) custom-call(s32[2,8]{1,0:T(2,128)S(1)} %subtract_bitcast_fusion.named_ref, bf16[1024,512]{1,0:T(8,128)(2,1)S(1)} %get-tuple-element.27.unit_ref, bf16[128,512]{1,0:T(8,128)(2,1)S(1)} %collective-permute-done.next_ref), custom_call_target="tpu_custom_call" | custom-call | flops 1000000000 | bytes 1000000 | tf_op jit(solution)/shard_map/near/pallas_call | solution.py:434
  39.1 3.3 %all-to-all-done.1.recv_ref = bf16[16,48,128]{2,1,0:T(8,128)(2,1)S(1)} async-done(((bf16[16,48,128]{2,1,0:T(8,128)(2,1)}), bf16[16,48,128]{2,1,0:T(8,128)(2,1)S(1)}, u32[]{:S(2)}, u32[]{:S(2)}) %all-to-all-start.1) | async-done | bytes 196640 | tf_op jit(solution)/shard_map/all_to_all | solution.py:406
  42.4 1.9 %degree.1 = (bf16[256,1024]{1,0:T(8,128)(2,1)S(1)}, f32[1,1024]{1,0:T(1,128)S(1)}, bf16[1024,128]{1,0:T(8,128)(2,1)S(1)}, bf16[16,96,128]{2,1,0:T(8,128)(2,1)}) custom-call(bf16[16,48,128]{2,1,0:T(8,128)(2,1)S(1)} %all-to-all-done.1.recv_ref, s32[8,128]{1,0:T(8,128)S(1)} %copy-done, s32[16,1,128]{2,1,0:T(1,128)S(1)} %all-to-all-done.asked_ref, ...), custom_call_target="tpu_custom_call" | custom-call | flops 1000000000 | bytes 1000000 | tf_op jit(solution)/shard_map/degree/pallas_call | solution.py:454
  44.3 3.9 %all-to-all-start.2 = ((bf16[16,96,128]{2,1,0:T(8,128)(2,1)}), bf16[16,96,128]{2,1,0:T(8,128)(2,1)S(1)}, u32[]{:S(2)}, u32[]{:S(2)}) async-start(bf16[16,96,128]{2,1,0:T(8,128)(2,1)} %get-tuple-element.34), calls=%async_computation.2 | async-start | bytes 786432 | tf_op jit(solution)/shard_map/all_to_all | solution.py:406
  48.2 2.2 %collective-permute-start.1 = (bf16[1024,128]{1,0:T(8,128)(2,1)S(1)}, bf16[1024,128]{1,0:T(8,128)(2,1)S(1)}, u32[]{:S(2)}, u32[]{:S(2)}) collective-permute-start(bf16[1024,128]{1,0:T(8,128)(2,1)S(1)} %get-tuple-element.35), channel_id=1, source_target_pairs={{1,0},{2,1},{3,2},{4,3},{5,4},{6,5},{7,6},{8,7},{9,8},{10,9},{11,1... | collective-permute-start | bytes 786440 | tf_op jit(solution)/shard_map/ppermute | solution.py:402
  50.4 5.1 %near_first.1 = (bf16[1024,768]{1,0:T(8,128)(2,1)S(1)}, bf16[24,1024,256]{2,1,0:T(8,128)(2,1)}) custom-call(s32[2,8]{1,0:T(2,128)S(1)} %subtract_bitcast_fusion.named_ref, bf16[24,1024,256]{2,1,0:T(8,128)(2,1)} %get-tuple-element.37.seed_any, f32[1,1024]{1,0:T(1,128)S(1)} %get-tuple-element.38.rinv_ref, bf16[128,384,128]{2,1,0:T(8,128)(2,1)} %get-tuple-element.39.w_any), custom_call_target="tpu_custom_call" | custom-call | flops 2000000000 | bytes 1000000 | tf_op jit(solution)/shard_map/near_first/pallas_call | solution.py:464
  55.6 2.4 %collective-permute-done.1.next_ref = bf16[1024,128]{1,0:T(8,128)(2,1)S(1)} collective-permute-done((bf16[1024,128]{1,0:T(8,128)(2,1)S(1)}, bf16[1024,128]{1,0:T(8,128)(2,1)S(1)}, u32[]{:S(2)}, u32[]{:S(2)}) %collective-permute-start.1) | collective-permute-done | bytes 262176 | tf_op jit(solution)/shard_map/ppermute | solution.py:402
  58.0 4.8 %all-to-all-done.2.recv_ref = bf16[16,96,128]{2,1,0:T(8,128)(2,1)S(1)} async-done(((bf16[16,96,128]{2,1,0:T(8,128)(2,1)}), bf16[16,96,128]{2,1,0:T(8,128)(2,1)S(1)}, u32[]{:S(2)}, u32[]{:S(2)}) %all-to-all-start.2) | async-done | bytes 393248 | tf_op jit(solution)/shard_map/all_to_all | solution.py:406
  62.8 3.5 %second.1 = (bf16[24,1024,256]{2,1,0:T(8,128)(2,1)}, bf16[1024,128]{1,0:T(8,128)(2,1)S(1)}, bf16[16,96,128]{2,1,0:T(8,128)(2,1)}) custom-call(bf16[16,96,128]{2,1,0:T(8,128)(2,1)S(1)} %all-to-all-done.2.recv_ref, s32[8,128]{1,0:T(8,128)S(1)} %copy-done, s32[16,1,128]{2,1,0:T(1,128)S(1)} %all-to-all-done.asked_ref, ...), custom_call_target="tpu_custom_call" | custom-call | flops 1000000000 | bytes 1000000 | tf_op jit(solution)/shard_map/second/pallas_call | solution.py:473
  66.3 3.5 %all-to-all-start.3 = ((bf16[16,96,128]{2,1,0:T(8,128)(2,1)}), bf16[16,96,128]{2,1,0:T(8,128)(2,1)S(1)}, u32[]{:S(2)}, u32[]{:S(2)}) async-start(bf16[16,96,128]{2,1,0:T(8,128)(2,1)} %get-tuple-element.42), calls=%async_computation.3 | async-start | bytes 786432 | tf_op jit(solution)/shard_map/all_to_all | solution.py:406
  69.7 3.9 %collective-permute-start.2 = (bf16[1024,128]{1,0:T(8,128)(2,1)S(1)}, bf16[1024,128]{1,0:T(8,128)(2,1)S(1)}, u32[]{:S(2)}, u32[]{:S(2)}) collective-permute-start(bf16[1024,128]{1,0:T(8,128)(2,1)S(1)} %get-tuple-element.43), channel_id=1, source_target_pairs={{1,0},{2,1},{3,2},{4,3},{5,4},{6,5},{7,6},{8,7},{9,8},{10,9},{11,1... | collective-permute-start | bytes 786440 | tf_op jit(solution)/shard_map/ppermute | solution.py:402
  73.7 7.0 %near_second.1 = (bf16[1024,768]{1,0:T(8,128)(2,1)S(1)}, bf16[24,1024,256]{2,1,0:T(8,128)(2,1)}) custom-call(s32[2,8]{1,0:T(2,128)S(1)} %subtract_bitcast_fusion.named_ref, bf16[24,1024,256]{2,1,0:T(8,128)(2,1)} %get-tuple-element.44.second_any, bf16[24,1024,256]{2,1,0:T(8,128)(2,1)} %get-tuple-element.37.seed_any, ...), custom_call_target="tpu_custom_call" | custom-call | flops 2000000000 | bytes 1000000 | tf_op jit(solution)/shard_map/near_second/pallas_call | solution.py:484
  80.8 3.0 %all-to-all-done.3.recv_ref = bf16[16,96,128]{2,1,0:T(8,128)(2,1)S(1)} async-done(((bf16[16,96,128]{2,1,0:T(8,128)(2,1)}), bf16[16,96,128]{2,1,0:T(8,128)(2,1)S(1)}, u32[]{:S(2)}, u32[]{:S(2)}) %all-to-all-start.3) | async-done | bytes 393248 | tf_op jit(solution)/shard_map/all_to_all | solution.py:406
  83.7 2.5 %last.1 = bf16[1000,1024]{1,0:T(8,128)(2,1)} custom-call(bf16[16,96,128]{2,1,0:T(8,128)(2,1)S(1)} %all-to-all-done.3.recv_ref, s32[8,128]{1,0:T(8,128)S(1)} %copy-done, bf16[1024,128]{1,0:T(8,128)(2,1)S(1)} %collective-permute-done.2.next_ref, bf16[256,1024]{1,0:T(8,128)(2,1)S(1)} %get-tuple-element.36.w_ref, ...), custom_call_target="tpu_custom_call" | custom-call | flops 1000000000 | bytes 1000000 | tf_op jit(solution)/shard_map/last/pallas_call | solution.py:493
  (9 shorter events, 0.7 us)
Async XLA Ops:
  1.6 40.8 %copy-start = (s32[8,128]{1,0:T(8,128)S(1)}, s32[8,128]{1,0:T(8,128)}, u32[]{:S(2)}) copy-start(s32[8,128]{1,0:T(8,128)} %get-tuple-element.28.place_ref) | copy-start | bytes 12292
  1.6 21.8 %all-to-all-start = ((s32[16,1,128]{2,1,0:T(1,128)}), s32[16,1,128]{2,1,0:T(1,128)S(1)}, u32[]{:S(2)}, u32[]{:S(2)}) async-start(s32[16,1,128]{2,1,0:T(1,128)} %get-tuple-element.26), calls=%async_computation | async-start | bytes 16384 | tf_op jit(solution)/shard_map/all_to_all | solution.py:406
  9.4 1.2 %copy-start.1 = (bf16[1024,512]{1,0:T(8,128)(2,1)S(1)}, bf16[1024,512]{1,0:T(8,128)(2,1)}, u32[]{:S(2)}) copy-start(bf16[1024,512]{1,0:T(8,128)(2,1)} %desc_ref.1) | copy-start | bytes 3145732
  10.6 0.7 copy-start.2
  12.5 24.2 %collective-permute-start = (bf16[128,512]{1,0:T(8,128)(2,1)S(1)}, bf16[128,512]{1,0:T(8,128)(2,1)S(1)}, u32[]{:S(2)}, u32[]{:S(2)}) collective-permute-start(bf16[128,512]{1,0:T(8,128)(2,1)S(1)} %get-tuple-element.29), channel_id=1, source_target_pairs={{1,0},{2,1},{3,2},{4,3},{5,4},{6,5},{7,6},{8,7},{9,8},{10,9},{11,1... | collective-permute-start | bytes 393224 | tf_op jit(solution)/shard_map/ppermute | solution.py:402
  24.6 17.8 %all-to-all-start.1 = ((bf16[16,48,128]{2,1,0:T(8,128)(2,1)}), bf16[16,48,128]{2,1,0:T(8,128)(2,1)S(1)}, u32[]{:S(2)}, u32[]{:S(2)}) async-start(bf16[16,48,128]{2,1,0:T(8,128)(2,1)} %gather_units.1), calls=%async_computation.1 | async-start | bytes 393216 | tf_op jit(solution)/shard_map/all_to_all | solution.py:406
  32.8 0.7 copy-start.3
  44.3 18.5 %all-to-all-start.2 = ((bf16[16,96,128]{2,1,0:T(8,128)(2,1)}), bf16[16,96,128]{2,1,0:T(8,128)(2,1)S(1)}, u32[]{:S(2)}, u32[]{:S(2)}) async-start(bf16[16,96,128]{2,1,0:T(8,128)(2,1)} %get-tuple-element.34), calls=%async_computation.2 | async-start | bytes 786432 | tf_op jit(solution)/shard_map/all_to_all | solution.py:406
  48.2 9.8 %collective-permute-start.1 = (bf16[1024,128]{1,0:T(8,128)(2,1)S(1)}, bf16[1024,128]{1,0:T(8,128)(2,1)S(1)}, u32[]{:S(2)}, u32[]{:S(2)}) collective-permute-start(bf16[1024,128]{1,0:T(8,128)(2,1)S(1)} %get-tuple-element.35), channel_id=1, source_target_pairs={{1,0},{2,1},{3,2},{4,3},{5,4},{6,5},{7,6},{8,7},{9,8},{10,9},{11,1... | collective-permute-start | bytes 786440 | tf_op jit(solution)/shard_map/ppermute | solution.py:402
  66.3 17.5 %all-to-all-start.3 = ((bf16[16,96,128]{2,1,0:T(8,128)(2,1)}), bf16[16,96,128]{2,1,0:T(8,128)(2,1)S(1)}, u32[]{:S(2)}, u32[]{:S(2)}) async-start(bf16[16,96,128]{2,1,0:T(8,128)(2,1)} %get-tuple-element.42), calls=%async_computation.3 | async-start | bytes 786432 | tf_op jit(solution)/shard_map/all_to_all | solution.py:406
  69.7 11.0 %collective-permute-start.2 = (bf16[1024,128]{1,0:T(8,128)(2,1)S(1)}, bf16[1024,128]{1,0:T(8,128)(2,1)S(1)}, u32[]{:S(2)}, u32[]{:S(2)}) collective-permute-start(bf16[1024,128]{1,0:T(8,128)(2,1)S(1)} %get-tuple-element.43), channel_id=1, source_target_pairs={{1,0},{2,1},{3,2},{4,3},{5,4},{6,5},{7,6},{8,7},{9,8},{10,9},{11,1... | collective-permute-start | bytes 786440 | tf_op jit(solution)/shard_map/ppermute | solution.py:402
